TPU v7x, 32 devices: a whole 2x2x4 slice. The times are simulated.
32 devices in a mesh: groups: 2 (over y), node: 4 (over z), local: 4 (over x, core).
Axes of the slice: x: 2, y: 2, z: 4, core: 2. Of those that a mesh axis runs over, the one named last changes fastest.
Arguments:
- tokens: bfloat16 [4096, 3584], P(('groups', 'node', 'local')), parts along dimension 0, may hold values from -6 to 6
- routing_gate_weight: float32 [4096, 8], P(('groups', 'node', 'local')), parts along dimension 0, may hold values from 0.1 to 0.5
- selected_expert_index: int32 [4096, 8], P(('groups', 'node', 'local')), parts along dimension 0, may hold values from 0 to 31, as said below
- w_gate: bfloat16 [4, 3584, 1024], P('node', None, 'local'), may hold values from -0.09375 to 0.09375
- w_up: bfloat16 [4, 3584, 1024], P('node', None, 'local'), may hold values from -0.09375 to 0.09375
- w_down: bfloat16 [4, 1024, 3584], P('node', 'local'), may hold values from -0.1875 to 0.1875
- s_gate: bfloat16 [3584, 1024], P(None, 'local'), may hold values from -0.09375 to 0.09375
- s_up: bfloat16 [3584, 1024], P(None, 'local'), may hold values from -0.09375 to 0.09375
- s_down: bfloat16 [1024, 3584], P('local'), may hold values from -0.1875 to 0.1875
Outputs:
- mixed: bfloat16 [4096, 3584], P(('groups', 'node', 'local')), parts along dimension 0
There are 2 independent parts, one for each index of `groups`. A program takes and returns all parts, laid end to end along the dimension named above; an argument that names none is the same for every part. Nothing has to cross between parts.
Inputs may be any that keep to these rules, and one draw needn't show every extreme that they name: `selected_expert_index`: expert e belongs to node e // 8. A token's 8 experts are two distinct experts in each of 4 distinct nodes. Among the tokens of one device at most 8 name the in-flight expert of any one node, and for one node, the same for every device of a part, the in-flight expert is named by exactly 8 tokens of every device; the other nodes' in-flight experts are named by at most 8.
All inputs are finite; a program needn't handle non-finite values.
Results may differ from a plain program's by a relative error of at most 0.0095.
Values may be sent and summed in bfloat16 or wider, within the bound.
No kernel may reach another device: no remote copies, remote signals or barrier semaphores. Data moves between devices by JAX's collectives and lax.ppermute only.
A program may use at most 128 MiB of HBM per device.

v0:
```python
import jax
import jax.numpy as jnp
from jax import lax
from jax.sharding import PartitionSpec as P

EXPERTS_PER_NODE = 8


def expert_part(row_block, proj_gate, proj_up, proj_down):
    gate = jnp.dot(row_block, proj_gate, preferred_element_type=jnp.float32)
    lifted = jnp.dot(row_block, proj_up, preferred_element_type=jnp.float32)
    hidden = (jax.nn.silu(gate) * lifted).astype(jnp.bfloat16)
    return jnp.dot(hidden, proj_down, preferred_element_type=jnp.float32)


def per_device(
    tokens, routing_gate_weight, selected_expert_index, w_gate, w_up, w_down, s_gate, s_up, s_down
):
    node_count = lax.axis_size("node")
    local_count = lax.axis_size("local")
    slot_capacity = tokens.shape[0] // 16
    width = tokens.shape[1]
    owners = jnp.arange(node_count, dtype=jnp.int32) * EXPERTS_PER_NODE
    matched = selected_expert_index[:, :, None] == owners[None, None, :]
    chosen = jnp.any(matched, axis=1).astype(jnp.int32)
    position = jnp.cumsum(chosen, axis=0) - chosen
    slots = jnp.arange(slot_capacity, dtype=jnp.int32)
    selector = (chosen[:, :, None] == 1) & (position[:, :, None] == slots[None, None, :])
    outgoing = jnp.einsum(
        "tnc,td->ncd", selector.astype(jnp.bfloat16), tokens, preferred_element_type=jnp.float32
    ).astype(jnp.bfloat16)
    expert_gate = w_gate[0]
    expert_up = w_up[0]
    expert_down = w_down[0]
    spread = jnp.broadcast_to(outgoing[:, None], (node_count, local_count, slot_capacity, width))
    spread = spread.reshape(node_count * local_count, slot_capacity, width)
    arrived = lax.all_to_all(spread, ("node", "local"), split_axis=0, concat_axis=0, tiled=True)
    received = arrived.reshape(node_count, local_count, slot_capacity, width)
    gate = jnp.einsum("mjcd,df->jmcf", received, expert_gate, preferred_element_type=jnp.float32)
    lifted = jnp.einsum("mjcd,df->jmcf", received, expert_up, preferred_element_type=jnp.float32)
    hidden = (jax.nn.silu(gate) * lifted).astype(jnp.bfloat16)
    partial_value = jnp.einsum(
        "jmcf,fe->jmce", hidden, expert_down, preferred_element_type=jnp.float32
    )
    partial_value = partial_value.reshape(local_count * node_count * slot_capacity, width)
    summed = lax.psum_scatter(
        partial_value.astype(jnp.bfloat16), "local", scatter_dimension=0, tiled=True
    )
    replies = summed.reshape(node_count, slot_capacity, width)
    returned = lax.all_to_all(replies, "node", split_axis=0, concat_axis=0, tiled=True)
    returned_rows = returned.reshape(node_count * slot_capacity, width)
    pending_transfer_flag = selected_expert_index % EXPERTS_PER_NODE == 0
    destination_node = selected_expert_index // EXPERTS_PER_NODE
    destination_slot = jnp.take_along_axis(position, destination_node, axis=1)
    token_row_index = jnp.where(
        pending_transfer_flag, destination_node * slot_capacity + destination_slot, 0
    )
    fetched = jnp.take(returned_rows, token_row_index, axis=0)
    capacity_factor = jnp.where(pending_transfer_flag, routing_gate_weight, jnp.float32(0.0))
    routed = jnp.sum(capacity_factor[:, :, None] * fetched.astype(jnp.float32), axis=1)
    shared_terms = expert_part(
        lax.all_gather(tokens, "local", axis=0, tiled=True), s_gate, s_up, s_down
    )
    shared = lax.psum_scatter(
        shared_terms.astype(jnp.bfloat16), "local", scatter_dimension=0, tiled=True
    ).astype(jnp.float32)
    return (shared + routed).astype(jnp.bfloat16)


def solution(mesh):
    in_specs = (
        P(("groups", "node", "local"), None),
        P(("groups", "node", "local"), None),
        P(("groups", "node", "local"), None),
        P("node", None, "local"),
        P("node", None, "local"),
        P("node", "local", None),
        P(None, "local"),
        P(None, "local"),
        P("local", None),
    )
    out_specs = P(("groups", "node", "local"), None)
    return jax.shard_map(
        per_device, mesh=mesh, in_specs=in_specs, out_specs=out_specs, check_vma=False
    )
```

profile of v0, /device:TPU:0, one launch (start us, length us, event | category | flops | bytes accessed | tf_op | source)
XLA Modules:
  0.0 131.5 jit_solution(14238551505304007549)
XLA Ops:
  6.5 0.0 copy-start
  6.5 0.0 all-gather.2.cloned.1.call-start
  6.5 0.7 all-gather.2.cloned.1.call-update
  7.3 0.0 reduce-scatter.5.cloned.1.call-start
  7.3 0.8 compare_reduce_fusion
  8.1 0.1 copy.48
  8.2 0.2 reduce_window_sum.11
  8.4 0.1 copy.49
  8.5 0.0 copy-start.4
  8.5 1.6 %convolution_convert_fusion.2 = bf16[4,8,3584]{2,1,0:T(8,128)(2,1)S(1)} fusion(bf16[128,3584]{1,0:T(8,128)(2,1)} %param.9, s32[128,4]{0,1:T(4,128)S(1)} %convert_subtract_fusion, pred[128,4]{0,1:T(4,128)(4,1)S(1)} %get-tuple-element.7), kind=kOutput, calls=%fused_computation.6 | convolution fusion | flops 29483008 | bytes 1149440 | tf_op jit(solution)/shard_map/tnc,td->ncd/dot_general | solution.py:29
  10.0 0.1 broadcast_in_dim.37
  10.1 29.7 %all_to_all.10 = bf16[16,8,3584]{2,1,0:T(8,128)(2,1)S(1)} all-to-all(bf16[16,8,3584]{2,1,0:T(8,128)(2,1)S(1)} %bitcast.58), channel_id=1, replica_groups=mesh['groups'=2,'node'=4,'local'=4] {'node','local'}, dimensions={0} | all-to-all | bytes 1835008 | tf_op jit(solution)/shard_map/all_to_all | solution.py:37
  39.8 0.0 copy-start.5
  39.8 0.0 copy-done.4
  39.8 0.4 fusion.6
  40.2 1.1 copy-done.5
  41.4 0.0 copy-start.1
  41.4 0.4 fusion.15
  41.8 1.1 copy-done.1
  42.9 1.3 %convolution_convert_fusion.1 = bf16[128,3584]{1,0:T(8,128)(2,1)} fusion(bf16[128,256]{1,0:T(8,128)(2,1)S(1)} %bitcast.61, bf16[1,256,3584]{2,1,0:T(8,128)(2,1)S(1)} %copy-done.1), kind=kOutput, calls=%fused_computation.5 | convolution fusion | flops 235339776 | bytes 2818048 | tf_op jit(solution)/shard_map/jmcf,fe->jmce/dot_general | solution.py:42
  44.2 0.0 reduce-scatter.5.cloned.1.call-update
  44.2 0.0 reduce-scatter.3.cloned.1.call-start
  44.3 7.2 %all-gather.2.cloned.1.call-done = bf16[512,3584]{1,0:T(8,128)(2,1)} async-done(((bf16[128,3584]{1,0:T(8,128)(2,1)}), bf16[512,3584]{1,0:T(8,128)(2,1)}) %all-gather.2.cloned.1.call-update) | async-done | bytes 3670032 | tf_op jit(solution)/shard_map/all_gather | solution.py:62
  51.5 3.7 %fusion.33 = f32[512,256]{1,0:T(8,128)S(1)} fusion(bf16[512,3584]{1,0:T(8,128)(2,1)} %all-gather.2.cloned.1.call-done, bf16[3584,256]{1,0:T(8,128)(2,1)} %param.15), kind=kOutput, calls=%fused_computation.50 | convolution fusion | flops 939524096 | bytes 6029312 | tf_op jit(solution)/shard_map/dot_general | solution.py:10
  55.2 0.0 copy-done
  55.2 8.5 %convolution_convert_fusion = bf16[512,3584]{1,0:T(8,128)(2,1)} fusion(bf16[256,3584]{1,0:T(8,128)(2,1)S(1)} %copy-done, bf16[512,3584]{1,0:T(8,128)(2,1)} %all-gather.2.cloned.1.call-done, bf16[3584,256]{1,0:T(8,128)(2,1)} %param.16, f32[512,256]{1,0:T(8,128)S(1)} %fusion.33), kind=kOutput, calls=%fused_computation.4 | convolution fusion | flops 1881669632 | bytes 11534336 | tf_op jit(solution)/shard_map/dot_general | solution.py:13
  63.7 0.0 copy-start.2
  63.7 0.0 reduce-scatter.3.cloned.1.call-update
  63.7 0.7 copy-done.2
  64.4 0.1 copy.43
  64.5 0.1 bitcast_or_fusion
  64.5 0.1 reshape.58
  64.6 0.0 copy-start.3
  64.6 8.7 %gather_fusion.1 = s32[1024]{0:T(1024)S(1)} fusion(s32[128,4]{0,1:T(4,128)S(1)} %convert_subtract_fusion, s32[1024]{0:T(1024)S(1)} %reshape.58), kind=kCustom, calls=%fused_computation.1 | custom fusion | bytes 16384 | tf_op jit(solution)/shard_map/jit(take_along_axis)/gather | solution.py:54
  73.3 0.1 reshape.61
  73.4 0.1 compare_and_fusion
  73.5 0.1 reshape.52
  73.6 0.0 copy-done.3
  73.6 0.1 copy.46
  73.7 4.4 %reduce-scatter.5.cloned.1.call-done = bf16[32,3584]{1,0:T(8,128)(2,1)} async-done(((bf16[128,3584]{1,0:T(8,128)(2,1)}), bf16[32,3584]{1,0:T(8,128)(2,1)}) %reduce-scatter.5.cloned.1.call-update) | async-done | bytes 229392 | tf_op jit(solution)/shard_map/reduce_scatter | solution.py:46
  78.2 4.6 %all-to-all-start.1 = ((bf16[4,8,3584]{2,1,0:T(8,128)(2,1)}), bf16[4,8,3584]{2,1,0:T(8,128)(2,1)S(1)}, u32[]{:S(2)}, u32[]{:S(2)}) async-start(bf16[4,8,3584]{2,1,0:T(8,128)(2,1)} %bitcast.62), calls=%async_computation.3 | async-start | bytes 458752 | tf_op jit(solution)/shard_map/all_to_all | solution.py:50
  82.8 8.2 %all-to-all-done.1 = bf16[4,8,3584]{2,1,0:T(8,128)(2,1)S(1)} async-done(((bf16[4,8,3584]{2,1,0:T(8,128)(2,1)}), bf16[4,8,3584]{2,1,0:T(8,128)(2,1)S(1)}, u32[]{:S(2)}, u32[]{:S(2)}) %all-to-all-start.1) | async-done | bytes 229408 | tf_op jit(solution)/shard_map/all_to_all | solution.py:50
  91.0 7.3 %gather_fusion = bf16[1024,3584]{1,0:T(8,128)(2,1)} fusion(bf16[32,3584]{1,0:T(8,128)(2,1)S(1)} %bitcast.57, s32[1024]{0:T(1024)S(1)} %broadcast_clamp_fusion), kind=kCustom, calls=%fused_computation | custom fusion | bytes 14684160 | tf_op jit(solution)/shard_map/jit(_take)/gather | solution.py:58
  98.3 13.7 %multiply_reduce_fusion = f32[128,3584]{1,0:T(8,128)} fusion(bf16[1024,3584]{1,0:T(8,128)(2,1)} %gather_fusion, f32[128,8]{1,0:T(8,128)S(1)} %broadcast_select_fusion, pred[128,8]{1,0:T(8,128)(4,1)S(1)} %get-tuple-element.5), kind=kLoop, calls=%fused_computation.2 | loop fusion | flops 14221312 | bytes 9180160 | tf_op jit(solution)/shard_map/reduce_sum | solution.py:60
  112.0 10.2 %reduce-scatter.3.cloned.1.call-done = bf16[128,3584]{1,0:T(8,128)(2,1)} async-done(((bf16[512,3584]{1,0:T(8,128)(2,1)}), bf16[128,3584]{1,0:T(8,128)(2,1)}) %reduce-scatter.3.cloned.1.call-update) | async-done | bytes 917520 | tf_op jit(solution)/shard_map/reduce_scatter | solution.py:64
  122.2 2.8 %add_convert_fusion = bf16[128,3584]{1,0:T(8,128)(2,1)} fusion(f32[128,3584]{1,0:T(8,128)} %multiply_reduce_fusion, bf16[128,3584]{1,0:T(8,128)(2,1)} %reduce-scatter.3.cloned.1.call-done), kind=kLoop, calls=%fused_computation.12 | loop fusion | flops 1376256 | bytes 3670016 | tf_op jit(solution)/shard_map/convert_element_type | solution.py:67
  (6 shorter events, 0.1 us)
Async XLA Ops:
  6.5 48.7 %copy-start = (bf16[256,3584]{1,0:T(8,128)(2,1)S(1)}, bf16[256,3584]{1,0:T(8,128)(2,1)}, u32[]{:S(2)}) copy-start(bf16[256,3584]{1,0:T(8,128)(2,1)} %param.17) | copy-start | bytes 5505028
  6.5 44.9 %all-gather.2.cloned.1.call-start = ((), (), s32[]{:S(2)}) async-start(), calls=%async_computation.4 | async-start | bytes 4587520 | tf_op jit(solution)/shard_map/all_gather | solution.py:62
  7.3 70.9 %reduce-scatter.5.cloned.1.call-start = ((), (), s32[]{:S(2)}) async-start(), calls=%async_computation.6 | async-start | bytes 1146880 | tf_op jit(solution)/shard_map/reduce_scatter | solution.py:46
  8.5 31.4 %copy-start.4 = (bf16[1,3584,256]{2,1,0:T(8,128)(2,1)S(1)}, bf16[1,3584,256]{2,1,0:T(8,128)(2,1)}, u32[]{:S(2)}) copy-start(bf16[1,3584,256]{2,1,0:T(8,128)(2,1)} %param.12) | copy-start | bytes 5505028
  39.8 1.5 %copy-start.5 = (bf16[1,3584,256]{2,1,0:T(8,128)(2,1)S(1)}, bf16[1,3584,256]{2,1,0:T(8,128)(2,1)}, u32[]{:S(2)}) copy-start(bf16[1,3584,256]{2,1,0:T(8,128)(2,1)} %param.13) | copy-start | bytes 5505028
  41.4 1.5 %copy-start.1 = (bf16[1,256,3584]{2,1,0:T(8,128)(2,1)S(1)}, bf16[1,256,3584]{2,1,0:T(8,128)(2,1)}, u32[]{:S(2)}) copy-start(bf16[1,256,3584]{2,1,0:T(8,128)(2,1)} %param.14) | copy-start | bytes 5505028
  44.2 77.9 %reduce-scatter.3.cloned.1.call-start = ((), (), s32[]{:S(2)}) async-start(), calls=%async_computation.5 | async-start | bytes 4587520 | tf_op jit(solution)/shard_map/reduce_scatter | solution.py:64
  63.7 0.7 copy-start.2
  64.6 9.0 %copy-start.3 = (f32[128,8]{0,1:T(8,128)S(1)}, f32[128,8]{0,1:T(8,128)}, u32[]{:S(2)}) copy-start(f32[128,8]{0,1:T(8,128)} %param.10) | copy-start | bytes 12292
  78.2 12.8 %all-to-all-start.1 = ((bf16[4,8,3584]{2,1,0:T(8,128)(2,1)}), bf16[4,8,3584]{2,1,0:T(8,128)(2,1)S(1)}, u32[]{:S(2)}, u32[]{:S(2)}) async-start(bf16[4,8,3584]{2,1,0:T(8,128)(2,1)} %bitcast.62), calls=%async_computation.3 | async-start | bytes 458752 | tf_op jit(solution)/shard_map/all_to_all | solution.py:50
Sparse Core Ops, SparseCore 0:
  8.9 42.5 all-gather.1
  54.0 24.0 reduce-scatter.4
  80.9 41.2 reduce-scatter.2
where the time goes:
time: 132 us; the launch traced here: 131 us
  waiting for transfers between devices  30.7 us (23%)
  blocking collectives  29.7 us (22%)
  local copies, waits for them, and re-layouts  19.6 us (15%)
  other arithmetic  17.7 us (13%)
  matrix products  15.9 us (12%)
  between operations  13.2 us (10%)
  starting transfers between devices  4.68 us (4%)
    all_to_all x1, blocking collectives, per_device(): lax.all_to_all(spread, ('node', 'local'), split_axis=0, concat_axis=0, ti...  29.7 us
    reduce_sum x1, other arithmetic, per_device(): jnp.sum(capacity_factor[:, :, None] * fetched.astype(jnp.float32), axis=1)  13.7 us
    reduce_scatter x1, waiting for transfers between devices, per_device(): lax.psum_scatter(shared_terms.astype(jnp.bfloat16), 'local', scatter_dime...  10.2 us
    gather x3, local copies, waits for them, and re-layouts, per_device(): destination_slot = jnp.take_along_axis(position, destination_node, axis=1)  8.85 us
    dot_general x1, matrix products, expert_part(): return jnp.dot(hidden, proj_down, preferred_element_type=jnp.float32)  8.47 us
    all_to_all x1, waiting for transfers between devices, per_device(): lax.all_to_all(replies, 'node', split_axis=0, concat_axis=0, tiled=True)  8.16 us
    gather x1, local copies, waits for them, and re-layouts, per_device(): fetched = jnp.take(returned_rows, token_row_index, axis=0)  7.32 us
    all_gather x1, waiting for transfers between devices, per_device(): lax.all_gather(tokens, 'local', axis=0, tiled=True)  7.21 us
  transfers between devices with their start and end apart: 4, of which 4 were waited for; matrix products, arithmetic and copies ran while one was open for 36% of the time, Pallas kernels for 0%

commit v1 on v0

v1 whole, which is shorter than its diff:
```python
import jax
import jax.numpy as jnp
from jax import lax
from jax.experimental import pallas as pl
from jax.experimental.pallas import tpu as pltpu
from jax.sharding import PartitionSpec as P

EXPERTS_PER_NODE = 8
CHUNKS = 2
FEW_NODES = 8


def shift(value, axis, mask):
    size = lax.axis_size(axis)
    return lax.ppermute(value, axis, [(i, i ^ mask) for i in range(size)])


def dispatch_kernel(node_count, capacity, owner_ref, index_ref, gate_ref, tokens_ref, rows_ref, weight_ref):
    count = index_ref.shape[1]
    index = index_ref[...]
    gates = gate_ref[...]
    before = lax.broadcasted_iota(jnp.int32, (count, count), 0)
    after = lax.broadcasted_iota(jnp.int32, (count, count), 1)
    earlier = (before < after).astype(jnp.bfloat16)
    chosen, weights = [], []
    for n in range(node_count):
        match = index == owner_ref[n]
        chosen.append(jnp.max(match.astype(jnp.float32), axis=0, keepdims=True))
        weights.append(jnp.sum(jnp.where(match, gates, 0.0), axis=0, keepdims=True))
    chosen = jnp.concatenate(chosen, axis=0)
    position = jnp.dot(chosen.astype(jnp.bfloat16), earlier, preferred_element_type=jnp.float32)
    slot = lax.broadcasted_iota(jnp.int32, (capacity, count), 0).astype(jnp.float32)
    picks, scaled = [], []
    for n in range(node_count):
        hit = (position[n : n + 1] == slot) & (chosen[n : n + 1] > 0.5)
        picks.append(hit.astype(jnp.float32))
        scaled.append(jnp.where(hit, weights[n], 0.0))
    pick = jnp.concatenate(picks, axis=0).astype(jnp.bfloat16)
    rows_ref[...] = jnp.dot(pick, tokens_ref[...], preferred_element_type=jnp.float32).astype(
        jnp.bfloat16
    )
    weight_ref[...] = jnp.concatenate(scaled, axis=0)


def dispatch(node_count, capacity, index, gates, tokens):
    count, width = tokens.shape
    slots = node_count * capacity
    vmem = pl.BlockSpec(memory_space=pltpu.VMEM)
    nodes = jnp.arange(node_count, dtype=jnp.int32)
    if node_count <= FEW_NODES:
        nodes = nodes ^ lax.axis_index("node")
    return pl.pallas_call(
        lambda *refs: dispatch_kernel(node_count, capacity, *refs),
        out_shape=(
            jax.ShapeDtypeStruct((slots, width), jnp.bfloat16),
            jax.ShapeDtypeStruct((slots, count), jnp.float32),
        ),
        in_specs=[pl.BlockSpec(memory_space=pltpu.SMEM), vmem, vmem, vmem],
        out_specs=(vmem, vmem),
        compiler_params=pltpu.CompilerParams(vmem_limit_bytes=32 * 1024 * 1024),
    )(nodes * EXPERTS_PER_NODE, index.T, gates.T, tokens)


def dot(a, b):
    return jnp.dot(a, b, preferred_element_type=jnp.float32)


def hidden_of(rows, gate, up):
    return (jax.nn.silu(dot(rows, gate)) * dot(rows, up)).astype(jnp.bfloat16)


def over_nodes(blocks):
    if blocks.shape[0] > FEW_NODES:
        return lax.all_to_all(blocks, "node", split_axis=0, concat_axis=0, tiled=True)
    return jnp.stack([shift(blocks[m], "node", m) if m else blocks[0] for m in range(len(blocks))])


def per_device(
    tokens, routing_gate_weight, selected_expert_index, w_gate, w_up, w_down, s_gate, s_up, s_down
):
    node_count = lax.axis_size("node")
    count, width = tokens.shape
    capacity = count // 16
    slots = node_count * capacity

    step = count // CHUNKS
    afar = [shift(tokens[i * step : (i + 1) * step], "local", 2) for i in range(CHUNKS)]
    p_gate, p_up, p_down = (shift(w, "local", 1) for w in (s_gate, s_up, s_down))

    outgoing, weight = dispatch(
        node_count, capacity, selected_expert_index, routing_gate_weight, tokens
    )
    near = over_nodes(outgoing.reshape(node_count, capacity, width)).reshape(slots, width)
    far = shift(near, "local", 2)
    pair = jnp.concatenate([near, far], axis=0)
    every = jnp.concatenate([pair, shift(pair, "local", 1)], axis=0)
    part = dot(hidden_of(every, w_gate[0], w_up[0]), w_down[0])
    mine, other = part[: 2 * slots], part[2 * slots :].astype(jnp.bfloat16)
    chip = mine + shift(other, "local", 1).astype(jnp.float32)
    crossing = shift(chip[slots:].astype(jnp.bfloat16), "local", 2)
    summed = (chip[:slots] + crossing.astype(jnp.float32)).astype(jnp.bfloat16)
    replies = over_nodes(summed.reshape(node_count, capacity, width)).reshape(slots, width)

    def shared_part(rows):
        return dot(hidden_of(rows, s_gate, s_up), s_down) + dot(
            hidden_of(rows, p_gate, p_up), p_down
        )

    own = shared_part(tokens)
    back = [shift(shared_part(rows).astype(jnp.bfloat16), "local", 2) for rows in afar]
    shared = own + jnp.concatenate(back, axis=0).astype(jnp.float32)

    high = weight.astype(jnp.bfloat16)
    low = (weight - high.astype(jnp.float32)).astype(jnp.bfloat16)
    both = jnp.concatenate([high, low], axis=0)
    twice = jnp.concatenate([replies, replies], axis=0)
    routed = lax.dot_general(
        both, twice, (((0,), (0,)), ((), ())), preferred_element_type=jnp.float32
    )
    return (shared + routed).astype(jnp.bfloat16)


def solution(mesh):
    in_specs = (
        P(("groups", "node", "local"), None),
        P(("groups", "node", "local"), None),
        P(("groups", "node", "local"), None),
        P("node", None, "local"),
        P("node", None, "local"),
        P("node", "local", None),
        P(None, "local"),
        P(None, "local"),
        P("local", None),
    )
    out_specs = P(("groups", "node", "local"), None)
    return jax.shard_map(
        per_device, mesh=mesh, in_specs=in_specs, out_specs=out_specs, check_vma=False
    )
```

time: 132 us -> 97.6 us (0.74)
  matrix products: 15.9 us -> 48 us
  blocking collectives: 29.7 us -> 0 us
  waiting for transfers between devices: 30.7 us -> 15.5 us
  starting transfers between devices: 4.68 us -> 19.3 us
  other arithmetic: 17.7 us -> 4.32 us
  between operations: 13.2 us -> 0.15 us
  local copies, waits for them, and re-layouts: 19.6 us -> 8.73 us
    dot_general x6 -> x15, matrix products: 15.9 us -> 48 us  [the longest x14 46.3 us: dot(): return jnp.dot(a, b, preferred_element_type=jnp.float32)]
    all_to_all x1 -> x0, blocking collectives: 29.7 us -> none  [per_device(): lax.all_to_all(spread, ('node', 'local'), split_axis=0, concat_axis=0, ti...]
    ppermute x0 -> x17, starting transfers between devices: none -> 19.3 us  [shift(): return lax.ppermute(value, axis, [(i, i ^ mask) for i in range(size)])]
    gather x4 -> x0, local copies, waits for them, and re-layouts: 16.2 us -> none  [the longest x3 8.85 us: per_device(): destination_slot = jnp.take_along_axis(position, destination_node, axis=1)]
    ppermute x0 -> x17, waiting for transfers between devices: none -> 15.5 us  [shift(): return lax.ppermute(value, axis, [(i, i ^ mask) for i in range(size)])]
    reduce_scatter x2 -> x0, waiting for transfers between devices: 14.6 us -> none  [the longest x1 10.2 us: per_device(): lax.psum_scatter(shared_terms.astype(jnp.bfloat16), 'local', scatter_dime...]
    reduce_sum x1 -> x0, other arithmetic: 13.7 us -> none  [per_device(): jnp.sum(capacity_factor[:, :, None] * fetched.astype(jnp.float32), axis=1)]
    all_to_all x1 -> x0, waiting for transfers between devices: 8.16 us -> none  [per_device(): lax.all_to_all(replies, 'node', split_axis=0, concat_axis=0, tiled=True)]
  transfers between devices with their start and end apart: 4 -> 17, of which waited for: 4 -> 5; matrix products, arithmetic and copies ran while one was open for 36% -> 53% of each run, Pallas kernels for 0% -> 0%
where the time goes in v1:
time: 97.6 us; the launch traced here: 96.9 us
  matrix products  48 us (49%)
  starting transfers between devices  19.3 us (20%)
  waiting for transfers between devices  15.5 us (16%)
  local copies, waits for them, and re-layouts  8.73 us (9%)
  other arithmetic  4.32 us (4%)
    dot_general x14, matrix products, dot(): return jnp.dot(a, b, preferred_element_type=jnp.float32)  46.3 us
    ppermute x17, starting transfers between devices, shift(): return lax.ppermute(value, axis, [(i, i ^ mask) for i in range(size)])  19.3 us
    ppermute x17, waiting for transfers between devices, shift(): return lax.ppermute(value, axis, [(i, i ^ mask) for i in range(size)])  15.5 us
    unnamed x16, local copies, waits for them, and re-layouts  4.38 us
    slice x1, local copies, waits for them, and re-layouts, per_device(): mine, other = (part[:2 * slots], part[2 * slots:].astype(jnp.bfloat16))  1.99 us
  transfers between devices with their start and end apart: 17, of which 5 were waited for; matrix products, arithmetic and copies ran while one was open for 53% of the time, Pallas kernels for 0%

profile of v1, /device:TPU:0, one launch (start us, length us, event | category | flops | bytes accessed | tf_op | source)
XLA Modules:
  0.0 96.9 jit_solution(7626892571134177131)
XLA Ops:
  0.0 1.3 %copy-done.1 = bf16[128,3584]{1,0:T(8,128)(2,1)S(1)} copy-done((bf16[128,3584]{1,0:T(8,128)(2,1)S(1)}, bf16[128,3584]{1,0:T(8,128)(2,1)}, u32[]{:S(2)}) %copy-start.1) | copy-done | bytes 917528
  1.3 0.7 copy-done.3
  2.0 0.7 copy-done.4
  2.7 0.9 shard_map.91
  3.6 3.1 %collective-permute-start.7 = (bf16[8,3584]{1,0:T(8,128)(2,1)S(1)}, bf16[8,3584]{1,0:T(8,128)(2,1)S(1)}, u32[]{:S(2)}, u32[]{:S(2)}) collective-permute-start(bf16[8,3584]{1,0:T(8,128)(2,1)S(1)} %get-tuple-element.20), channel_id=1, source_target_pairs={{0,4},{4,0},{8,12},{12,8},{1,5},{5,1},{9,13},{13,9},{2,6},{6,2},{1... | collective-permute-start | bytes 172040 | tf_op jit(solution)/shard_map/ppermute | solution.py:15
  6.7 2.6 %collective-permute-start.8 = (bf16[8,3584]{1,0:T(8,128)(2,1)S(1)}, bf16[8,3584]{1,0:T(8,128)(2,1)S(1)}, u32[]{:S(2)}, u32[]{:S(2)}) collective-permute-start(bf16[8,3584]{1,0:T(8,128)(2,1)S(1)} %get-tuple-element.19), channel_id=1, source_target_pairs={{0,8},{4,12},{8,0},{12,4},{1,9},{5,13},{9,1},{13,5},{2,10},{6,14},... | collective-permute-start | bytes 172040 | tf_op jit(solution)/shard_map/ppermute | solution.py:15
  9.3 1.0 %fusion.50 = (bf16[64,3584]{1,0:T(8,128)(2,1)}, bf16[64,3584]{1,0:T(8,128)(2,1)}) fusion(bf16[128,3584]{1,0:T(8,128)(2,1)S(1)} %copy-done.1), kind=kLoop, calls=%fused_computation.67 | loop fusion | bytes 1835008 | tf_op jit(solution)/shard_map/slice | solution.py:87
  10.3 1.7 %collective-permute-start.3 = (bf16[64,3584]{1,0:T(8,128)(2,1)}, bf16[64,3584]{1,0:T(8,128)(2,1)S(1)}, u32[]{:S(2)}, u32[]{:S(2)}) collective-permute-start(bf16[64,3584]{1,0:T(8,128)(2,1)} %get-tuple-element.11), channel_id=1, source_target_pairs={{0,2},{1,3},{2,0},{3,1},{4,6},{5,7},{6,4},{7,5},{8,10},{9,11},{10,... | collective-permute-start | bytes 1376264 | tf_op jit(solution)/shard_map/ppermute | solution.py:15
  12.0 2.6 %fusion.61 = f32[128,256]{1,0:T(8,128)} fusion(bf16[128,3584]{1,0:T(8,128)(2,1)S(1)} %copy-done.1, bf16[3584,256]{1,0:T(8,128)(2,1)} %param.15), kind=kOutput, calls=%fused_computation.73 | convolution fusion | flops 234881024 | bytes 2883584 | tf_op jit(solution)/shard_map/dot_general | solution.py:65
  14.6 0.5 collective-permute-start.1
  15.2 0.1 collective-permute-done.9
  15.3 1.6 %collective-permute-start.10 = (bf16[32,3584]{1,0:T(8,128)(2,1)S(1)}, bf16[32,3584]{1,0:T(8,128)(2,1)}, u32[]{:S(2)}, u32[]{:S(2)}) collective-permute-start(bf16[32,3584]{1,0:T(8,128)(2,1)S(1)} %maximum_bitcast_fusion), channel_id=1, source_target_pairs={{0,2},{1,3},{2,0},{3,1},{4,6},{5,7},{6,4},{7,5},{8,10},{9,11},{10,... | collective-permute-start | bytes 688136 | tf_op jit(solution)/shard_map/ppermute | solution.py:15
  16.9 4.6 %fusion.12 = f32[128,3584]{1,0:T(8,128)} fusion(bf16[256,3584]{1,0:T(8,128)(2,1)} %param.17, bf16[128,3584]{1,0:T(8,128)(2,1)S(1)} %copy-done.2, bf16[3584,256]{1,0:T(8,128)(2,1)} %param.16, f32[128,256]{1,0:T(8,128)} %fusion.61), kind=kOutput, calls=%fused_computation.16 | convolution fusion | flops 469958656 | bytes 6553600 | tf_op jit(solution)/shard_map/dot_general | solution.py:65
  21.5 5.8 %collective-permute-done.10 = bf16[32,3584]{1,0:T(8,128)(2,1)} collective-permute-done((bf16[32,3584]{1,0:T(8,128)(2,1)S(1)}, bf16[32,3584]{1,0:T(8,128)(2,1)}, u32[]{:S(2)}, u32[]{:S(2)}) %collective-permute-start.10) | collective-permute-done | bytes 229408 | tf_op jit(solution)/shard_map/ppermute | solution.py:15
  27.3 1.0 pad_maximum_fusion.1
  28.2 0.1 collective-permute-start.11
  28.3 1.6 %collective-permute-start.5 = (bf16[64,3584]{1,0:T(8,128)(2,1)}, bf16[64,3584]{1,0:T(8,128)(2,1)}, u32[]{:S(2)}, u32[]{:S(2)}) collective-permute-start(bf16[64,3584]{1,0:T(8,128)(2,1)} %get-tuple-element.12), channel_id=1, source_target_pairs={{0,2},{1,3},{2,0},{3,1},{4,6},{5,7},{6,4},{7,5},{8,10},{9,11},{10,... | collective-permute-start | bytes 1376264 | tf_op jit(solution)/shard_map/ppermute | solution.py:15
  29.9 1.9 %fusion.63 = f32[64,256]{1,0:T(8,128)S(1)} fusion(bf16[64,3584]{1,0:T(8,128)(2,1)S(1)} %collective-permute-done.3, bf16[3584,256]{1,0:T(8,128)(2,1)} %param.15), kind=kOutput, calls=%fused_computation.75 | convolution fusion | flops 117440512 | bytes 2359296 | tf_op jit(solution)/shard_map/dot_general | solution.py:65
  31.8 0.8 copy-done.6
  32.6 2.0 %fusion.7 = f32[128,256]{1,0:T(8,128)} fusion(bf16[1,3584,256]{2,1,0:T(8,128)(2,1)S(1)} %copy-done.7, bf16[64,3584]{1,0:T(8,128)(2,1)S(1)} %collective-permute-done.11, bf16[32,3584]{1,0:T(8,128)(2,1)} %collective-permute-done.10, bf16[32,3584]{1,0:T(8,128)(2,1)S(1)} %maximum_bitcast_fusion), kind=kOutput, calls=%fused_computation.10 | convolution fusion | flops 237633536 | bytes 2883584 | tf_op jit(solution)/shard_map/dot_general | solution.py:65
  34.6 4.3 %fusion.5 = f32[128,3584]{1,0:T(8,128)} fusion(bf16[1,256,3584]{2,1,0:T(8,128)(2,1)S(1)} %copy-done, f32[128,256]{1,0:T(8,128)} %fusion.7, bf16[1,3584,256]{2,1,0:T(8,128)(2,1)} %param.12, bf16[64,3584]{1,0:T(8,128)(2,1)} %copy-done.6, bf16[32,3584]{1,0:T(8,128)(2,1)} %collective-permute-done.10, bf16[32,3584]{1,0:T(8,128)(2,1)S(1)} %maximum_bitcast_fusion), kind=kOutput, calls=%fused_computation.8 | convolution fusion | flops 472711168 | bytes 6553600 | tf_op jit(solution)/shard_map/dot_general | solution.py:65
  38.9 2.0 %slice.88 = bf16[64,3584]{1,0:T(8,128)(2,1)} slice(f32[128,3584]{1,0:T(8,128)} %fusion.5), slice={[64:128], [0:3584]} | slice | bytes 917504 | tf_op jit(solution)/shard_map/slice | solution.py:98
  40.9 0.2 collective-permute-start.12
  41.1 0.5 collective-permute-done.5
  41.6 2.1 %fusion.65 = f32[64,256]{1,0:T(8,128)S(1)} fusion(bf16[64,3584]{1,0:T(8,128)(2,1)} %collective-permute-done.5, bf16[3584,256]{1,0:T(8,128)(2,1)} %param.15), kind=kOutput, calls=%fused_computation.77 | convolution fusion | flops 117440512 | bytes 2359296 | tf_op jit(solution)/shard_map/dot_general | solution.py:65
  43.7 4.2 %fusion.30 = f32[64,3584]{1,0:T(8,128)} fusion(bf16[256,3584]{1,0:T(8,128)(2,1)} %param.17, f32[64,256]{1,0:T(8,128)S(1)} %fusion.63, bf16[64,3584]{1,0:T(8,128)(2,1)S(1)} %collective-permute-done.3, bf16[3584,256]{1,0:T(8,128)(2,1)} %param.16), kind=kOutput, calls=%fused_computation.46 | convolution fusion | flops 234979328 | bytes 5111808 | tf_op jit(solution)/shard_map/dot_general | solution.py:65
  47.9 1.4 %slice_add_fusion = f32[64,3584]{1,0:T(8,128)S(1)} fusion(f32[128,3584]{1,0:T(8,128)} %fusion.5, bf16[64,3584]{1,0:T(8,128)(2,1)} %collective-permute-done.12), kind=kLoop, calls=%fused_computation.18 | loop fusion | flops 458752 | bytes 2293760 | tf_op jit(solution)/shard_map/add | solution.py:99
  49.3 0.9 copy-done.5
  50.2 0.7 slice.89
  51.0 1.5 %collective-permute-start.13 = (bf16[32,3584]{1,0:T(8,128)(2,1)}, bf16[32,3584]{1,0:T(8,128)(2,1)S(1)}, u32[]{:S(2)}, u32[]{:S(2)}) collective-permute-start(bf16[32,3584]{1,0:T(8,128)(2,1)} %slice.89), channel_id=1, source_target_pairs={{0,2},{1,3},{2,0},{3,1},{4,6},{5,7},{6,4},{7,5},{8,10},{9,11},{10,... | collective-permute-start | bytes 688136 | tf_op jit(solution)/shard_map/ppermute | solution.py:15
  52.4 4.4 %fusion.31 = f32[64,3584]{1,0:T(8,128)} fusion(bf16[256,3584]{1,0:T(8,128)(2,1)} %param.17, f32[64,256]{1,0:T(8,128)S(1)} %fusion.65, bf16[64,3584]{1,0:T(8,128)(2,1)} %collective-permute-done.5, bf16[3584,256]{1,0:T(8,128)(2,1)} %param.16), kind=kOutput, calls=%fused_computation.47 | convolution fusion | flops 234979328 | bytes 5111808 | tf_op jit(solution)/shard_map/dot_general | solution.py:65
  56.9 1.6 %collective-permute-done.13 = bf16[32,3584]{1,0:T(8,128)(2,1)S(1)} collective-permute-done((bf16[32,3584]{1,0:T(8,128)(2,1)}, bf16[32,3584]{1,0:T(8,128)(2,1)S(1)}, u32[]{:S(2)}, u32[]{:S(2)}) %collective-permute-start.13) | collective-permute-done | bytes 229408 | tf_op jit(solution)/shard_map/ppermute | solution.py:15
  58.5 1.1 %fusion.13 = bf16[32,3584]{1,0:T(8,128)(2,1)S(1)} fusion(f32[64,3584]{1,0:T(8,128)} %copy-done.5, bf16[32,3584]{1,0:T(8,128)(2,1)S(1)} %collective-permute-done.13), kind=kLoop, calls=%fused_computation.22 | loop fusion | flops 344064 | bytes 917504 | tf_op jit(solution)/shard_map/convert_element_type | solution.py:101
  59.5 0.6 slice_bitcast_fusion
  60.2 0.6 collective-permute-start.14
  60.8 3.5 %collective-permute-start.15 = (bf16[8,3584]{1,0:T(8,128)(2,1)S(1)}, bf16[8,3584]{1,0:T(8,128)(2,1)}, u32[]{:S(2)}, u32[]{:S(2)}) collective-permute-start(bf16[8,3584]{1,0:T(8,128)(2,1)S(1)} %get-tuple-element.15), channel_id=1, source_target_pairs={{0,8},{4,12},{8,0},{12,4},{1,9},{5,13},{9,1},{13,5},{2,10},{6,14},... | collective-permute-start | bytes 172040 | tf_op jit(solution)/shard_map/ppermute | solution.py:15
  64.3 0.3 collective-permute-start.16
  64.6 1.9 %fusion.64 = f32[64,256]{1,0:T(8,128)S(1)} fusion(bf16[64,3584]{1,0:T(8,128)(2,1)S(1)} %collective-permute-done.3, bf16[3584,256]{1,0:T(8,128)(2,1)} %collective-permute-done), kind=kOutput, calls=%fused_computation.76 | convolution fusion | flops 117440512 | bytes 2359296 | tf_op jit(solution)/shard_map/dot_general | solution.py:65
  66.5 4.3 %fusion.3 = bf16[64,3584]{1,0:T(8,128)(2,1)} fusion(f32[64,3584]{1,0:T(8,128)} %fusion.30, bf16[256,3584]{1,0:T(8,128)(2,1)} %collective-permute-done.2, f32[64,256]{1,0:T(8,128)S(1)} %fusion.64, bf16[64,3584]{1,0:T(8,128)(2,1)S(1)} %collective-permute-done.3, bf16[3584,256]{1,0:T(8,128)(2,1)} %collective-permute-done.1), kind=kOutput, calls=%fused_computation.6 | convolution fusion | flops 235438080 | bytes 5570560 | tf_op jit(solution)/shard_map/dot_general | solution.py:65
  70.9 1.4 %collective-permute-start.4 = (bf16[64,3584]{1,0:T(8,128)(2,1)}, bf16[64,3584]{1,0:T(8,128)(2,1)}, u32[]{:S(2)}, u32[]{:S(2)}) collective-permute-start(bf16[64,3584]{1,0:T(8,128)(2,1)} %fusion.3), channel_id=1, source_target_pairs={{0,2},{1,3},{2,0},{3,1},{4,6},{5,7},{6,4},{7,5},{8,10},{9,11},{10,... | collective-permute-start | bytes 1376264 | tf_op jit(solution)/shard_map/ppermute | solution.py:15
  72.3 2.1 %fusion.66 = f32[64,256]{1,0:T(8,128)S(1)} fusion(bf16[64,3584]{1,0:T(8,128)(2,1)} %collective-permute-done.5, bf16[3584,256]{1,0:T(8,128)(2,1)} %collective-permute-done), kind=kOutput, calls=%fused_computation.78 | convolution fusion | flops 117440512 | bytes 2359296 | tf_op jit(solution)/shard_map/dot_general | solution.py:65
  74.3 4.4 %fusion.4 = bf16[64,3584]{1,0:T(8,128)(2,1)} fusion(f32[64,3584]{1,0:T(8,128)} %fusion.31, bf16[256,3584]{1,0:T(8,128)(2,1)} %collective-permute-done.2, f32[64,256]{1,0:T(8,128)S(1)} %fusion.66, bf16[64,3584]{1,0:T(8,128)(2,1)} %collective-permute-done.5, bf16[3584,256]{1,0:T(8,128)(2,1)} %collective-permute-done.1), kind=kOutput, calls=%fused_computation.7 | convolution fusion | flops 235438080 | bytes 5570560 | tf_op jit(solution)/shard_map/dot_general | solution.py:65
  78.8 0.6 collective-permute-start.6
  79.4 0.9 maximum_bitcast_fusion.1
  80.3 1.8 %fusion.14 = f32[128,3584]{1,0:T(8,128)} fusion(bf16[32,3584]{1,0:T(8,128)(2,1)S(1)} %maximum_bitcast_fusion.1, bf16[32,128]{1,0:T(8,128)(2,1)S(1)} %get-tuple-element.9, bf16[32,128]{1,0:T(8,128)(2,1)S(1)} %get-tuple-element.10), kind=kOutput, calls=%fused_computation.24 | convolution fusion | flops 59670528 | bytes 2080768 | tf_op jit(solution)/shard_map/dot_general | solution.py:117
  82.1 1.9 %fusion.62 = f32[128,256]{1,0:T(8,128)S(1)} fusion(bf16[128,3584]{1,0:T(8,128)(2,1)S(1)} %copy-done.2, bf16[3584,256]{1,0:T(8,128)(2,1)} %collective-permute-done), kind=kOutput, calls=%fused_computation.74 | convolution fusion | flops 234881024 | bytes 2883584 | tf_op jit(solution)/shard_map/dot_general | solution.py:65
  84.0 7.5 %collective-permute-done.6 = bf16[64,3584]{1,0:T(8,128)(2,1)} collective-permute-done((bf16[64,3584]{1,0:T(8,128)(2,1)}, bf16[64,3584]{1,0:T(8,128)(2,1)}, u32[]{:S(2)}, u32[]{:S(2)}) %collective-permute-start.6) | collective-permute-done | bytes 458784 | tf_op jit(solution)/shard_map/ppermute | solution.py:15
  91.5 5.4 %fusion.2 = bf16[128,3584]{1,0:T(8,128)(2,1)} fusion(f32[128,3584]{1,0:T(8,128)} %fusion.14, f32[128,3584]{1,0:T(8,128)} %fusion.12, bf16[256,3584]{1,0:T(8,128)(2,1)} %collective-permute-done.2, bf16[64,3584]{1,0:T(8,128)(2,1)} %collective-permute-done.6, bf16[64,3584]{1,0:T(8,128)(2,1)} %collective-permute-done.4, f32[128,256]{1,0:T(8,128)S(1)} %fusion.62, ...), kind=kOutput, calls=%fused_computation.3 | convolution fusion | flops 473628672 | bytes 10223616 | tf_op jit(solution)/shard_map/dot_general | solution.py:65
  (30 shorter events, 0.2 us)
Async XLA Ops:
  0.0 34.6 %copy-start = (bf16[1,256,3584]{2,1,0:T(8,128)(2,1)S(1)}, bf16[1,256,3584]{2,1,0:T(8,128)(2,1)}, u32[]{:S(2)}) copy-start(bf16[1,256,3584]{2,1,0:T(8,128)(2,1)} %param.14) | copy-start | bytes 5505028
  0.0 1.3 %copy-start.1 = (bf16[128,3584]{1,0:T(8,128)(2,1)S(1)}, bf16[128,3584]{1,0:T(8,128)(2,1)}, u32[]{:S(2)}) copy-start(bf16[128,3584]{1,0:T(8,128)(2,1)} %refs_3_.1) | copy-start | bytes 2752516
  1.3 0.7 copy-start.3
  2.0 0.7 copy-start.4
  3.6 11.0 %collective-permute-start.7 = (bf16[8,3584]{1,0:T(8,128)(2,1)S(1)}, bf16[8,3584]{1,0:T(8,128)(2,1)S(1)}, u32[]{:S(2)}, u32[]{:S(2)}) collective-permute-start(bf16[8,3584]{1,0:T(8,128)(2,1)S(1)} %get-tuple-element.20), channel_id=1, source_target_pairs={{0,4},{4,0},{8,12},{12,8},{1,5},{5,1},{9,13},{13,9},{2,6},{6,2},{1... | collective-permute-start | bytes 172040 | tf_op jit(solution)/shard_map/ppermute | solution.py:15
  6.7 8.4 %collective-permute-start.8 = (bf16[8,3584]{1,0:T(8,128)(2,1)S(1)}, bf16[8,3584]{1,0:T(8,128)(2,1)S(1)}, u32[]{:S(2)}, u32[]{:S(2)}) collective-permute-start(bf16[8,3584]{1,0:T(8,128)(2,1)S(1)} %get-tuple-element.19), channel_id=1, source_target_pairs={{0,8},{4,12},{8,0},{12,4},{1,9},{5,13},{9,1},{13,5},{2,10},{6,14},... | collective-permute-start | bytes 172040 | tf_op jit(solution)/shard_map/ppermute | solution.py:15
  9.3 6.0 %collective-permute-start.9 = (bf16[8,3584]{1,0:T(8,128)(2,1)S(1)}, bf16[8,3584]{1,0:T(8,128)(2,1)S(1)}, u32[]{:S(2)}, u32[]{:S(2)}) collective-permute-start(bf16[8,3584]{1,0:T(8,128)(2,1)S(1)} %get-tuple-element.18), channel_id=1, source_target_pairs={{0,12},{4,8},{8,4},{12,0},{1,13},{5,9},{9,5},{13,1},{2,14},{6,10},... | collective-permute-start | bytes 172040 | tf_op jit(solution)/shard_map/ppermute | solution.py:15
  10.3 6.6 %copy-start.2 = (bf16[128,3584]{1,0:T(8,128)(2,1)S(1)}, bf16[128,3584]{1,0:T(8,128)(2,1)}, u32[]{:S(2)}) copy-start(bf16[128,3584]{1,0:T(8,128)(2,1)} %refs_3_.1) | copy-start | bytes 2752516
  10.3 18.0 %collective-permute-start.3 = (bf16[64,3584]{1,0:T(8,128)(2,1)}, bf16[64,3584]{1,0:T(8,128)(2,1)S(1)}, u32[]{:S(2)}, u32[]{:S(2)}) collective-permute-start(bf16[64,3584]{1,0:T(8,128)(2,1)} %get-tuple-element.11), channel_id=1, source_target_pairs={{0,2},{1,3},{2,0},{3,1},{4,6},{5,7},{6,4},{7,5},{8,10},{9,11},{10,... | collective-permute-start | bytes 1376264 | tf_op jit(solution)/shard_map/ppermute | solution.py:15
  12.0 52.2 %collective-permute-start = (bf16[3584,256]{1,0:T(8,128)(2,1)}, bf16[3584,256]{1,0:T(8,128)(2,1)}, u32[]{:S(2)}, u32[]{:S(2)}) collective-permute-start(bf16[3584,256]{1,0:T(8,128)(2,1)} %param.15), channel_id=1, source_target_pairs={{0,1},{1,0},{2,3},{3,2},{4,5},{5,4},{6,7},{7,6},{8,9},{9,8},{10,11... | collective-permute-start | bytes 5505032 | tf_op jit(solution)/shard_map/ppermute | solution.py:15
  14.6 51.9 %collective-permute-start.1 = (bf16[3584,256]{1,0:T(8,128)(2,1)}, bf16[3584,256]{1,0:T(8,128)(2,1)}, u32[]{:S(2)}, u32[]{:S(2)}) collective-permute-start(bf16[3584,256]{1,0:T(8,128)(2,1)} %param.16), channel_id=1, source_target_pairs={{0,1},{1,0},{2,3},{3,2},{4,5},{5,4},{6,7},{7,6},{8,9},{9,8},{10,11... | collective-permute-start | bytes 5505032 | tf_op jit(solution)/shard_map/ppermute | solution.py:15
  15.1 51.4 %collective-permute-start.2 = (bf16[256,3584]{1,0:T(8,128)(2,1)}, bf16[256,3584]{1,0:T(8,128)(2,1)}, u32[]{:S(2)}, u32[]{:S(2)}) collective-permute-start(bf16[256,3584]{1,0:T(8,128)(2,1)} %param.17), channel_id=1, source_target_pairs={{0,1},{1,0},{2,3},{3,2},{4,5},{5,4},{6,7},{7,6},{8,9},{9,8},{10,11... | collective-permute-start | bytes 5505032 | tf_op jit(solution)/shard_map/ppermute | solution.py:15
  15.3 11.9 %collective-permute-start.10 = (bf16[32,3584]{1,0:T(8,128)(2,1)S(1)}, bf16[32,3584]{1,0:T(8,128)(2,1)}, u32[]{:S(2)}, u32[]{:S(2)}) collective-permute-start(bf16[32,3584]{1,0:T(8,128)(2,1)S(1)} %maximum_bitcast_fusion), channel_id=1, source_target_pairs={{0,2},{1,3},{2,0},{3,1},{4,6},{5,7},{6,4},{7,5},{8,10},{9,11},{10,... | collective-permute-start | bytes 688136 | tf_op jit(solution)/shard_map/ppermute | solution.py:15
  21.5 11.1 %copy-start.7 = (bf16[1,3584,256]{2,1,0:T(8,128)(2,1)S(1)}, bf16[1,3584,256]{2,1,0:T(8,128)(2,1)}, u32[]{:S(2)}) copy-start(bf16[1,3584,256]{2,1,0:T(8,128)(2,1)} %param.13) | copy-start | bytes 5505028
  28.2 3.6 %collective-permute-start.11 = (bf16[64,3584]{1,0:T(8,128)(2,1)S(1)}, bf16[64,3584]{1,0:T(8,128)(2,1)S(1)}, u32[]{:S(2)}, u32[]{:S(2)}) collective-permute-start(bf16[64,3584]{1,0:T(8,128)(2,1)S(1)} %pad_maximum_fusion.1), channel_id=1, source_target_pairs={{0,1},{1,0},{2,3},{3,2},{4,5},{5,4},{6,7},{7,6},{8,9},{9,8},{10,11... | collective-permute-start | bytes 1376264 | tf_op jit(solution)/shard_map/ppermute | solution.py:15
  28.3 13.3 %collective-permute-start.5 = (bf16[64,3584]{1,0:T(8,128)(2,1)}, bf16[64,3584]{1,0:T(8,128)(2,1)}, u32[]{:S(2)}, u32[]{:S(2)}) collective-permute-start(bf16[64,3584]{1,0:T(8,128)(2,1)} %get-tuple-element.12), channel_id=1, source_target_pairs={{0,2},{1,3},{2,0},{3,1},{4,6},{5,7},{6,4},{7,5},{8,10},{9,11},{10,... | collective-permute-start | bytes 1376264 | tf_op jit(solution)/shard_map/ppermute | solution.py:15
  31.8 0.8 copy-start.6
  40.9 7.0 %collective-permute-start.12 = (bf16[64,3584]{1,0:T(8,128)(2,1)}, bf16[64,3584]{1,0:T(8,128)(2,1)}, u32[]{:S(2)}, u32[]{:S(2)}) collective-permute-start(bf16[64,3584]{1,0:T(8,128)(2,1)} %slice.88), channel_id=1, source_target_pairs={{0,1},{1,0},{2,3},{3,2},{4,5},{5,4},{6,7},{7,6},{8,9},{9,8},{10,11... | collective-permute-start | bytes 1376264 | tf_op jit(solution)/shard_map/ppermute | solution.py:15
  49.3 0.9 copy-start.5
  51.0 7.5 %collective-permute-start.13 = (bf16[32,3584]{1,0:T(8,128)(2,1)}, bf16[32,3584]{1,0:T(8,128)(2,1)S(1)}, u32[]{:S(2)}, u32[]{:S(2)}) collective-permute-start(bf16[32,3584]{1,0:T(8,128)(2,1)} %slice.89), channel_id=1, source_target_pairs={{0,2},{1,3},{2,0},{3,1},{4,6},{5,7},{6,4},{7,5},{8,10},{9,11},{10,... | collective-permute-start | bytes 688136 | tf_op jit(solution)/shard_map/ppermute | solution.py:15
  60.2 19.2 %collective-permute-start.14 = (bf16[8,3584]{1,0:T(8,128)(2,1)}, bf16[8,3584]{1,0:T(8,128)(2,1)S(1)}, u32[]{:S(2)}, u32[]{:S(2)}) collective-permute-start(bf16[8,3584]{1,0:T(8,128)(2,1)} %get-tuple-element.16), channel_id=1, source_target_pairs={{0,4},{4,0},{8,12},{12,8},{1,5},{5,1},{9,13},{13,9},{2,6},{6,2},{1... | collective-permute-start | bytes 172040 | tf_op jit(solution)/shard_map/ppermute | solution.py:15
  60.8 18.6 %collective-permute-start.15 = (bf16[8,3584]{1,0:T(8,128)(2,1)S(1)}, bf16[8,3584]{1,0:T(8,128)(2,1)}, u32[]{:S(2)}, u32[]{:S(2)}) collective-permute-start(bf16[8,3584]{1,0:T(8,128)(2,1)S(1)} %get-tuple-element.15), channel_id=1, source_target_pairs={{0,8},{4,12},{8,0},{12,4},{1,9},{5,13},{9,1},{13,5},{2,10},{6,14},... | collective-permute-start | bytes 172040 | tf_op jit(solution)/shard_map/ppermute | solution.py:15
  64.3 15.2 %collective-permute-start.16 = (bf16[8,3584]{1,0:T(8,128)(2,1)S(1)}, bf16[8,3584]{1,0:T(8,128)(2,1)}, u32[]{:S(2)}, u32[]{:S(2)}) collective-permute-start(bf16[8,3584]{1,0:T(8,128)(2,1)S(1)} %get-tuple-element.14), channel_id=1, source_target_pairs={{0,12},{4,8},{8,4},{12,0},{1,13},{5,9},{9,5},{13,1},{2,14},{6,10},... | collective-permute-start | bytes 172040 | tf_op jit(solution)/shard_map/ppermute | solution.py:15
  70.9 13.1 %collective-permute-start.4 = (bf16[64,3584]{1,0:T(8,128)(2,1)}, bf16[64,3584]{1,0:T(8,128)(2,1)}, u32[]{:S(2)}, u32[]{:S(2)}) collective-permute-start(bf16[64,3584]{1,0:T(8,128)(2,1)} %fusion.3), channel_id=1, source_target_pairs={{0,2},{1,3},{2,0},{3,1},{4,6},{5,7},{6,4},{7,5},{8,10},{9,11},{10,... | collective-permute-start | bytes 1376264 | tf_op jit(solution)/shard_map/ppermute | solution.py:15
  78.8 12.7 %collective-permute-start.6 = (bf16[64,3584]{1,0:T(8,128)(2,1)}, bf16[64,3584]{1,0:T(8,128)(2,1)}, u32[]{:S(2)}, u32[]{:S(2)}) collective-permute-start(bf16[64,3584]{1,0:T(8,128)(2,1)} %fusion.4), channel_id=1, source_target_pairs={{0,2},{1,3},{2,0},{3,1},{4,6},{5,7},{6,4},{7,5},{8,10},{9,11},{10,... | collective-permute-start | bytes 1376264 | tf_op jit(solution)/shard_map/ppermute | solution.py:15

commit v2 on v0

v2 whole, which is shorter than its diff:
```python
import jax
import jax.numpy as jnp
from jax import lax
from jax.experimental import pallas as pl
from jax.experimental.pallas import tpu as pltpu
from jax.sharding import PartitionSpec as P

EXPERTS_PER_NODE = 8
FEW_NODES = 8
PIECES = 4
HBM = pl.BlockSpec(memory_space=pltpu.HBM)
VMEM = pl.BlockSpec(memory_space=pltpu.VMEM)
SMEM = pl.BlockSpec(memory_space=pltpu.SMEM)
ROWS = (((0,), (0,)), ((), ()))
COLS = (((1,), (1,)), ((), ()))


def shift(value, axis, mask):
    size = lax.axis_size(axis)
    return lax.ppermute(value, axis, [(i, i ^ mask) for i in range(size)])


def over_nodes(pieces):
    count = len(pieces)
    if count > FEW_NODES:
        moved = lax.all_to_all(jnp.stack(pieces), "node", split_axis=0, concat_axis=0, tiled=True)
        return [moved[n] for n in range(count)]
    return [shift(piece, "node", m) if m else piece for m, piece in enumerate(pieces)]


def dot(a, b, dims=(((1,), (0,)), ((), ()))):
    return lax.dot_general(a, b, dims, preferred_element_type=jnp.float32)


def bf16(value):
    return value.astype(jnp.bfloat16)


def struct(rows, cols, dtype=jnp.bfloat16):
    return jax.ShapeDtypeStruct((rows, cols), dtype)


def call(kernel, outs, args, specs=None, scratch=(), room=0, flops=0):
    return pl.pallas_call(
        kernel,
        out_shape=outs,
        in_specs=specs or [VMEM] * len(args),
        out_specs=jax.tree.map(lambda _: VMEM, outs),
        scratch_shapes=scratch,
        cost_estimate=pl.CostEstimate(flops=flops, bytes_accessed=0, transcendentals=0),
        compiler_params=pltpu.CompilerParams(vmem_limit_bytes=(8 << 20) + room),
    )(*args)


def head_kernel(
    nodes, block, owner_ref, index_hbm, gate_hbm, tokens_hbm,
    first_ref, mix_ref, pick_ref, tokens_ref, index_ref, gate_ref, sems,
):
    copies = [
        pltpu.make_async_copy(index_hbm, index_ref, sems.at[0]),
        pltpu.make_async_copy(gate_hbm, gate_ref, sems.at[1]),
        pltpu.make_async_copy(tokens_hbm, tokens_ref, sems.at[2]),
    ]
    for copy in copies:
        copy.start()
    count, width = tokens_ref.shape
    head = first_ref.shape[0]
    row = lax.broadcasted_iota(jnp.int32, (count, count), 0)
    col = lax.broadcasted_iota(jnp.int32, (count, count), 1)
    earlier = bf16((row < col).astype(jnp.float32))
    copies[0].wait()
    copies[1].wait()
    index = index_ref[...]
    gates = gate_ref[...]
    chosen, weights = [], []
    for n in range(nodes):
        match = index == owner_ref[n]
        chosen.append(jnp.max(match.astype(jnp.float32), axis=0, keepdims=True))
        weights.append(jnp.sum(jnp.where(match, gates, 0.0), axis=0, keepdims=True))
    wanted = jnp.max(jnp.concatenate(chosen, axis=0), axis=0, keepdims=True)
    flags = jnp.concatenate(chosen + [wanted] + [jnp.zeros_like(wanted)] * (-(nodes + 1) % 8), axis=0)
    position = dot(bf16(flags), earlier)
    ahead = position[nodes : nodes + 1]
    total = jnp.sum(wanted)
    place = lax.broadcasted_iota(jnp.int32, (1, count), 1).astype(jnp.float32)
    rank = jnp.where(wanted > 0.5, ahead, total + place - ahead)
    order = bf16((rank == row.astype(jnp.float32)).astype(jnp.float32))
    slot = lax.broadcasted_iota(jnp.int32, (block, count), 0).astype(jnp.float32)
    picks, own, other = [], [], []
    for n in range(nodes):
        here = (position[n : n + 1] == slot) & (chosen[n] > 0.5)
        there = (position[n : n + 1] + block // 2 == slot) & (chosen[n] > 0.5)
        picks.append(here.astype(jnp.float32))
        own.append(jnp.where(here, weights[n], 0.0))
        other.append(jnp.where(there, weights[n], 0.0))
    own = jnp.concatenate(own, axis=0)
    other = jnp.concatenate(other, axis=0)
    own_high, other_high = bf16(own), bf16(other)
    own_low = bf16(own - own_high.astype(jnp.float32))
    other_low = bf16(other - other_high.astype(jnp.float32))
    slots = nodes * block
    mix_ref[:count] = order
    mix_ref[count : count + slots] = own_high
    mix_ref[count + slots :] = own_low
    pick_ref[...] = bf16(jnp.concatenate(picks, axis=0))
    first_ref[:, width : width + slots] = bf16(dot(order[:head], other_high, COLS))
    first_ref[:, width + slots :] = bf16(dot(order[:head], other_low, COLS))
    copies[2].wait()
    first_ref[:, :width] = bf16(dot(order[:head], tokens_ref[...]))


def tail_kernel(head, mix_ref, pick_ref, tokens_ref, near_ref, rest_ref=None):
    tokens = tokens_ref[...]
    if rest_ref is not None:
        rest_ref[...] = bf16(dot(mix_ref[head : tokens_ref.shape[0]], tokens))
    near_ref[...] = bf16(dot(pick_ref[...], tokens))


def join_kernel(block, near_ref, first_ref, *outs):
    slots, width = near_ref.shape
    high = first_ref[:, width : width + slots].astype(jnp.float32)
    pick = bf16((high != 0.0).astype(jnp.float32))
    far = dot(pick, first_ref[:, :width], ROWS)
    both = near_ref[...].astype(jnp.float32) + far
    for n, out in enumerate(outs):
        out[...] = bf16(both[n * block : (n + 1) * block])


def mlp(rows, gate, up, down):
    v = dot(rows, gate[...])
    hidden = bf16(v / (1.0 + jnp.exp(-v)) * dot(rows, up[...]))
    return dot(hidden, down[...])


def expert_kernel(nodes, *refs):
    rows = [r[...] for r in refs[:nodes]]
    mats, outs = refs[nodes : nodes + 6], refs[nodes + 6 :]
    block = rows[0].shape[0]
    rows = jnp.concatenate(rows, axis=0)
    part = mlp(rows, *mats[:3]) + mlp(rows, *mats[3:])
    for n, out in enumerate(outs):
        out[...] = bf16(part[n * block : (n + 1) * block])


def own_kernel(
    tokens_ref, gate, up, down, sg_hbm, su_hbm, sd_hbm, wg_hbm, wu_hbm, wd_hbm,
    own_ref, sg, su, sd, wg, wu, wd, sems,
):
    pairs = zip((sg_hbm, su_hbm, sd_hbm, wg_hbm, wu_hbm, wd_hbm), (sg, su, sd, wg, wu, wd))
    copies = [pltpu.make_async_copy(a, b, sems.at[i]) for i, (a, b) in enumerate(pairs)]
    for copy in copies:
        copy.start()
    rows = tokens_ref[...]
    own_ref[...] = mlp(rows, gate, up, down)
    for copy in copies[:3]:
        copy.wait()
    own_ref[...] += mlp(rows, sg, su, sd)
    for copy in copies[3:]:
        copy.wait()


def far_kernel(groups, *refs):
    ins, mats, outs = refs[:groups], refs[groups : groups + 6], refs[groups + 6 :]
    rows = jnp.concatenate([r[:, : outs[0].shape[1]] for r in ins], axis=0)
    sums = mlp(rows, *mats[:3]) + mlp(rows, *mats[3:])
    start = 0
    for out in outs:
        out[...] = sums[start : start + out.shape[0]].astype(out.dtype)
        start += out.shape[0]


def fold_kernel(part_ref, first_ref, *refs):
    width = part_ref.shape[1]
    replies = jnp.concatenate([r[...] for r in refs[:-1]], axis=0)
    slots = replies.shape[0]
    high = first_ref[:, width : width + slots]
    low = first_ref[:, width + slots :]
    refs[-1][...] = bf16(part_ref[...] + dot(high, replies) + dot(low, replies))


def final_kernel(back_count, *refs):
    own_ref, mix_ref = refs[:2]
    backs, replies = refs[2 : 2 + back_count], refs[2 + back_count : -3]
    out_hbm, out_ref, sems = refs[-3:]
    width = out_ref.shape[1]
    tile = width // PIECES
    copies = []
    for i in range(PIECES):
        cols = slice(i * tile, (i + 1) * tile)
        reply = [r[:, cols] for r in replies]
        terms = jnp.concatenate([*[r[:, cols] for r in backs], *reply, *reply], axis=0)
        out_ref[:, cols] = bf16(own_ref[:, cols] + dot(mix_ref[...], terms, ROWS))
        copies.append(pltpu.make_async_copy(out_ref.at[:, cols], out_hbm.at[:, cols], sems.at[i]))
        copies[-1].start()
    for copy in copies:
        copy.wait()


def per_device(
    tokens, routing_gate_weight, selected_expert_index, w_gate, w_up, w_down, s_gate, s_up, s_down
):
    nodes = lax.axis_size("node")
    count, width = tokens.shape
    capacity = count // 16
    block = 2 * capacity
    slots = nodes * block
    head = min(nodes * capacity, count)
    tail = count - head

    owners = jnp.arange(nodes, dtype=jnp.int32)
    if nodes <= FEW_NODES:
        owners = owners ^ lax.axis_index("node")
    topk = selected_expert_index.shape[1]
    first, mix, pick, held = call(
        lambda *refs: head_kernel(nodes, block, *refs),
        (
            struct(head, width + 2 * slots),
            struct(count + 2 * slots, count),
            struct(slots, count),
            struct(count, width),
        ),
        (owners * EXPERTS_PER_NODE, selected_expert_index.T, routing_gate_weight.T, tokens),
        specs=[SMEM, HBM, HBM, HBM],
        scratch=[
            pltpu.VMEM((topk, count), jnp.int32),
            pltpu.VMEM((topk, count), jnp.float32),
            pltpu.SemaphoreType.DMA((3,)),
        ],
        room=4 * slots * width,
    )
    far_first = shift(first, "local", 2)
    near, *rest = call(
        lambda *refs: tail_kernel(head, *refs),
        [struct(slots, width)] + [struct(tail, width)] * (tail > 0),
        (mix, pick, held),
        room=4 * (slots + count) * width,
    )
    far = [far_first] + [shift(r, "local", 2) for r in rest]
    shared_mats = (s_gate, s_up, s_down)
    shared_far = [shift(w, "local", 1) for w in shared_mats]
    routed_mats = (w_gate[0], w_up[0], w_down[0])
    routed_far = [shift(w, "local", 1) for w in routed_mats]

    own, *mats = call(
        own_kernel,
        [
            struct(count, width, jnp.float32),
            *[struct(*w.shape) for w in shared_mats],
            *[struct(*w.shape) for w in routed_mats],
        ],
        (held, *shared_far, *shared_mats, *routed_mats),
        specs=[VMEM] * 4 + [HBM] * 6,
        scratch=[pltpu.SemaphoreType.DMA((6,))],
        room=12 * count * width,
        flops=30 * count * width * s_gate.shape[1],
    )
    sent = call(
        lambda *refs: join_kernel(block, *refs),
        [struct(block, width)] * nodes,
        (near, far_first),
        room=8 * slots * width,
    )
    arrived = over_nodes(sent)
    replied = call(
        lambda *refs: expert_kernel(nodes, *refs),
        [struct(block, width)] * nodes,
        (*arrived, *routed_far, *mats[3:]),
        room=12 * slots * width,
        flops=40 * slots * width * w_gate.shape[2],
    )
    replies = over_nodes(replied)
    part, *sums = call(
        lambda *refs: far_kernel(len(far), *refs),
        [struct(head, width, jnp.float32)] + [struct(tail, width)] * len(rest),
        (*far, *shared_far, *mats[:3]),
        room=12 * count * width,
        flops=24 * count * width * s_gate.shape[1],
    )
    late = [shift(r, "local", 2) for r in sums]
    folded = call(
        fold_kernel,
        struct(head, width),
        (part, far_first, *replies),
        room=8 * slots * width,
    )
    backs = [shift(folded, "local", 2)] + late
    return pl.pallas_call(
        lambda *refs: final_kernel(len(backs), *refs),
        out_shape=struct(count, width),
        in_specs=[VMEM] * (2 + len(backs) + nodes),
        out_specs=HBM,
        scratch_shapes=[
            pltpu.VMEM((count, width), jnp.bfloat16),
            pltpu.SemaphoreType.DMA((PIECES,)),
        ],
        compiler_params=pltpu.CompilerParams(vmem_limit_bytes=(8 << 20) + 8 * slots * width),
    )(own, mix, *backs, *replies)


def solution(mesh):
    in_specs = (
        P(("groups", "node", "local"), None),
        P(("groups", "node", "local"), None),
        P(("groups", "node", "local"), None),
        P("node", None, "local"),
        P("node", None, "local"),
        P("node", "local", None),
        P(None, "local"),
        P(None, "local"),
        P("local", None),
    )
    out_specs = P(("groups", "node", "local"), None)
    return jax.shard_map(
        per_device, mesh=mesh, in_specs=in_specs, out_specs=out_specs, check_vma=False
    )
```

time: 132 us -> 68.4 us (0.52)
  blocking collectives: 29.7 us -> 0 us
  other arithmetic: 17.7 us -> 0.01 us
  starting transfers between devices: 4.68 us -> 21.2 us
  matrix products: 15.9 us -> 0 us
  Pallas kernels: 0 us -> 14.4 us
  between operations: 13.2 us -> 0.1 us
  local copies, waits for them, and re-layouts: 19.6 us -> 10.2 us
  waiting for transfers between devices: 30.7 us -> 22.3 us
    all_to_all x1 -> x0, blocking collectives: 29.7 us -> none  [per_device(): lax.all_to_all(spread, ('node', 'local'), split_axis=0, concat_axis=0, ti...]
    ppermute x0 -> x16, waiting for transfers between devices: none -> 22.3 us  [shift(): return lax.ppermute(value, axis, [(i, i ^ mask) for i in range(size)])]
    ppermute x0 -> x16, starting transfers between devices: none -> 21.2 us  [shift(): return lax.ppermute(value, axis, [(i, i ^ mask) for i in range(size)])]
    gather x4 -> x0, local copies, waits for them, and re-layouts: 16.2 us -> none  [the longest x3 8.85 us: per_device(): destination_slot = jnp.take_along_axis(position, destination_node, axis=1)]
    dot_general x6 -> x0, matrix products: 15.9 us -> none  [the longest x1 8.47 us: expert_part(): return jnp.dot(hidden, proj_down, preferred_element_type=jnp.float32)]
    reduce_scatter x2 -> x0, waiting for transfers between devices: 14.6 us -> none  [the longest x1 10.2 us: per_device(): lax.psum_scatter(shared_terms.astype(jnp.bfloat16), 'local', scatter_dime...]
    pallas_call x0 -> x8, Pallas kernels: none -> 14.4 us  [the longest x7 13.1 us: call(): pl.pallas_call(kernel, out_shape=outs, in_specs=specs or [VMEM] * len(arg...]
    reduce_sum x1 -> x0, other arithmetic: 13.7 us -> none  [per_device(): jnp.sum(capacity_factor[:, :, None] * fetched.astype(jnp.float32), axis=1)]
  transfers between devices with their start and end apart: 4 -> 16, of which waited for: 4 -> 6; matrix products, arithmetic and copies ran while one was open for 36% -> 0% of each run, Pallas kernels for 0% -> 19%
where the time goes in v2:
time: 68.4 us; the launch traced here: 68.1 us
  waiting for transfers between devices  22.3 us (33%)
  starting transfers between devices  21.2 us (31%)
  Pallas kernels  14.4 us (21%)
  local copies, waits for them, and re-layouts  10.2 us (15%)
    ppermute x16, waiting for transfers between devices, shift(): return lax.ppermute(value, axis, [(i, i ^ mask) for i in range(size)])  22.3 us
    ppermute x16, starting transfers between devices, shift(): return lax.ppermute(value, axis, [(i, i ^ mask) for i in range(size)])  21.2 us
    pallas_call x7, Pallas kernels, call(): pl.pallas_call(kernel, out_shape=outs, in_specs=specs or [VMEM] * len(arg...  13.1 us
    unnamed x18, local copies, waits for them, and re-layouts  10.2 us
  transfers between devices with their start and end apart: 16, of which 6 were waited for; matrix products, arithmetic and copies ran while one was open for 0% of the time, Pallas kernels for 19%

profile of v2, /device:TPU:0, one launch (start us, length us, event | category | flops | bytes accessed | tf_op | source)
XLA Modules:
  0.0 68.1 jit_solution(2975170469376343719)
XLA Ops:
  0.0 0.5 collective-permute-start
  0.5 0.1 collective-permute-start.1
  0.5 0.5 collective-permute-start.2
  1.0 1.3 %copy-done.6 = bf16[128,3584]{1,0:T(8,128)(2,1)S(1)} copy-done((bf16[128,3584]{1,0:T(8,128)(2,1)S(1)}, bf16[128,3584]{1,0:T(8,128)(2,1)}, u32[]{:S(2)}) %copy-start.6) | copy-done | bytes 917528
  2.3 0.7 %copy-done.7 = s32[128,8]{0,1:T(8,128)S(1)} copy-done((s32[128,8]{0,1:T(8,128)S(1)}, s32[128,8]{0,1:T(8,128)}, u32[]{:S(2)}) %copy-start.7) | copy-done | bytes 4120
  3.0 0.7 %copy-done.8 = f32[128,8]{0,1:T(8,128)S(1)} copy-done((f32[128,8]{0,1:T(8,128)S(1)}, f32[128,8]{0,1:T(8,128)}, u32[]{:S(2)}) %copy-start.8) | copy-done | bytes 4120
  3.7 1.4 %shard_map.91 = (bf16[32,3712]{1,0:T(8,128)(2,1)S(1)}, bf16[256,128]{1,0:T(8,128)(2,1)S(1)}, bf16[64,128]{1,0:T(8,128)(2,1)S(1)}, bf16[128,3584]{1,0:T(8,128)(2,1)S(1)}) custom-call(s32[4]{0:T(128)S(1)} %xor_multiply_fusion.refs_0_, s32[8,128]{1,0:T(8,128)S(1)} %bitcast.11, f32[8,128]{1,0:T(8,128)S(1)} %bitcast.12, bf16[128,3584]{1,0:T(8,128)(2,1)S(1)} %copy-done.6), custom_call_target="tpu_custom_call" | custom-call | tf_op jit(solution)/shard_map/pallas_call | solution.py:44
  5.1 2.6 %collective-permute-start.3 = (bf16[32,3712]{1,0:T(8,128)(2,1)S(1)}, bf16[32,3712]{1,0:T(8,128)(2,1)S(1)}, u32[]{:S(2)}, u32[]{:S(2)}) collective-permute-start(bf16[32,3712]{1,0:T(8,128)(2,1)S(1)} %get-tuple-element.31), channel_id=1, source_target_pairs={{0,2},{1,3},{2,0},{3,1},{4,6},{5,7},{6,4},{7,5},{8,10},{9,11},{10,... | collective-permute-start | bytes 712712 | tf_op jit(solution)/shard_map/ppermute | solution.py:20
  7.7 0.2 collective-permute-start.8
  7.9 6.2 %collective-permute-done.3.refs_0_.refs_1_.first_ref = bf16[32,3712]{1,0:T(8,128)(2,1)S(1)} collective-permute-done((bf16[32,3712]{1,0:T(8,128)(2,1)S(1)}, bf16[32,3712]{1,0:T(8,128)(2,1)S(1)}, u32[]{:S(2)}, u32[]{:S(2)}) %collective-permute-start.3) | collective-permute-done | bytes 237600 | tf_op jit(solution)/shard_map/ppermute | solution.py:20
  14.1 0.0 collective-permute-start.9
  14.1 0.0 collective-permute-done.gate.refs_2_
  14.1 0.5 collective-permute-start.10
  14.6 0.4 shard_map.93
  15.1 0.0 collective-permute-done.1.up.refs_3_
  15.1 1.8 %collective-permute-start.4 = (bf16[96,3584]{1,0:T(8,128)(2,1)S(1)}, bf16[96,3584]{1,0:T(8,128)(2,1)S(1)}, u32[]{:S(2)}, u32[]{:S(2)}) collective-permute-start(bf16[96,3584]{1,0:T(8,128)(2,1)S(1)} %get-tuple-element.33), channel_id=1, source_target_pairs={{0,2},{1,3},{2,0},{3,1},{4,6},{5,7},{6,4},{7,5},{8,10},{9,11},{10,... | collective-permute-start | bytes 2064392 | tf_op jit(solution)/shard_map/ppermute | solution.py:20
  16.9 0.3 shard_map.95
  17.2 0.0 collective-permute-done.2.down.refs_4_
  17.2 1.6 %collective-permute-start.5 = (bf16[16,3584]{1,0:T(8,128)(2,1)S(1)}, bf16[16,3584]{1,0:T(8,128)(2,1)S(1)}, u32[]{:S(2)}, u32[]{:S(2)}) collective-permute-start(bf16[16,3584]{1,0:T(8,128)(2,1)S(1)} %get-tuple-element.40), channel_id=1, source_target_pairs={{0,4},{4,0},{8,12},{12,8},{1,5},{5,1},{9,13},{13,9},{2,6},{6,2},{1... | collective-permute-start | bytes 344072 | tf_op jit(solution)/shard_map/ppermute | solution.py:20
  18.9 1.5 %copy-done.1 = bf16[3584,256]{1,0:T(8,128)(2,1)S(1)} copy-done((bf16[3584,256]{1,0:T(8,128)(2,1)S(1)}, bf16[3584,256]{1,0:T(8,128)(2,1)}, u32[]{:S(2)}) %copy-start.1) | copy-done | bytes 1835032
  20.4 1.5 %copy-done.2 = bf16[256,3584]{1,0:T(8,128)(2,1)S(1)} copy-done((bf16[256,3584]{1,0:T(8,128)(2,1)S(1)}, bf16[256,3584]{1,0:T(8,128)(2,1)}, u32[]{:S(2)}) %copy-start.2) | copy-done | bytes 1835032
  21.9 1.5 %copy-done.3 = bf16[1,3584,256]{2,1,0:T(8,128)(2,1)S(1)} copy-done((bf16[1,3584,256]{2,1,0:T(8,128)(2,1)S(1)}, bf16[1,3584,256]{2,1,0:T(8,128)(2,1)}, u32[]{:S(2)}) %copy-start.3) | copy-done | bytes 1835032
  23.4 1.5 %copy-done.4 = bf16[1,3584,256]{2,1,0:T(8,128)(2,1)S(1)} copy-done((bf16[1,3584,256]{2,1,0:T(8,128)(2,1)S(1)}, bf16[1,3584,256]{2,1,0:T(8,128)(2,1)}, u32[]{:S(2)}) %copy-start.4) | copy-done | bytes 1835032
  24.9 1.5 %copy-done.5 = bf16[1,256,3584]{2,1,0:T(8,128)(2,1)S(1)} copy-done((bf16[1,256,3584]{2,1,0:T(8,128)(2,1)S(1)}, bf16[1,256,3584]{2,1,0:T(8,128)(2,1)}, u32[]{:S(2)}) %copy-start.5) | copy-done | bytes 1835032
  26.4 4.8 %shard_map.92 = (f32[128,3584]{1,0:T(8,128)S(1)}, bf16[3584,256]{1,0:T(8,128)(2,1)S(1)}, bf16[3584,256]{1,0:T(8,128)(2,1)S(1)}, bf16[256,3584]{1,0:T(8,128)(2,1)...) custom-call(bf16[128,3584]{1,0:T(8,128)(2,1)S(1)} %get-tuple-element.28.tokens_ref, ...), custom_call_target="tpu_custom_call" | custom-call | flops 3523215360 | tf_op jit(solution)/shard_map/pallas_call | solution.py:44
  31.1 1.3 %collective-permute-done.4.refs_1_ = bf16[96,3584]{1,0:T(8,128)(2,1)S(1)} collective-permute-done((bf16[96,3584]{1,0:T(8,128)(2,1)S(1)}, bf16[96,3584]{1,0:T(8,128)(2,1)S(1)}, u32[]{:S(2)}, u32[]{:S(2)}) %collective-permute-start.4) | collective-permute-done | bytes 688160 | tf_op jit(solution)/shard_map/ppermute | solution.py:20
  32.5 2.8 %collective-permute-start.6 = (bf16[16,3584]{1,0:T(8,128)(2,1)S(1)}, bf16[16,3584]{1,0:T(8,128)(2,1)S(1)}, u32[]{:S(2)}, u32[]{:S(2)}) collective-permute-start(bf16[16,3584]{1,0:T(8,128)(2,1)S(1)} %get-tuple-element.41), channel_id=1, source_target_pairs={{0,8},{4,12},{8,0},{12,4},{1,9},{5,13},{9,1},{13,5},{2,10},{6,14},... | collective-permute-start | bytes 344072 | tf_op jit(solution)/shard_map/ppermute | solution.py:20
  35.3 3.8 %shard_map.94 = (f32[32,3584]{1,0:T(8,128)S(1)}, bf16[96,3584]{1,0:T(8,128)(2,1)S(1)}) custom-call(bf16[32,3712]{1,0:T(8,128)(2,1)S(1)} %collective-permute-done.3.refs_0_.refs_1_.first_ref, bf16[96,3584]{1,0:T(8,128)(2,1)S(1)} %collective-permute-done.4.refs_1_, bf16[3584,256]{1,0:T(8,128)(2,1)S(1)} %collective-permute-done.gate.refs_2_, ...), custom_call_target="tpu_custom_call" | custom-call | flops 2818572288 | tf_op jit(solution)/shard_map/pallas_call | solution.py:44
  39.1 0.0 collective-permute-done.5.refs_1_
  39.1 1.6 %collective-permute-start.15 = (bf16[96,3584]{1,0:T(8,128)(2,1)S(1)}, bf16[96,3584]{1,0:T(8,128)(2,1)S(1)}, u32[]{:S(2)}, u32[]{:S(2)}) collective-permute-start(bf16[96,3584]{1,0:T(8,128)(2,1)S(1)} %get-tuple-element.50), channel_id=1, source_target_pairs={{0,2},{1,3},{2,0},{3,1},{4,6},{5,7},{6,4},{7,5},{8,10},{9,11},{10,... | collective-permute-start | bytes 2064392 | tf_op jit(solution)/shard_map/ppermute | solution.py:20
  40.7 0.0 collective-permute-done.6.refs_2_
  40.7 3.1 %collective-permute-start.7 = (bf16[16,3584]{1,0:T(8,128)(2,1)S(1)}, bf16[16,3584]{1,0:T(8,128)(2,1)S(1)}, u32[]{:S(2)}, u32[]{:S(2)}) collective-permute-start(bf16[16,3584]{1,0:T(8,128)(2,1)S(1)} %get-tuple-element.42), channel_id=1, source_target_pairs={{0,12},{4,8},{8,4},{12,0},{1,13},{5,9},{9,5},{13,1},{2,14},{6,10},... | collective-permute-start | bytes 344072 | tf_op jit(solution)/shard_map/ppermute | solution.py:20
  43.8 3.6 %collective-permute-done.7.refs_3_ = bf16[16,3584]{1,0:T(8,128)(2,1)S(1)} collective-permute-done((bf16[16,3584]{1,0:T(8,128)(2,1)S(1)}, bf16[16,3584]{1,0:T(8,128)(2,1)S(1)}, u32[]{:S(2)}, u32[]{:S(2)}) %collective-permute-start.7) | collective-permute-done | bytes 114720 | tf_op jit(solution)/shard_map/ppermute | solution.py:20
  47.4 0.0 collective-permute-done.8.refs_4_
  47.4 0.0 collective-permute-done.9.refs_5_
  47.4 0.0 collective-permute-done.10.refs_6_
  47.4 2.1 %shard_map.96 = (bf16[16,3584]{1,0:T(8,128)(2,1)S(1)}, bf16[16,3584]{1,0:T(8,128)(2,1)S(1)}, bf16[16,3584]{1,0:T(8,128)(2,1)S(1)}, bf16[16,3584]{1,0:T(8,128)(2,1)S(1)}) custom-call(bf16[16,3584]{1,0:T(8,128)(2,1)S(1)} %get-tuple-element.39.refs_0_, bf16[16,3584]{1,0:T(8,128)(2,1)S(1)} %collective-permute-done.5.refs_1_, ...), custom_call_target="tpu_custom_call" | custom-call | flops 2348810240 | tf_op jit(solution)/shard_map/pallas_call | solution.py:44
  49.5 1.1 %collective-permute-start.11 = (bf16[16,3584]{1,0:T(8,128)(2,1)S(1)}, bf16[16,3584]{1,0:T(8,128)(2,1)S(1)}, u32[]{:S(2)}, u32[]{:S(2)}) collective-permute-start(bf16[16,3584]{1,0:T(8,128)(2,1)S(1)} %get-tuple-element.47), channel_id=1, source_target_pairs={{0,4},{4,0},{8,12},{12,8},{1,5},{5,1},{9,13},{13,9},{2,6},{6,2},{1... | collective-permute-start | bytes 344072 | tf_op jit(solution)/shard_map/ppermute | solution.py:20
  50.6 2.6 %collective-permute-start.12 = (bf16[16,3584]{1,0:T(8,128)(2,1)S(1)}, bf16[16,3584]{1,0:T(8,128)(2,1)S(1)}, u32[]{:S(2)}, u32[]{:S(2)}) collective-permute-start(bf16[16,3584]{1,0:T(8,128)(2,1)S(1)} %get-tuple-element.48), channel_id=1, source_target_pairs={{0,8},{4,12},{8,0},{12,4},{1,9},{5,13},{9,1},{13,5},{2,10},{6,14},... | collective-permute-start | bytes 344072 | tf_op jit(solution)/shard_map/ppermute | solution.py:20
  53.1 0.8 %collective-permute-start.13 = (bf16[16,3584]{1,0:T(8,128)(2,1)S(1)}, bf16[16,3584]{1,0:T(8,128)(2,1)S(1)}, u32[]{:S(2)}, u32[]{:S(2)}) collective-permute-start(bf16[16,3584]{1,0:T(8,128)(2,1)S(1)} %get-tuple-element.49), channel_id=1, source_target_pairs={{0,12},{4,8},{8,4},{12,0},{1,13},{5,9},{9,5},{13,1},{2,14},{6,10},... | collective-permute-start | bytes 344072 | tf_op jit(solution)/shard_map/ppermute | solution.py:20
  54.0 0.6 collective-permute-done.11.refs_1_.refs_5_
  54.6 6.0 %collective-permute-done.12.refs_2_.refs_6_ = bf16[16,3584]{1,0:T(8,128)(2,1)S(1)} collective-permute-done((bf16[16,3584]{1,0:T(8,128)(2,1)S(1)}, bf16[16,3584]{1,0:T(8,128)(2,1)S(1)}, u32[]{:S(2)}, u32[]{:S(2)}) %collective-permute-start.12) | collective-permute-done | bytes 114720 | tf_op jit(solution)/shard_map/ppermute | solution.py:20
  60.5 0.0 collective-permute-done.13.refs_3_.refs_7_
  60.5 0.3 shard_map.97
  60.8 1.6 %collective-permute-start.14 = (bf16[32,3584]{1,0:T(8,128)(2,1)S(1)}, bf16[32,3584]{1,0:T(8,128)(2,1)S(1)}, u32[]{:S(2)}, u32[]{:S(2)}) collective-permute-start(bf16[32,3584]{1,0:T(8,128)(2,1)S(1)} %shard_map.97), channel_id=1, source_target_pairs={{0,2},{1,3},{2,0},{3,1},{4,6},{5,7},{6,4},{7,5},{8,10},{9,11},{10,... | collective-permute-start | bytes 688136 | tf_op jit(solution)/shard_map/ppermute | solution.py:20
  62.4 4.5 %collective-permute-done.14.refs_2_ = bf16[32,3584]{1,0:T(8,128)(2,1)S(1)} collective-permute-done((bf16[32,3584]{1,0:T(8,128)(2,1)S(1)}, bf16[32,3584]{1,0:T(8,128)(2,1)S(1)}, u32[]{:S(2)}, u32[]{:S(2)}) %collective-permute-start.14) | collective-permute-done | bytes 229408 | tf_op jit(solution)/shard_map/ppermute | solution.py:20
  66.9 0.0 collective-permute-done.15.refs_3_
  66.9 1.2 %shard_map.98 = bf16[128,3584]{1,0:T(8,128)(2,1)} custom-call(f32[128,3584]{1,0:T(8,128)S(1)} %get-tuple-element.29.refs_0_, bf16[256,128]{1,0:T(8,128)(2,1)S(1)} %get-tuple-element.30.refs_0_.refs_1_, bf16[32,3584]{1,0:T(8,128)(2,1)S(1)} %collective-permute-done.14.refs_2_, bf16[96,3584]{1,0:T(8,128)(2,1)S(1)} %collective-permute-done.15.refs_3_, ...), custom_call_target="tpu_custom_call" | custom-call | tf_op jit(solution)/shard_map/pallas_call | solution.py:287
  (11 shorter events, 0.0 us)
Async XLA Ops:
  0.0 14.1 %collective-permute-start = (bf16[3584,256]{1,0:T(8,128)(2,1)}, bf16[3584,256]{1,0:T(8,128)(2,1)S(1)}, u32[]{:S(2)}, u32[]{:S(2)}) collective-permute-start(bf16[3584,256]{1,0:T(8,128)(2,1)} %sg_hbm.1), channel_id=1, source_target_pairs={{0,1},{1,0},{2,3},{3,2},{4,5},{5,4},{6,7},{7,6},{8,9},{9,8},{10,11... | collective-permute-start | bytes 5505032 | tf_op jit(solution)/shard_map/ppermute | solution.py:20
  0.5 14.6 %collective-permute-start.1 = (bf16[3584,256]{1,0:T(8,128)(2,1)}, bf16[3584,256]{1,0:T(8,128)(2,1)}, u32[]{:S(2)}, u32[]{:S(2)}) collective-permute-start(bf16[3584,256]{1,0:T(8,128)(2,1)} %su_hbm.1), channel_id=1, source_target_pairs={{0,1},{1,0},{2,3},{3,2},{4,5},{5,4},{6,7},{7,6},{8,9},{9,8},{10,11... | collective-permute-start | bytes 5505032 | tf_op jit(solution)/shard_map/ppermute | solution.py:20
  0.5 16.7 %collective-permute-start.2 = (bf16[256,3584]{1,0:T(8,128)(2,1)}, bf16[256,3584]{1,0:T(8,128)(2,1)}, u32[]{:S(2)}, u32[]{:S(2)}) collective-permute-start(bf16[256,3584]{1,0:T(8,128)(2,1)} %sd_hbm.1), channel_id=1, source_target_pairs={{0,1},{1,0},{2,3},{3,2},{4,5},{5,4},{6,7},{7,6},{8,9},{9,8},{10,11... | collective-permute-start | bytes 5505032 | tf_op jit(solution)/shard_map/ppermute | solution.py:20
  1.0 17.9 %copy-start = (bf16[3584,256]{1,0:T(8,128)(2,1)S(1)}, bf16[3584,256]{1,0:T(8,128)(2,1)}, u32[]{:S(2)}) copy-start(bf16[3584,256]{1,0:T(8,128)(2,1)} %sg_hbm.1) | copy-start | bytes 5505028
  1.0 1.3 %copy-start.6 = (bf16[128,3584]{1,0:T(8,128)(2,1)S(1)}, bf16[128,3584]{1,0:T(8,128)(2,1)}, u32[]{:S(2)}) copy-start(bf16[128,3584]{1,0:T(8,128)(2,1)} %refs_3_.1) | copy-start | bytes 2752516
  2.3 0.7 %copy-start.7 = (s32[128,8]{0,1:T(8,128)S(1)}, s32[128,8]{0,1:T(8,128)}, u32[]{:S(2)}) copy-start(s32[128,8]{0,1:T(8,128)} %param.11) | copy-start | bytes 12292
  3.0 0.7 %copy-start.8 = (f32[128,8]{0,1:T(8,128)S(1)}, f32[128,8]{0,1:T(8,128)}, u32[]{:S(2)}) copy-start(f32[128,8]{0,1:T(8,128)} %param.10) | copy-start | bytes 12292
  5.1 9.0 %collective-permute-start.3 = (bf16[32,3712]{1,0:T(8,128)(2,1)S(1)}, bf16[32,3712]{1,0:T(8,128)(2,1)S(1)}, u32[]{:S(2)}, u32[]{:S(2)}) collective-permute-start(bf16[32,3712]{1,0:T(8,128)(2,1)S(1)} %get-tuple-element.31), channel_id=1, source_target_pairs={{0,2},{1,3},{2,0},{3,1},{4,6},{5,7},{6,4},{7,5},{8,10},{9,11},{10,... | collective-permute-start | bytes 712712 | tf_op jit(solution)/shard_map/ppermute | solution.py:20
  7.7 39.7 %collective-permute-start.8 = (bf16[3584,256]{1,0:T(8,128)(2,1)}, bf16[3584,256]{1,0:T(8,128)(2,1)S(1)}, u32[]{:S(2)}, u32[]{:S(2)}) collective-permute-start(bf16[3584,256]{1,0:T(8,128)(2,1)} %bitcast.5), channel_id=1, source_target_pairs={{0,1},{1,0},{2,3},{3,2},{4,5},{5,4},{6,7},{7,6},{8,9},{9,8},{10,11... | collective-permute-start | bytes 5505032 | tf_op jit(solution)/shard_map/ppermute | solution.py:20
  14.1 33.3 %collective-permute-start.9 = (bf16[3584,256]{1,0:T(8,128)(2,1)}, bf16[3584,256]{1,0:T(8,128)(2,1)S(1)}, u32[]{:S(2)}, u32[]{:S(2)}) collective-permute-start(bf16[3584,256]{1,0:T(8,128)(2,1)} %bitcast.7), channel_id=1, source_target_pairs={{0,1},{1,0},{2,3},{3,2},{4,5},{5,4},{6,7},{7,6},{8,9},{9,8},{10,11... | collective-permute-start | bytes 5505032 | tf_op jit(solution)/shard_map/ppermute | solution.py:20
  14.1 33.3 %collective-permute-start.10 = (bf16[256,3584]{1,0:T(8,128)(2,1)}, bf16[256,3584]{1,0:T(8,128)(2,1)S(1)}, u32[]{:S(2)}, u32[]{:S(2)}) collective-permute-start(bf16[256,3584]{1,0:T(8,128)(2,1)} %bitcast.9), channel_id=1, source_target_pairs={{0,1},{1,0},{2,3},{3,2},{4,5},{5,4},{6,7},{7,6},{8,9},{9,8},{10,11... | collective-permute-start | bytes 5505032 | tf_op jit(solution)/shard_map/ppermute | solution.py:20
  15.1 17.4 %collective-permute-start.4 = (bf16[96,3584]{1,0:T(8,128)(2,1)S(1)}, bf16[96,3584]{1,0:T(8,128)(2,1)S(1)}, u32[]{:S(2)}, u32[]{:S(2)}) collective-permute-start(bf16[96,3584]{1,0:T(8,128)(2,1)S(1)} %get-tuple-element.33), channel_id=1, source_target_pairs={{0,2},{1,3},{2,0},{3,1},{4,6},{5,7},{6,4},{7,5},{8,10},{9,11},{10,... | collective-permute-start | bytes 2064392 | tf_op jit(solution)/shard_map/ppermute | solution.py:20
  17.2 21.9 %collective-permute-start.5 = (bf16[16,3584]{1,0:T(8,128)(2,1)S(1)}, bf16[16,3584]{1,0:T(8,128)(2,1)S(1)}, u32[]{:S(2)}, u32[]{:S(2)}) collective-permute-start(bf16[16,3584]{1,0:T(8,128)(2,1)S(1)} %get-tuple-element.40), channel_id=1, source_target_pairs={{0,4},{4,0},{8,12},{12,8},{1,5},{5,1},{9,13},{13,9},{2,6},{6,2},{1... | collective-permute-start | bytes 344072 | tf_op jit(solution)/shard_map/ppermute | solution.py:20
  18.9 1.5 %copy-start.1 = (bf16[3584,256]{1,0:T(8,128)(2,1)S(1)}, bf16[3584,256]{1,0:T(8,128)(2,1)}, u32[]{:S(2)}) copy-start(bf16[3584,256]{1,0:T(8,128)(2,1)} %su_hbm.1) | copy-start | bytes 5505028
  20.4 1.5 %copy-start.2 = (bf16[256,3584]{1,0:T(8,128)(2,1)S(1)}, bf16[256,3584]{1,0:T(8,128)(2,1)}, u32[]{:S(2)}) copy-start(bf16[256,3584]{1,0:T(8,128)(2,1)} %sd_hbm.1) | copy-start | bytes 5505028
  21.9 1.5 %copy-start.3 = (bf16[1,3584,256]{2,1,0:T(8,128)(2,1)S(1)}, bf16[1,3584,256]{2,1,0:T(8,128)(2,1)}, u32[]{:S(2)}) copy-start(bf16[1,3584,256]{2,1,0:T(8,128)(2,1)} %param.12) | copy-start | bytes 5505028
  23.4 1.5 %copy-start.4 = (bf16[1,3584,256]{2,1,0:T(8,128)(2,1)S(1)}, bf16[1,3584,256]{2,1,0:T(8,128)(2,1)}, u32[]{:S(2)}) copy-start(bf16[1,3584,256]{2,1,0:T(8,128)(2,1)} %param.13) | copy-start | bytes 5505028
  24.9 1.5 %copy-start.5 = (bf16[1,256,3584]{2,1,0:T(8,128)(2,1)S(1)}, bf16[1,256,3584]{2,1,0:T(8,128)(2,1)}, u32[]{:S(2)}) copy-start(bf16[1,256,3584]{2,1,0:T(8,128)(2,1)} %param.14) | copy-start | bytes 5505028
  32.5 8.2 %collective-permute-start.6 = (bf16[16,3584]{1,0:T(8,128)(2,1)S(1)}, bf16[16,3584]{1,0:T(8,128)(2,1)S(1)}, u32[]{:S(2)}, u32[]{:S(2)}) collective-permute-start(bf16[16,3584]{1,0:T(8,128)(2,1)S(1)} %get-tuple-element.41), channel_id=1, source_target_pairs={{0,8},{4,12},{8,0},{12,4},{1,9},{5,13},{9,1},{13,5},{2,10},{6,14},... | collective-permute-start | bytes 344072 | tf_op jit(solution)/shard_map/ppermute | solution.py:20
  39.1 27.7 %collective-permute-start.15 = (bf16[96,3584]{1,0:T(8,128)(2,1)S(1)}, bf16[96,3584]{1,0:T(8,128)(2,1)S(1)}, u32[]{:S(2)}, u32[]{:S(2)}) collective-permute-start(bf16[96,3584]{1,0:T(8,128)(2,1)S(1)} %get-tuple-element.50), channel_id=1, source_target_pairs={{0,2},{1,3},{2,0},{3,1},{4,6},{5,7},{6,4},{7,5},{8,10},{9,11},{10,... | collective-permute-start | bytes 2064392 | tf_op jit(solution)/shard_map/ppermute | solution.py:20
  40.7 6.7 %collective-permute-start.7 = (bf16[16,3584]{1,0:T(8,128)(2,1)S(1)}, bf16[16,3584]{1,0:T(8,128)(2,1)S(1)}, u32[]{:S(2)}, u32[]{:S(2)}) collective-permute-start(bf16[16,3584]{1,0:T(8,128)(2,1)S(1)} %get-tuple-element.42), channel_id=1, source_target_pairs={{0,12},{4,8},{8,4},{12,0},{1,13},{5,9},{9,5},{13,1},{2,14},{6,10},... | collective-permute-start | bytes 344072 | tf_op jit(solution)/shard_map/ppermute | solution.py:20
  49.5 5.0 %collective-permute-start.11 = (bf16[16,3584]{1,0:T(8,128)(2,1)S(1)}, bf16[16,3584]{1,0:T(8,128)(2,1)S(1)}, u32[]{:S(2)}, u32[]{:S(2)}) collective-permute-start(bf16[16,3584]{1,0:T(8,128)(2,1)S(1)} %get-tuple-element.47), channel_id=1, source_target_pairs={{0,4},{4,0},{8,12},{12,8},{1,5},{5,1},{9,13},{13,9},{2,6},{6,2},{1... | collective-permute-start | bytes 344072 | tf_op jit(solution)/shard_map/ppermute | solution.py:20
  50.6 9.9 %collective-permute-start.12 = (bf16[16,3584]{1,0:T(8,128)(2,1)S(1)}, bf16[16,3584]{1,0:T(8,128)(2,1)S(1)}, u32[]{:S(2)}, u32[]{:S(2)}) collective-permute-start(bf16[16,3584]{1,0:T(8,128)(2,1)S(1)} %get-tuple-element.48), channel_id=1, source_target_pairs={{0,8},{4,12},{8,0},{12,4},{1,9},{5,13},{9,1},{13,5},{2,10},{6,14},... | collective-permute-start | bytes 344072 | tf_op jit(solution)/shard_map/ppermute | solution.py:20
  53.1 7.4 %collective-permute-start.13 = (bf16[16,3584]{1,0:T(8,128)(2,1)S(1)}, bf16[16,3584]{1,0:T(8,128)(2,1)S(1)}, u32[]{:S(2)}, u32[]{:S(2)}) collective-permute-start(bf16[16,3584]{1,0:T(8,128)(2,1)S(1)} %get-tuple-element.49), channel_id=1, source_target_pairs={{0,12},{4,8},{8,4},{12,0},{1,13},{5,9},{9,5},{13,1},{2,14},{6,10},... | collective-permute-start | bytes 344072 | tf_op jit(solution)/shard_map/ppermute | solution.py:20
  60.8 6.1 %collective-permute-start.14 = (bf16[32,3584]{1,0:T(8,128)(2,1)S(1)}, bf16[32,3584]{1,0:T(8,128)(2,1)S(1)}, u32[]{:S(2)}, u32[]{:S(2)}) collective-permute-start(bf16[32,3584]{1,0:T(8,128)(2,1)S(1)} %shard_map.97), channel_id=1, source_target_pairs={{0,2},{1,3},{2,0},{3,1},{4,6},{5,7},{6,4},{7,5},{8,10},{9,11},{10,... | collective-permute-start | bytes 688136 | tf_op jit(solution)/shard_map/ppermute | solution.py:20

commit v3 on v2

--- a/solution.py
+++ b/solution.py
@@ -7,6 +7,7 @@
 
 EXPERTS_PER_NODE = 8
 FEW_NODES = 8
+COST = {"head": 3000000000, "tail": 100000000, "load": 100000000000, "join": 1000000000, "own": 3000000000, "expert": 100000000, "far": 100000000000, "fold": 3000000000, "final": 100000000000}
 PIECES = 4
 HBM = pl.BlockSpec(memory_space=pltpu.HBM)
 VMEM = pl.BlockSpec(memory_space=pltpu.VMEM)
@@ -40,15 +41,21 @@
     return jax.ShapeDtypeStruct((rows, cols), dtype)
 
 
-def call(kernel, outs, args, specs=None, scratch=(), room=0, flops=0):
+def call(name, kernel, outs, args, specs=None, scratch=(), room=0, limit=0):
+    if specs:
+        args = [
+            pltpu.with_memory_space_constraint(a, pltpu.HBM) if s is HBM else a
+            for a, s in zip(args, specs)
+        ]
     return pl.pallas_call(
         kernel,
+        name="scope_" + name,
         out_shape=outs,
         in_specs=specs or [VMEM] * len(args),
         out_specs=jax.tree.map(lambda _: VMEM, outs),
         scratch_shapes=scratch,
-        cost_estimate=pl.CostEstimate(flops=flops, bytes_accessed=0, transcendentals=0),
-        compiler_params=pltpu.CompilerParams(vmem_limit_bytes=(8 << 20) + room),
+        cost_estimate=pl.CostEstimate(flops=COST[name], bytes_accessed=0, transcendentals=0),
+        compiler_params=pltpu.CompilerParams(vmem_limit_bytes=limit or (8 << 20) + room),
     )(*args)
 
 
@@ -132,31 +139,51 @@
     return dot(hidden, down[...])
 
 
+def load_kernel(gate_hbm, up_hbm, down_hbm, near_ref, pack_ref, sems):
+    width, part = gate_hbm.shape
+    copies = [(gate_hbm, 0), (up_hbm, width)]
+    copies += [(down_hbm.at[:, i : i + part], 2 * width + i) for i in range(0, width, part)]
+    copies = [
+        pltpu.make_async_copy(
+            source, pack_ref.at[place : place + source.shape[0]], sems.at[i]
+        )
+        for i, (source, place) in enumerate(copies)
+    ]
+    for copy in copies:
+        copy.start()
+    for copy in copies:
+        copy.wait()
+
+
 def expert_kernel(nodes, *refs):
     rows = [r[...] for r in refs[:nodes]]
-    mats, outs = refs[nodes : nodes + 6], refs[nodes + 6 :]
-    block = rows[0].shape[0]
+    packs, outs = refs[nodes : nodes + 2], refs[nodes + 2 :]
+    block, width = rows[0].shape
+    part = packs[0].shape[1]
     rows = jnp.concatenate(rows, axis=0)
-    part = mlp(rows, *mats[:3]) + mlp(rows, *mats[3:])
-    for n, out in enumerate(outs):
-        out[...] = bf16(part[n * block : (n + 1) * block])
+    hidden = []
+    for pack in packs:
+        v = dot(rows, pack[:width])
+        hidden.append(bf16(v / (1.0 + jnp.exp(-v)) * dot(rows, pack[width : 2 * width])))
+    for i in range(0, width, part):
+        down = slice(2 * width + i, 2 * width + i + part)
+        sums = dot(hidden[0], packs[0][down]) + dot(hidden[1], packs[1][down])
+        for n, out in enumerate(outs):
+            out[:, i : i + part] = bf16(sums[n * block : (n + 1) * block])
 
 
 def own_kernel(
-    tokens_ref, gate, up, down, sg_hbm, su_hbm, sd_hbm, wg_hbm, wu_hbm, wd_hbm,
-    own_ref, sg, su, sd, wg, wu, wd, sems,
+    tokens_ref, gate, up, down, after_ref, sg_hbm, su_hbm, sd_hbm, own_ref, sg, su, sd, sems,
 ):
-    pairs = zip((sg_hbm, su_hbm, sd_hbm, wg_hbm, wu_hbm, wd_hbm), (sg, su, sd, wg, wu, wd))
+    pairs = zip((sg_hbm, su_hbm, sd_hbm), (sg, su, sd))
     copies = [pltpu.make_async_copy(a, b, sems.at[i]) for i, (a, b) in enumerate(pairs)]
     for copy in copies:
         copy.start()
     rows = tokens_ref[...]
     own_ref[...] = mlp(rows, gate, up, down)
-    for copy in copies[:3]:
+    for copy in copies:
         copy.wait()
     own_ref[...] += mlp(rows, sg, su, sd)
-    for copy in copies[3:]:
-        copy.wait()
 
 
 def far_kernel(groups, *refs):
@@ -212,6 +239,7 @@
         owners = owners ^ lax.axis_index("node")
     topk = selected_expert_index.shape[1]
     first, mix, pick, held = call(
+        "head",
         lambda *refs: head_kernel(nodes, block, *refs),
         (
             struct(head, width + 2 * slots),
@@ -226,10 +254,11 @@
             pltpu.VMEM((topk, count), jnp.float32),
             pltpu.SemaphoreType.DMA((3,)),
         ],
-        room=4 * slots * width,
+        limit=16 << 20,
     )
     far_first = shift(first, "local", 2)
     near, *rest = call(
+        "tail",
         lambda *refs: tail_kernel(head, *refs),
         [struct(slots, width)] + [struct(tail, width)] * (tail > 0),
         (mix, pick, held),
@@ -238,54 +267,64 @@
     far = [far_first] + [shift(r, "local", 2) for r in rest]
     shared_mats = (s_gate, s_up, s_down)
     shared_far = [shift(w, "local", 1) for w in shared_mats]
-    routed_mats = (w_gate[0], w_up[0], w_down[0])
-    routed_far = [shift(w, "local", 1) for w in routed_mats]
-
+    sent = call(
+        "join",
+        lambda *refs: join_kernel(block, *refs),
+        [struct(block, width)] * nodes,
+        (near, far_first),
+        room=8 * slots * width,
+    )
+    part = w_gate.shape[2]
+    pack = call(
+        "load",
+        load_kernel,
+        struct(3 * width, part),
+        (w_gate[0], w_up[0], w_down[0], sent[0]),
+        specs=[HBM] * 3 + [VMEM],
+        scratch=[pltpu.SemaphoreType.DMA((2 + width // part,))],
+        limit=16 << 20,
+    )
+    far_pack = shift(pack, "local", 1)
+    arrived = over_nodes(sent)
     own, *mats = call(
+        "own",
         own_kernel,
         [
             struct(count, width, jnp.float32),
             *[struct(*w.shape) for w in shared_mats],
-            *[struct(*w.shape) for w in routed_mats],
         ],
-        (held, *shared_far, *shared_mats, *routed_mats),
-        specs=[VMEM] * 4 + [HBM] * 6,
-        scratch=[pltpu.SemaphoreType.DMA((6,))],
-        room=12 * count * width,
-        flops=30 * count * width * s_gate.shape[1],
-    )
-    sent = call(
-        lambda *refs: join_kernel(block, *refs),
-        [struct(block, width)] * nodes,
-        (near, far_first),
-        room=8 * slots * width,
-    )
-    arrived = over_nodes(sent)
+        (held, *shared_far, near, *shared_mats),
+        specs=[VMEM] * 5 + [HBM] * 3,
+        scratch=[pltpu.SemaphoreType.DMA((3,))],
+        limit=16 << 20,
+    )
     replied = call(
+        "expert",
         lambda *refs: expert_kernel(nodes, *refs),
         [struct(block, width)] * nodes,
-        (*arrived, *routed_far, *mats[3:]),
-        room=12 * slots * width,
-        flops=40 * slots * width * w_gate.shape[2],
+        (*arrived, pack, far_pack),
+        room=20 * slots * width + (4 << 20),
     )
     replies = over_nodes(replied)
-    part, *sums = call(
+    sums_first, *sums = call(
+        "far",
         lambda *refs: far_kernel(len(far), *refs),
         [struct(head, width, jnp.float32)] + [struct(tail, width)] * len(rest),
-        (*far, *shared_far, *mats[:3]),
+        (*far, *shared_far, *mats),
         room=12 * count * width,
-        flops=24 * count * width * s_gate.shape[1],
     )
     late = [shift(r, "local", 2) for r in sums]
     folded = call(
+        "fold",
         fold_kernel,
         struct(head, width),
-        (part, far_first, *replies),
+        (sums_first, far_first, *replies),
         room=8 * slots * width,
     )
     backs = [shift(folded, "local", 2)] + late
     return pl.pallas_call(
         lambda *refs: final_kernel(len(backs), *refs),
+        name="scope_final",
         out_shape=struct(count, width),
         in_specs=[VMEM] * (2 + len(backs) + nodes),
         out_specs=HBM,
@@ -293,6 +332,7 @@
             pltpu.VMEM((count, width), jnp.bfloat16),
             pltpu.SemaphoreType.DMA((PIECES,)),
         ],
+        cost_estimate=pl.CostEstimate(flops=COST["final"], bytes_accessed=0, transcendentals=0),
         compiler_params=pltpu.CompilerParams(vmem_limit_bytes=(8 << 20) + 8 * slots * width),
     )(own, mix, *backs, *replies)
 

time: 68.4 us -> 53.8 us (0.79)
  local copies, waits for them, and re-layouts: 10.2 us -> 0.02 us
  starting transfers between devices: 21.2 us -> 16.3 us
  Pallas kernels: 14.4 us -> 16.3 us
  waiting for transfers between devices: 22.3 us -> 20.8 us
    unnamed x18 -> x10, local copies, waits for them, and re-layouts: 10.2 us -> 0.02 us
    ppermute x16 -> x14, starting transfers between devices: 21.2 us -> 16.3 us  [shift(): return lax.ppermute(value, axis, [(i, i ^ mask) for i in range(size)])]
    pallas_call x8 -> x9, Pallas kernels: 14.4 us -> 16.3 us  [the longest x8 15.1 us: call(): pl.pallas_call(kernel, name='scope_' + name, out_shape=outs, in_specs=spe...]
    ppermute x16 -> x14, waiting for transfers between devices: 22.3 us -> 20.8 us  [shift(): return lax.ppermute(value, axis, [(i, i ^ mask) for i in range(size)])]
  transfers between devices with their start and end apart: 16 -> 14, of which waited for: 6 -> 6; matrix products, arithmetic and copies ran while one was open for 0% -> 0% of each run, Pallas kernels for 19% -> 24%
where the time goes in v3:
time: 53.8 us; the launch traced here: 53.6 us
  waiting for transfers between devices  20.8 us (39%)
  Pallas kernels  16.3 us (30%)
  starting transfers between devices  16.3 us (30%)
    ppermute x14, waiting for transfers between devices, shift(): return lax.ppermute(value, axis, [(i, i ^ mask) for i in range(size)])  20.8 us
    ppermute x14, starting transfers between devices, shift(): return lax.ppermute(value, axis, [(i, i ^ mask) for i in range(size)])  16.3 us
    pallas_call x8, Pallas kernels, call(): pl.pallas_call(kernel, name='scope_' + name, out_shape=outs, in_specs=spe...  15.1 us
    pallas_call x1, Pallas kernels, per_device(): pl.pallas_call(lambda *refs: final_kernel(len(backs), *refs), name='scope...  1.22 us
  transfers between devices with their start and end apart: 14, of which 6 were waited for; matrix products, arithmetic and copies ran while one was open for 0% of the time, Pallas kernels for 24%

profile of v3, /device:TPU:0, one launch (start us, length us, event | category | flops | bytes accessed | tf_op | source)
XLA Modules:
  0.0 53.6 jit_solution(10802564534528348131)
XLA Ops:
  0.0 0.0 copy-start.2
  0.0 0.0 copy-start.3
  0.0 0.0 copy-start.4
  0.0 2.3 %scope_head.1 = (bf16[32,3712]{1,0:T(8,128)(2,1)S(1)}, bf16[256,128]{1,0:T(8,128)(2,1)S(1)}, bf16[64,128]{1,0:T(8,128)(2,1)S(1)}, bf16[128,3584]{1,0:T(8,128)(2,1)S(1)}) custom-call(s32[4]{0:T(128)S(1)} %xor_multiply_fusion.refs_0_, s32[8,128]{1,0:T(8,128)} %bitcast.8, f32[8,128]{1,0:T(8,128)} %bitcast.9, bf16[128,3584]{1,0:T(8,128)(2,1)} %refs_3_.1), custom_call_target="tpu_custom_call" | custom-call | flops 3000000000 | tf_op jit(solution)/shard_map/scope_head/pallas_call | solution.py:50
  2.3 0.0 copy-start
  2.4 3.0 %collective-permute-start.3 = (bf16[32,3712]{1,0:T(8,128)(2,1)S(1)}, bf16[32,3712]{1,0:T(8,128)(2,1)S(1)}, u32[]{:S(2)}, u32[]{:S(2)}) collective-permute-start(bf16[32,3712]{1,0:T(8,128)(2,1)S(1)} %get-tuple-element.30), channel_id=1, source_target_pairs={{0,2},{1,3},{2,0},{3,1},{4,6},{5,7},{6,4},{7,5},{8,10},{9,11},{10,... | collective-permute-start | bytes 712712 | tf_op jit(solution)/shard_map/ppermute | solution.py:21
  5.4 0.0 copy-done.2
  5.4 0.0 collective-permute-start
  5.4 0.0 copy-done.3
  5.4 0.5 collective-permute-start.1
  5.9 0.0 copy-done.4
  5.9 0.1 collective-permute-start.2
  6.0 0.5 scope_tail.1
  6.4 0.2 collective-permute-start.4
  6.6 5.4 %collective-permute-done.3.refs_0_.refs_1_.first_ref = bf16[32,3712]{1,0:T(8,128)(2,1)S(1)} collective-permute-done((bf16[32,3712]{1,0:T(8,128)(2,1)S(1)}, bf16[32,3712]{1,0:T(8,128)(2,1)S(1)}, u32[]{:S(2)}, u32[]{:S(2)}) %collective-permute-start.3) | collective-permute-done | bytes 237600 | tf_op jit(solution)/shard_map/ppermute | solution.py:21
  12.0 0.0 copy-done
  12.0 0.9 %scope_join.1 = (bf16[16,3584]{1,0:T(8,128)(2,1)S(1)}, bf16[16,3584]{1,0:T(8,128)(2,1)}, bf16[16,3584]{1,0:T(8,128)(2,1)S(1)}, bf16[16,3584]{1,0:T(8,128)(2,1)S(1)}) custom-call(bf16[64,3584]{1,0:T(8,128)(2,1)S(1)} %get-tuple-element.28.after_ref.refs_0_, bf16[32,3712]{1,0:T(8,128)(2,1)S(1)} %collective-permute-done.3.refs_0_.refs_1_.first_ref), custom_call_target="tpu_custom_call" | custom-call | flops 1000000000 | tf_op jit(solution)/shard_map/scope_join/pallas_call | solution.py:50
  12.9 2.1 %collective-permute-start.5 = (bf16[16,3584]{1,0:T(8,128)(2,1)}, bf16[16,3584]{1,0:T(8,128)(2,1)}, u32[]{:S(2)}, u32[]{:S(2)}) collective-permute-start(bf16[16,3584]{1,0:T(8,128)(2,1)} %get-tuple-element.37), channel_id=1, source_target_pairs={{0,4},{4,0},{8,12},{12,8},{1,5},{5,1},{9,13},{13,9},{2,6},{6,2},{1... | collective-permute-start | bytes 344072 | tf_op jit(solution)/shard_map/ppermute | solution.py:21
  15.1 2.7 %scope_load.1.refs_4_ = bf16[10752,256]{1,0:T(8,128)(2,1)S(1)} custom-call(bf16[3584,256]{1,0:T(8,128)(2,1)} %bitcast.5, bf16[3584,256]{1,0:T(8,128)(2,1)} %bitcast.6, bf16[256,3584]{1,0:T(8,128)(2,1)} %bitcast.7, bf16[16,3584]{1,0:T(8,128)(2,1)S(1)} %get-tuple-element.36.near_ref.refs_0_), custom_call_target="tpu_custom_call" | custom-call | flops 99999997952 | tf_op jit(solution)/shard_map/scope_load/pallas_call | solution.py:50
  17.8 0.0 collective-permute-done.gate.refs_2_
  17.8 2.7 %collective-permute-start.6 = (bf16[16,3584]{1,0:T(8,128)(2,1)S(1)}, bf16[16,3584]{1,0:T(8,128)(2,1)S(1)}, u32[]{:S(2)}, u32[]{:S(2)}) collective-permute-start(bf16[16,3584]{1,0:T(8,128)(2,1)S(1)} %get-tuple-element.38), channel_id=1, source_target_pairs={{0,8},{4,12},{8,0},{12,4},{1,9},{5,13},{9,1},{13,5},{2,10},{6,14},... | collective-permute-start | bytes 344072 | tf_op jit(solution)/shard_map/ppermute | solution.py:21
  20.4 0.0 collective-permute-done.1.up.refs_3_
  20.4 0.0 collective-permute-start.7
  20.4 0.0 collective-permute-done.2.down.refs_4_
  20.5 0.1 collective-permute-start.8
  20.5 3.7 %scope_own.1 = (f32[128,3584]{1,0:T(8,128)S(1)}, bf16[3584,256]{1,0:T(8,128)(2,1)S(1)}, bf16[3584,256]{1,0:T(8,128)(2,1)S(1)}, bf16[256,3584]{1,0:T(8,128)(2,1)S(1)}) custom-call(bf16[128,3584]{1,0:T(8,128)(2,1)S(1)} %get-tuple-element.25.refs_2_.tokens_ref, bf16[3584,256]{1,0:T(8,128)(2,1)S(1)} %collective-permute-done.gate.refs_2_, ...), custom_call_target="tpu_custom_call" | custom-call | flops 3000000000 | tf_op jit(solution)/shard_map/scope_own/pallas_call | solution.py:50
  24.2 1.7 %collective-permute-done.4.refs_1_ = bf16[96,3584]{1,0:T(8,128)(2,1)S(1)} collective-permute-done((bf16[96,3584]{1,0:T(8,128)(2,1)S(1)}, bf16[96,3584]{1,0:T(8,128)(2,1)S(1)}, u32[]{:S(2)}, u32[]{:S(2)}) %collective-permute-start.4) | collective-permute-done | bytes 688160 | tf_op jit(solution)/shard_map/ppermute | solution.py:21
  25.9 1.8 %scope_far.1 = (f32[32,3584]{1,0:T(8,128)S(1)}, bf16[96,3584]{1,0:T(8,128)(2,1)S(1)}) custom-call(bf16[32,3712]{1,0:T(8,128)(2,1)S(1)} %collective-permute-done.3.refs_0_.refs_1_.first_ref, bf16[96,3584]{1,0:T(8,128)(2,1)S(1)} %collective-permute-done.4.refs_1_, bf16[3584,256]{1,0:T(8,128)(2,1)S(1)} %collective-permute-done.gate.refs_2_, ...), custom_call_target="tpu_custom_call" | custom-call | flops 99999997952 | tf_op jit(solution)/shard_map/scope_far/pallas_call | solution.py:50
  27.7 1.8 %collective-permute-start.13 = (bf16[96,3584]{1,0:T(8,128)(2,1)S(1)}, bf16[96,3584]{1,0:T(8,128)(2,1)S(1)}, u32[]{:S(2)}, u32[]{:S(2)}) collective-permute-start(bf16[96,3584]{1,0:T(8,128)(2,1)S(1)} %get-tuple-element.44), channel_id=1, source_target_pairs={{0,2},{1,3},{2,0},{3,1},{4,6},{5,7},{6,4},{7,5},{8,10},{9,11},{10,... | collective-permute-start | bytes 2064392 | tf_op jit(solution)/shard_map/ppermute | solution.py:21
  29.5 0.0 collective-permute-done.5.refs_1_
  29.5 0.0 collective-permute-done.6.refs_2_
  29.5 0.0 collective-permute-done.7.refs_3_
  29.5 0.1 collective-permute-done.8.refs_5_
  29.6 3.0 %scope_expert.1 = (bf16[16,3584]{1,0:T(8,128)(2,1)S(1)}, bf16[16,3584]{1,0:T(8,128)(2,1)S(1)}, bf16[16,3584]{1,0:T(8,128)(2,1)S(1)}, bf16[16,3584]{1,0:T(8,128)(2,1)S(1)}) custom-call(bf16[16,3584]{1,0:T(8,128)(2,1)S(1)} %get-tuple-element.36.near_ref.refs_0_, bf16[16,3584]{1,0:T(8,128)(2,1)} %collective-permute-done.5.refs_1_, ...), custom_call_target="tpu_custom_call" | custom-call | flops 100000000 | tf_op jit(solution)/shard_map/scope_expert/pallas_call | solution.py:50
  32.6 1.6 %collective-permute-start.9 = (bf16[16,3584]{1,0:T(8,128)(2,1)S(1)}, bf16[16,3584]{1,0:T(8,128)(2,1)S(1)}, u32[]{:S(2)}, u32[]{:S(2)}) collective-permute-start(bf16[16,3584]{1,0:T(8,128)(2,1)S(1)} %get-tuple-element.41), channel_id=1, source_target_pairs={{0,4},{4,0},{8,12},{12,8},{1,5},{5,1},{9,13},{13,9},{2,6},{6,2},{1... | collective-permute-start | bytes 344072 | tf_op jit(solution)/shard_map/ppermute | solution.py:21
  34.2 2.8 %collective-permute-start.10 = (bf16[16,3584]{1,0:T(8,128)(2,1)S(1)}, bf16[16,3584]{1,0:T(8,128)(2,1)S(1)}, u32[]{:S(2)}, u32[]{:S(2)}) collective-permute-start(bf16[16,3584]{1,0:T(8,128)(2,1)S(1)} %get-tuple-element.42), channel_id=1, source_target_pairs={{0,8},{4,12},{8,0},{12,4},{1,9},{5,13},{9,1},{13,5},{2,10},{6,14},... | collective-permute-start | bytes 344072 | tf_op jit(solution)/shard_map/ppermute | solution.py:21
  37.0 0.1 collective-permute-start.11
  37.0 2.3 %collective-permute-done.9.refs_1_.refs_5_ = bf16[16,3584]{1,0:T(8,128)(2,1)S(1)} collective-permute-done((bf16[16,3584]{1,0:T(8,128)(2,1)S(1)}, bf16[16,3584]{1,0:T(8,128)(2,1)S(1)}, u32[]{:S(2)}, u32[]{:S(2)}) %collective-permute-start.9) | collective-permute-done | bytes 114720 | tf_op jit(solution)/shard_map/ppermute | solution.py:21
  39.3 6.7 %collective-permute-done.10.refs_2_.refs_6_ = bf16[16,3584]{1,0:T(8,128)(2,1)S(1)} collective-permute-done((bf16[16,3584]{1,0:T(8,128)(2,1)S(1)}, bf16[16,3584]{1,0:T(8,128)(2,1)S(1)}, u32[]{:S(2)}, u32[]{:S(2)}) %collective-permute-start.10) | collective-permute-done | bytes 114720 | tf_op jit(solution)/shard_map/ppermute | solution.py:21
  46.0 0.0 collective-permute-done.11.refs_3_.refs_7_
  46.0 0.0 copy-start.1
  46.0 0.3 scope_fold.1
  46.3 1.4 %collective-permute-start.12 = (bf16[32,3584]{1,0:T(8,128)(2,1)S(1)}, bf16[32,3584]{1,0:T(8,128)(2,1)S(1)}, u32[]{:S(2)}, u32[]{:S(2)}) collective-permute-start(bf16[32,3584]{1,0:T(8,128)(2,1)S(1)} %scope_fold.1), channel_id=1, source_target_pairs={{0,2},{1,3},{2,0},{3,1},{4,6},{5,7},{6,4},{7,5},{8,10},{9,11},{10,... | collective-permute-start | bytes 688136 | tf_op jit(solution)/shard_map/ppermute | solution.py:21
  47.7 0.0 collective-permute-done.13.refs_3_
  47.7 4.7 %collective-permute-done.12.refs_2_ = bf16[32,3584]{1,0:T(8,128)(2,1)S(1)} collective-permute-done((bf16[32,3584]{1,0:T(8,128)(2,1)S(1)}, bf16[32,3584]{1,0:T(8,128)(2,1)S(1)}, u32[]{:S(2)}, u32[]{:S(2)}) %collective-permute-start.12) | collective-permute-done | bytes 229408 | tf_op jit(solution)/shard_map/ppermute | solution.py:21
  52.4 0.0 copy-done.1
  52.4 1.2 %scope_final.1 = bf16[128,3584]{1,0:T(8,128)(2,1)} custom-call(f32[128,3584]{1,0:T(8,128)S(1)} %get-tuple-element.29.refs_0_, bf16[256,128]{1,0:T(8,128)(2,1)S(1)} %copy-done.1, bf16[32,3584]{1,0:T(8,128)(2,1)S(1)} %collective-permute-done.12.refs_2_, bf16[96,3584]{1,0:T(8,128)(2,1)S(1)} %collective-permute-done.13.refs_3_, ...), custom_call_target="tpu_custom_call" | custom-call | flops 99999997952 | tf_op jit(solution)/shard_map/scope_final/pallas_call | solution.py:325
  (1 shorter events, 0.0 us)
Async XLA Ops:
  0.0 5.4 %copy-start.2 = (bf16[3584,256]{1,0:T(8,128)(2,1)S(1)}, bf16[3584,256]{1,0:T(8,128)(2,1)}, u32[]{:S(2)}) copy-start(bf16[3584,256]{1,0:T(8,128)(2,1)} %sg_hbm.1) | copy-start | bytes 5505028
  0.0 5.4 %copy-start.3 = (bf16[3584,256]{1,0:T(8,128)(2,1)S(1)}, bf16[3584,256]{1,0:T(8,128)(2,1)}, u32[]{:S(2)}) copy-start(bf16[3584,256]{1,0:T(8,128)(2,1)} %su_hbm.1) | copy-start | bytes 5505028
  0.0 5.9 %copy-start.4 = (bf16[256,3584]{1,0:T(8,128)(2,1)S(1)}, bf16[256,3584]{1,0:T(8,128)(2,1)}, u32[]{:S(2)}) copy-start(bf16[256,3584]{1,0:T(8,128)(2,1)} %sd_hbm.1) | copy-start | bytes 5505028
  2.3 9.6 %copy-start = (bf16[256,128]{1,0:T(8,128)(2,1)}, bf16[256,128]{1,0:T(8,128)(2,1)S(1)}, u32[]{:S(2)}) copy-start(bf16[256,128]{1,0:T(8,128)(2,1)S(1)} %get-tuple-element.26.refs_0_.refs_1_) | copy-start | bytes 196612
  2.4 9.6 %collective-permute-start.3 = (bf16[32,3712]{1,0:T(8,128)(2,1)S(1)}, bf16[32,3712]{1,0:T(8,128)(2,1)S(1)}, u32[]{:S(2)}, u32[]{:S(2)}) collective-permute-start(bf16[32,3712]{1,0:T(8,128)(2,1)S(1)} %get-tuple-element.30), channel_id=1, source_target_pairs={{0,2},{1,3},{2,0},{3,1},{4,6},{5,7},{6,4},{7,5},{8,10},{9,11},{10,... | collective-permute-start | bytes 712712 | tf_op jit(solution)/shard_map/ppermute | solution.py:21
  5.4 12.4 %collective-permute-start = (bf16[3584,256]{1,0:T(8,128)(2,1)S(1)}, bf16[3584,256]{1,0:T(8,128)(2,1)S(1)}, u32[]{:S(2)}, u32[]{:S(2)}) collective-permute-start(bf16[3584,256]{1,0:T(8,128)(2,1)S(1)} %copy-done.2), channel_id=1, source_target_pairs={{0,1},{1,0},{2,3},{3,2},{4,5},{5,4},{6,7},{7,6},{8,9},{9,8},{10,11... | collective-permute-start | bytes 5505032 | tf_op jit(solution)/shard_map/ppermute | solution.py:21
  5.4 15.0 %collective-permute-start.1 = (bf16[3584,256]{1,0:T(8,128)(2,1)S(1)}, bf16[3584,256]{1,0:T(8,128)(2,1)S(1)}, u32[]{:S(2)}, u32[]{:S(2)}) collective-permute-start(bf16[3584,256]{1,0:T(8,128)(2,1)S(1)} %copy-done.3), channel_id=1, source_target_pairs={{0,1},{1,0},{2,3},{3,2},{4,5},{5,4},{6,7},{7,6},{8,9},{9,8},{10,11... | collective-permute-start | bytes 5505032 | tf_op jit(solution)/shard_map/ppermute | solution.py:21
  5.9 14.5 %collective-permute-start.2 = (bf16[256,3584]{1,0:T(8,128)(2,1)S(1)}, bf16[256,3584]{1,0:T(8,128)(2,1)S(1)}, u32[]{:S(2)}, u32[]{:S(2)}) collective-permute-start(bf16[256,3584]{1,0:T(8,128)(2,1)S(1)} %copy-done.4), channel_id=1, source_target_pairs={{0,1},{1,0},{2,3},{3,2},{4,5},{5,4},{6,7},{7,6},{8,9},{9,8},{10,11... | collective-permute-start | bytes 5505032 | tf_op jit(solution)/shard_map/ppermute | solution.py:21
  6.4 19.5 %collective-permute-start.4 = (bf16[96,3584]{1,0:T(8,128)(2,1)S(1)}, bf16[96,3584]{1,0:T(8,128)(2,1)S(1)}, u32[]{:S(2)}, u32[]{:S(2)}) collective-permute-start(bf16[96,3584]{1,0:T(8,128)(2,1)S(1)} %get-tuple-element.31), channel_id=1, source_target_pairs={{0,2},{1,3},{2,0},{3,1},{4,6},{5,7},{6,4},{7,5},{8,10},{9,11},{10,... | collective-permute-start | bytes 2064392 | tf_op jit(solution)/shard_map/ppermute | solution.py:21
  12.9 16.5 %collective-permute-start.5 = (bf16[16,3584]{1,0:T(8,128)(2,1)}, bf16[16,3584]{1,0:T(8,128)(2,1)}, u32[]{:S(2)}, u32[]{:S(2)}) collective-permute-start(bf16[16,3584]{1,0:T(8,128)(2,1)} %get-tuple-element.37), channel_id=1, source_target_pairs={{0,4},{4,0},{8,12},{12,8},{1,5},{5,1},{9,13},{13,9},{2,6},{6,2},{1... | collective-permute-start | bytes 344072 | tf_op jit(solution)/shard_map/ppermute | solution.py:21
  17.8 11.7 %collective-permute-start.6 = (bf16[16,3584]{1,0:T(8,128)(2,1)S(1)}, bf16[16,3584]{1,0:T(8,128)(2,1)S(1)}, u32[]{:S(2)}, u32[]{:S(2)}) collective-permute-start(bf16[16,3584]{1,0:T(8,128)(2,1)S(1)} %get-tuple-element.38), channel_id=1, source_target_pairs={{0,8},{4,12},{8,0},{12,4},{1,9},{5,13},{9,1},{13,5},{2,10},{6,14},... | collective-permute-start | bytes 344072 | tf_op jit(solution)/shard_map/ppermute | solution.py:21
  20.4 9.0 %collective-permute-start.7 = (bf16[16,3584]{1,0:T(8,128)(2,1)S(1)}, bf16[16,3584]{1,0:T(8,128)(2,1)S(1)}, u32[]{:S(2)}, u32[]{:S(2)}) collective-permute-start(bf16[16,3584]{1,0:T(8,128)(2,1)S(1)} %get-tuple-element.39), channel_id=1, source_target_pairs={{0,12},{4,8},{8,4},{12,0},{1,13},{5,9},{9,5},{13,1},{2,14},{6,10},... | collective-permute-start | bytes 344072 | tf_op jit(solution)/shard_map/ppermute | solution.py:21
  20.5 9.1 %collective-permute-start.8 = (bf16[10752,256]{1,0:T(8,128)(2,1)S(1)}, bf16[10752,256]{1,0:T(8,128)(2,1)S(1)}, u32[]{:S(2)}, u32[]{:S(2)}) collective-permute-start(bf16[10752,256]{1,0:T(8,128)(2,1)S(1)} %scope_load.1.refs_4_), channel_id=1, source_target_pairs={{0,1},{1,0},{2,3},{3,2},{4,5},{5,4},{6,7},{7,6},{8,9},{9,8},{10,11... | collective-permute-start | bytes 16515080 | tf_op jit(solution)/shard_map/ppermute | solution.py:21
  27.7 20.0 %collective-permute-start.13 = (bf16[96,3584]{1,0:T(8,128)(2,1)S(1)}, bf16[96,3584]{1,0:T(8,128)(2,1)S(1)}, u32[]{:S(2)}, u32[]{:S(2)}) collective-permute-start(bf16[96,3584]{1,0:T(8,128)(2,1)S(1)} %get-tuple-element.44), channel_id=1, source_target_pairs={{0,2},{1,3},{2,0},{3,1},{4,6},{5,7},{6,4},{7,5},{8,10},{9,11},{10,... | collective-permute-start | bytes 2064392 | tf_op jit(solution)/shard_map/ppermute | solution.py:21
  32.6 6.7 %collective-permute-start.9 = (bf16[16,3584]{1,0:T(8,128)(2,1)S(1)}, bf16[16,3584]{1,0:T(8,128)(2,1)S(1)}, u32[]{:S(2)}, u32[]{:S(2)}) collective-permute-start(bf16[16,3584]{1,0:T(8,128)(2,1)S(1)} %get-tuple-element.41), channel_id=1, source_target_pairs={{0,4},{4,0},{8,12},{12,8},{1,5},{5,1},{9,13},{13,9},{2,6},{6,2},{1... | collective-permute-start | bytes 344072 | tf_op jit(solution)/shard_map/ppermute | solution.py:21
  34.2 11.9 %collective-permute-start.10 = (bf16[16,3584]{1,0:T(8,128)(2,1)S(1)}, bf16[16,3584]{1,0:T(8,128)(2,1)S(1)}, u32[]{:S(2)}, u32[]{:S(2)}) collective-permute-start(bf16[16,3584]{1,0:T(8,128)(2,1)S(1)} %get-tuple-element.42), channel_id=1, source_target_pairs={{0,8},{4,12},{8,0},{12,4},{1,9},{5,13},{9,1},{13,5},{2,10},{6,14},... | collective-permute-start | bytes 344072 | tf_op jit(solution)/shard_map/ppermute | solution.py:21
  37.0 9.1 %collective-permute-start.11 = (bf16[16,3584]{1,0:T(8,128)(2,1)S(1)}, bf16[16,3584]{1,0:T(8,128)(2,1)S(1)}, u32[]{:S(2)}, u32[]{:S(2)}) collective-permute-start(bf16[16,3584]{1,0:T(8,128)(2,1)S(1)} %get-tuple-element.43), channel_id=1, source_target_pairs={{0,12},{4,8},{8,4},{12,0},{1,13},{5,9},{9,5},{13,1},{2,14},{6,10},... | collective-permute-start | bytes 344072 | tf_op jit(solution)/shard_map/ppermute | solution.py:21
  46.0 6.4 %copy-start.1 = (bf16[256,128]{1,0:T(8,128)(2,1)S(1)}, bf16[256,128]{1,0:T(8,128)(2,1)}, u32[]{:S(2)}) copy-start(bf16[256,128]{1,0:T(8,128)(2,1)} %copy-done) | copy-start | bytes 196612
  46.3 6.1 %collective-permute-start.12 = (bf16[32,3584]{1,0:T(8,128)(2,1)S(1)}, bf16[32,3584]{1,0:T(8,128)(2,1)S(1)}, u32[]{:S(2)}, u32[]{:S(2)}) collective-permute-start(bf16[32,3584]{1,0:T(8,128)(2,1)S(1)} %scope_fold.1), channel_id=1, source_target_pairs={{0,2},{1,3},{2,0},{3,1},{4,6},{5,7},{6,4},{7,5},{8,10},{9,11},{10,... | collective-permute-start | bytes 688136 | tf_op jit(solution)/shard_map/ppermute | solution.py:21

commit v4 on v3

--- a/solution.py
+++ b/solution.py
@@ -7,7 +7,7 @@
 
 EXPERTS_PER_NODE = 8
 FEW_NODES = 8
-COST = {"head": 3000000000, "tail": 100000000, "load": 100000000000, "join": 1000000000, "own": 3000000000, "expert": 100000000, "far": 100000000000, "fold": 3000000000, "final": 100000000000}
+COST = {"head": 100000000, "tail": 3000000000, "load": 30000000000, "join": 30000000000, "own": 100000000, "expert": 30000000000, "far0": 1, "far1": 10000000000, "fold": 1000000000, "final": 10000000000, "last": 30000000000}
 PIECES = 4
 HBM = pl.BlockSpec(memory_space=pltpu.HBM)
 VMEM = pl.BlockSpec(memory_space=pltpu.VMEM)
@@ -21,12 +21,16 @@
     return lax.ppermute(value, axis, [(i, i ^ mask) for i in range(size)])
 
 
-def over_nodes(pieces):
+def over_nodes(pieces, known=()):
     count = len(pieces)
+    known = known or [None] * count
     if count > FEW_NODES:
         moved = lax.all_to_all(jnp.stack(pieces), "node", split_axis=0, concat_axis=0, tiled=True)
         return [moved[n] for n in range(count)]
-    return [shift(piece, "node", m) if m else piece for m, piece in enumerate(pieces)]
+    moved = list(pieces)
+    for m in range(count - 1, 0, -1):
+        moved[m] = shift(pieces[m], "node", m) if known[m] is None else known[m]
+    return moved
 
 
 def dot(a, b, dims=(((1,), (0,)), ((), ()))):
@@ -116,14 +120,20 @@
     first_ref[:, :width] = bf16(dot(order[:head], tokens_ref[...]))
 
 
-def tail_kernel(head, mix_ref, pick_ref, tokens_ref, near_ref, rest_ref=None):
+def tail_kernel(head, mix_ref, pick_ref, tokens_ref, near_ref, *rest):
     tokens = tokens_ref[...]
-    if rest_ref is not None:
-        rest_ref[...] = bf16(dot(mix_ref[head : tokens_ref.shape[0]], tokens))
+    for out in rest:
+        out[...] = bf16(dot(mix_ref[head : head + out.shape[0]], tokens))
+        head += out.shape[0]
     near_ref[...] = bf16(dot(pick_ref[...], tokens))
 
 
-def join_kernel(block, near_ref, first_ref, *outs):
+def last_kernel(start, mix_ref, tokens_ref, after_ref, out_ref):
+    out_ref[...] = bf16(dot(mix_ref[start : start + out_ref.shape[0]], tokens_ref[...]))
+
+
+def join_kernel(nodes, block, near_ref, first_ref, *outs):
+    outs = outs[-nodes:]
     slots, width = near_ref.shape
     high = first_ref[:, width : width + slots].astype(jnp.float32)
     pick = bf16((high != 0.0).astype(jnp.float32))
@@ -159,6 +169,7 @@
     rows = [r[...] for r in refs[:nodes]]
     packs, outs = refs[nodes : nodes + 2], refs[nodes + 2 :]
     block, width = rows[0].shape
+    half = block // 2
     part = packs[0].shape[1]
     rows = jnp.concatenate(rows, axis=0)
     hidden = []
@@ -168,8 +179,19 @@
     for i in range(0, width, part):
         down = slice(2 * width + i, 2 * width + i + part)
         sums = dot(hidden[0], packs[0][down]) + dot(hidden[1], packs[1][down])
-        for n, out in enumerate(outs):
-            out[:, i : i + part] = bf16(sums[n * block : (n + 1) * block])
+        start = 0
+        for out in outs:
+            size = out.shape[0]
+            out[:, i : i + part] = bf16(sums[start : start + size])
+            start += size
+
+
+def blocks_of(refs, block, cols=slice(None)):
+    pieces = []
+    for r in refs:
+        piece = r[:, cols].astype(jnp.float32)
+        pieces += [piece] * (block // piece.shape[0])
+    return bf16(jnp.concatenate(pieces, axis=0))
 
 
 def own_kernel(
@@ -196,16 +218,16 @@
         start += out.shape[0]
 
 
-def fold_kernel(part_ref, first_ref, *refs):
+def fold_kernel(block, part_ref, first_ref, *refs):
     width = part_ref.shape[1]
-    replies = jnp.concatenate([r[...] for r in refs[:-1]], axis=0)
+    replies = blocks_of(refs[:-1], block)
     slots = replies.shape[0]
     high = first_ref[:, width : width + slots]
     low = first_ref[:, width + slots :]
     refs[-1][...] = bf16(part_ref[...] + dot(high, replies) + dot(low, replies))
 
 
-def final_kernel(back_count, *refs):
+def final_kernel(block, back_count, *refs):
     own_ref, mix_ref = refs[:2]
     backs, replies = refs[2 : 2 + back_count], refs[2 + back_count : -3]
     out_hbm, out_ref, sems = refs[-3:]
@@ -214,8 +236,8 @@
     copies = []
     for i in range(PIECES):
         cols = slice(i * tile, (i + 1) * tile)
-        reply = [r[:, cols] for r in replies]
-        terms = jnp.concatenate([*[r[:, cols] for r in backs], *reply, *reply], axis=0)
+        reply = blocks_of(replies, block, cols)
+        terms = jnp.concatenate([*[r[:, cols] for r in backs], reply, reply], axis=0)
         out_ref[:, cols] = bf16(own_ref[:, cols] + dot(mix_ref[...], terms, ROWS))
         copies.append(pltpu.make_async_copy(out_ref.at[:, cols], out_hbm.at[:, cols], sems.at[i]))
         copies[-1].start()
@@ -257,21 +279,22 @@
         limit=16 << 20,
     )
     far_first = shift(first, "local", 2)
+    cut = tail * 2 // 3 // 16 * 16
     near, *rest = call(
         "tail",
         lambda *refs: tail_kernel(head, *refs),
-        [struct(slots, width)] + [struct(tail, width)] * (tail > 0),
+        [struct(slots, width)] + [struct(cut, width)] * (cut > 0),
         (mix, pick, held),
         room=4 * (slots + count) * width,
     )
-    far = [far_first] + [shift(r, "local", 2) for r in rest]
+    rest_far = [shift(r, "local", 2) for r in rest]
     shared_mats = (s_gate, s_up, s_down)
     shared_far = [shift(w, "local", 1) for w in shared_mats]
     sent = call(
         "join",
-        lambda *refs: join_kernel(block, *refs),
+        lambda *refs: join_kernel(nodes, block, *refs),
         [struct(block, width)] * nodes,
-        (near, far_first),
+        (near, far_first, *[]),
         room=8 * slots * width,
     )
     part = w_gate.shape[2]
@@ -279,13 +302,22 @@
         "load",
         load_kernel,
         struct(3 * width, part),
-        (w_gate[0], w_up[0], w_down[0], sent[0]),
+        (w_gate[0], w_up[0], w_down[0], first),
         specs=[HBM] * 3 + [VMEM],
         scratch=[pltpu.SemaphoreType.DMA((2 + width // part,))],
         limit=16 << 20,
     )
     far_pack = shift(pack, "local", 1)
     arrived = over_nodes(sent)
+    if tail > cut:
+        last = call(
+            "last",
+            lambda *refs: last_kernel(head + cut, *refs),
+            struct(tail - cut, width),
+            (mix, held, sent[0]),
+            room=4 * count * width,
+        )
+        rest_far.append(shift(last, "local", 2))
     own, *mats = call(
         "own",
         own_kernel,
@@ -298,32 +330,47 @@
         scratch=[pltpu.SemaphoreType.DMA((3,))],
         limit=16 << 20,
     )
+    whole = [n == 1 and nodes <= FEW_NODES for n in range(nodes)]
     replied = call(
         "expert",
         lambda *refs: expert_kernel(nodes, *refs),
-        [struct(block, width)] * nodes,
+        [
+            struct(rows, width)
+            for n in range(nodes)
+            for rows in ([block] if whole[n] else [capacity] * 2)
+        ],
         (*arrived, pack, far_pack),
         room=20 * slots * width + (4 << 20),
     )
-    replies = over_nodes(replied)
-    sums_first, *sums = call(
-        "far",
-        lambda *refs: far_kernel(len(far), *refs),
-        [struct(head, width, jnp.float32)] + [struct(tail, width)] * len(rest),
-        (*far, *shared_far, *mats),
-        room=12 * count * width,
-    )
-    late = [shift(r, "local", 2) for r in sums]
+    split = iter(replied)
+    pairs = [[next(split)] if w else [next(split), next(split)] for w in whole]
+    far_replies = over_nodes([p[-1] for p in pairs])
+    replies = over_nodes([p[0] for p in pairs], [f if w else None for f, w in zip(far_replies, whole)])
+
+    sums, late = [], []
+    for i, rows in enumerate(([far_first] + rest_far[:1], rest_far[1:])):
+        if rows:
+            sums += call(
+                "far" + str(i),
+                lambda *refs, n=len(rows): far_kernel(n, *refs),
+                [
+                    struct(r.shape[0], width, jnp.float32 if r is far_first else jnp.bfloat16)
+                    for r in rows
+                ],
+                (*rows, *shared_far, *mats),
+                room=12 * count * width,
+            )
+    late = [shift(r, "local", 2) for r in sums[1:]]
     folded = call(
         "fold",
-        fold_kernel,
+        lambda *refs: fold_kernel(block, *refs),
         struct(head, width),
-        (sums_first, far_first, *replies),
+        (sums[0], far_first, *far_replies),
         room=8 * slots * width,
     )
     backs = [shift(folded, "local", 2)] + late
     return pl.pallas_call(
-        lambda *refs: final_kernel(len(backs), *refs),
+        lambda *refs: final_kernel(block, len(backs), *refs),
         name="scope_final",
         out_shape=struct(count, width),
         in_specs=[VMEM] * (2 + len(backs) + nodes),

time: 53.8 us -> 51.6 us (0.959)
  waiting for transfers between devices: 20.8 us -> 10.3 us
  starting transfers between devices: 16.3 us -> 22 us
  local copies, waits for them, and re-layouts: 0.02 us -> 2.09 us
  Pallas kernels: 16.3 us -> 17 us
    ppermute x14 -> x18, waiting for transfers between devices: 20.8 us -> 10.3 us  [shift(): return lax.ppermute(value, axis, [(i, i ^ mask) for i in range(size)])]
    ppermute x14 -> x18, starting transfers between devices: 16.3 us -> 22 us  [shift(): return lax.ppermute(value, axis, [(i, i ^ mask) for i in range(size)])]
    unnamed x10 -> x6, local copies, waits for them, and re-layouts: 0.02 us -> 2.09 us
    pallas_call x8 -> x10, Pallas kernels: 15.1 us -> 15.8 us  [call(): pl.pallas_call(kernel, name='scope_' + name, out_shape=outs, in_specs=spe...]
  transfers between devices with their start and end apart: 14 -> 18, of which waited for: 6 -> 6; matrix products, arithmetic and copies ran while one was open for 0% -> 0% of each run, Pallas kernels for 24% -> 27%
where the time goes in v4:
time: 51.6 us; the launch traced here: 51.5 us
  starting transfers between devices  22 us (43%)
  Pallas kernels  17 us (33%)
  waiting for transfers between devices  10.3 us (20%)
  local copies, waits for them, and re-layouts  2.09 us (4%)
    ppermute x18, starting transfers between devices, shift(): return lax.ppermute(value, axis, [(i, i ^ mask) for i in range(size)])  22 us
    pallas_call x10, Pallas kernels, call(): pl.pallas_call(kernel, name='scope_' + name, out_shape=outs, in_specs=spe...  15.8 us
    ppermute x18, waiting for transfers between devices, shift(): return lax.ppermute(value, axis, [(i, i ^ mask) for i in range(size)])  10.3 us
    unnamed x6, local copies, waits for them, and re-layouts  2.09 us
    pallas_call x1, Pallas kernels, per_device(): pl.pallas_call(lambda *refs: final_kernel(block, len(backs), *refs), name...  1.22 us
  transfers between devices with their start and end apart: 18, of which 6 were waited for; matrix products, arithmetic and copies ran while one was open for 0% of the time, Pallas kernels for 27%

profile of v4, /device:TPU:0, one launch (start us, length us, event | category | flops | bytes accessed | tf_op | source)
XLA Modules:
  0.0 51.5 jit_solution(11883606374728507887)
XLA Ops:
  0.0 2.0 %scope_head.1 = (bf16[32,3712]{1,0:T(8,128)(2,1)S(1)}, bf16[256,128]{1,0:T(8,128)(2,1)S(1)}, bf16[64,128]{1,0:T(8,128)(2,1)S(1)}, bf16[128,3584]{1,0:T(8,128)(2,1)S(1)}) custom-call(s32[4]{0:T(128)S(1)} %xor_multiply_fusion.refs_0_, s32[8,128]{1,0:T(8,128)} %bitcast.5, f32[8,128]{1,0:T(8,128)} %bitcast.6, bf16[128,3584]{1,0:T(8,128)(2,1)} %refs_3_.1), custom_call_target="tpu_custom_call" | custom-call | flops 100000000 | tf_op jit(solution)/shard_map/scope_head/pallas_call | solution.py:54
  2.1 3.0 %collective-permute-start.3 = (bf16[32,3712]{1,0:T(8,128)(2,1)S(1)}, bf16[32,3712]{1,0:T(8,128)(2,1)S(1)}, u32[]{:S(2)}, u32[]{:S(2)}) collective-permute-start(bf16[32,3712]{1,0:T(8,128)(2,1)S(1)} %get-tuple-element.33.near_ref), channel_id=1, source_target_pairs={{0,2},{1,3},{2,0},{3,1},{4,6},{5,7},{6,4},{7,5},{8,10},{9,11},{10,... | collective-permute-start | bytes 712712 | tf_op jit(solution)/shard_map/ppermute | solution.py:21
  5.1 0.4 scope_tail.1
  5.5 0.1 collective-permute-start.4
  5.6 1.0 %copy-done = bf16[3584,256]{1,0:T(8,128)(2,1)S(1)} copy-done((bf16[3584,256]{1,0:T(8,128)(2,1)S(1)}, bf16[3584,256]{1,0:T(8,128)(2,1)}, u32[]{:S(2)}) %copy-start) | copy-done | bytes 1835032
  6.6 0.0 collective-permute-start
  6.6 0.5 %copy-done.1 = bf16[3584,256]{1,0:T(8,128)(2,1)S(1)} copy-done((bf16[3584,256]{1,0:T(8,128)(2,1)S(1)}, bf16[3584,256]{1,0:T(8,128)(2,1)}, u32[]{:S(2)}) %copy-start.1) | copy-done | bytes 1835032
  7.1 0.0 collective-permute-start.1
  7.1 0.6 %copy-done.2 = bf16[256,3584]{1,0:T(8,128)(2,1)S(1)} copy-done((bf16[256,3584]{1,0:T(8,128)(2,1)S(1)}, bf16[256,3584]{1,0:T(8,128)(2,1)}, u32[]{:S(2)}) %copy-start.2) | copy-done | bytes 1835032
  7.7 0.0 collective-permute-start.2
  7.7 2.7 %scope_load.1.refs_4_ = bf16[10752,256]{1,0:T(8,128)(2,1)S(1)} custom-call(bf16[3584,256]{1,0:T(8,128)(2,1)} %bitcast.7, bf16[3584,256]{1,0:T(8,128)(2,1)} %bitcast.8, bf16[256,3584]{1,0:T(8,128)(2,1)} %bitcast.9, bf16[32,3712]{1,0:T(8,128)(2,1)S(1)} %get-tuple-element.33.near_ref), custom_call_target="tpu_custom_call" | custom-call | flops 30000001024 | tf_op jit(solution)/shard_map/scope_load/pallas_call | solution.py:54
  10.4 1.3 %collective-permute-done.3.refs_0_.refs_1_ = bf16[32,3712]{1,0:T(8,128)(2,1)S(1)} collective-permute-done((bf16[32,3712]{1,0:T(8,128)(2,1)S(1)}, bf16[32,3712]{1,0:T(8,128)(2,1)S(1)}, u32[]{:S(2)}, u32[]{:S(2)}) %collective-permute-start.3) | collective-permute-done | bytes 237600 | tf_op jit(solution)/shard_map/ppermute | solution.py:21
  11.7 0.0 collective-permute-start.8
  11.7 0.3 scope_join.1
  12.0 0.0 collective-permute-done.gate.refs_2_.refs_1_
  12.0 2.2 %collective-permute-start.5 = (bf16[16,3584]{1,0:T(8,128)(2,1)S(1)}, bf16[16,3584]{1,0:T(8,128)(2,1)S(1)}, u32[]{:S(2)}, u32[]{:S(2)}) collective-permute-start(bf16[16,3584]{1,0:T(8,128)(2,1)S(1)} %get-tuple-element.40), channel_id=1, source_target_pairs={{0,4},{4,0},{8,12},{12,8},{1,5},{5,1},{9,13},{13,9},{2,6},{6,2},{1... | collective-permute-start | bytes 344072 | tf_op jit(solution)/shard_map/ppermute | solution.py:21
  14.2 0.0 collective-permute-done.1.up.refs_3_.refs_2_
  14.2 2.6 %collective-permute-start.6 = (bf16[16,3584]{1,0:T(8,128)(2,1)S(1)}, bf16[16,3584]{1,0:T(8,128)(2,1)S(1)}, u32[]{:S(2)}, u32[]{:S(2)}) collective-permute-start(bf16[16,3584]{1,0:T(8,128)(2,1)S(1)} %get-tuple-element.41), channel_id=1, source_target_pairs={{0,8},{4,12},{8,0},{12,4},{1,9},{5,13},{9,1},{13,5},{2,10},{6,14},... | collective-permute-start | bytes 344072 | tf_op jit(solution)/shard_map/ppermute | solution.py:21
  16.8 0.0 collective-permute-done.2.down.refs_4_.refs_3_
  16.8 2.4 %collective-permute-start.7 = (bf16[16,3584]{1,0:T(8,128)(2,1)S(1)}, bf16[16,3584]{1,0:T(8,128)(2,1)S(1)}, u32[]{:S(2)}, u32[]{:S(2)}) collective-permute-start(bf16[16,3584]{1,0:T(8,128)(2,1)S(1)} %get-tuple-element.42), channel_id=1, source_target_pairs={{0,12},{4,8},{8,4},{12,0},{1,13},{5,9},{9,5},{13,1},{2,14},{6,10},... | collective-permute-start | bytes 344072 | tf_op jit(solution)/shard_map/ppermute | solution.py:21
  19.2 0.2 scope_last.1
  19.5 3.7 %scope_own.1 = (f32[128,3584]{1,0:T(8,128)S(1)}, bf16[3584,256]{1,0:T(8,128)(2,1)S(1)}, bf16[3584,256]{1,0:T(8,128)(2,1)S(1)}, bf16[256,3584]{1,0:T(8,128)(2,1)S(1)}) custom-call(bf16[128,3584]{1,0:T(8,128)(2,1)S(1)} %get-tuple-element.28.refs_2_.tokens_ref.refs_1_, bf16[3584,256]{1,0:T(8,128)(2,1)S(1)} %collective-permute-done.gate.refs_2_.refs_1_, ...), custom_call_target="tpu_custom_call" | custom-call | flops 100000000 | tf_op jit(solution)/shard_map/scope_own/pallas_call | solution.py:54
  23.1 0.0 collective-permute-done.4.refs_1_
  23.1 1.1 %collective-permute-start.14 = (bf16[32,3584]{1,0:T(8,128)(2,1)S(1)}, bf16[32,3584]{1,0:T(8,128)(2,1)S(1)}, u32[]{:S(2)}, u32[]{:S(2)}) collective-permute-start(bf16[32,3584]{1,0:T(8,128)(2,1)S(1)} %scope_last.1), channel_id=1, source_target_pairs={{0,2},{1,3},{2,0},{3,1},{4,6},{5,7},{6,4},{7,5},{8,10},{9,11},{10,... | collective-permute-start | bytes 688136 | tf_op jit(solution)/shard_map/ppermute | solution.py:21
  24.2 2.0 %scope_far0.1 = (f32[32,3584]{1,0:T(8,128)S(1)}, bf16[64,3584]{1,0:T(8,128)(2,1)S(1)}) custom-call(bf16[32,3712]{1,0:T(8,128)(2,1)S(1)} %collective-permute-done.3.refs_0_.refs_1_, bf16[64,3584]{1,0:T(8,128)(2,1)S(1)} %collective-permute-done.4.refs_1_, bf16[3584,256]{1,0:T(8,128)(2,1)S(1)} %collective-permute-done.gate.refs_2_.refs_1_, ...), custom_call_target="tpu_custom_call" | custom-call | flops 1 | tf_op jit(solution)/shard_map/scope_far0/pallas_call | solution.py:54
  26.2 0.0 collective-permute-done.5.refs_1_
  26.2 1.1 %collective-permute-start.13 = (bf16[64,3584]{1,0:T(8,128)(2,1)S(1)}, bf16[64,3584]{1,0:T(8,128)(2,1)S(1)}, u32[]{:S(2)}, u32[]{:S(2)}) collective-permute-start(bf16[64,3584]{1,0:T(8,128)(2,1)S(1)} %get-tuple-element.47), channel_id=1, source_target_pairs={{0,2},{1,3},{2,0},{3,1},{4,6},{5,7},{6,4},{7,5},{8,10},{9,11},{10,... | collective-permute-start | bytes 1376264 | tf_op jit(solution)/shard_map/ppermute | solution.py:21
  27.3 0.0 collective-permute-done.6.refs_2_
  27.3 0.0 collective-permute-done.7.refs_3_
  27.3 0.0 collective-permute-done.8.refs_5_
  27.3 2.1 %scope_expert.1 = (bf16[8,3584]{1,0:T(8,128)(2,1)S(1)}, bf16[8,3584]{1,0:T(8,128)(2,1)S(1)}, bf16[16,3584]{1,0:T(8,128)(2,1)S(1)}, bf16[8,3584]{1,0:T(8,128)(2,1...) custom-call(bf16[16,3584]{1,0:T(8,128)(2,1)S(1)} %get-tuple-element.39.refs_0_.refs_2_,, ...), custom_call_target="tpu_custom_call" | custom-call | flops 30000001024 | tf_op jit(solution)/shard_map/scope_expert/pallas_call | solution.py:54
  29.4 2.2 %collective-permute-start.10 = (bf16[8,3584]{1,0:T(8,128)(2,1)S(1)}, bf16[8,3584]{1,0:T(8,128)(2,1)S(1)}, u32[]{:S(2)}, u32[]{:S(2)}) collective-permute-start(bf16[8,3584]{1,0:T(8,128)(2,1)S(1)} %get-tuple-element.45), channel_id=1, source_target_pairs={{0,8},{4,12},{8,0},{12,4},{1,9},{5,13},{9,1},{13,5},{2,10},{6,14},... | collective-permute-start | bytes 172040 | tf_op jit(solution)/shard_map/ppermute | solution.py:21
  31.6 1.3 %collective-permute-start.11 = (bf16[8,3584]{1,0:T(8,128)(2,1)S(1)}, bf16[8,3584]{1,0:T(8,128)(2,1)S(1)}, u32[]{:S(2)}, u32[]{:S(2)}) collective-permute-start(bf16[8,3584]{1,0:T(8,128)(2,1)S(1)} %get-tuple-element.46), channel_id=1, source_target_pairs={{0,12},{4,8},{8,4},{12,0},{1,13},{5,9},{9,5},{13,1},{2,14},{6,10},... | collective-permute-start | bytes 172040 | tf_op jit(solution)/shard_map/ppermute | solution.py:21
  32.9 0.1 collective-permute-start.9
  33.0 0.0 collective-permute-done.14.refs_0_
  33.0 2.1 %scope_far1.1 = bf16[32,3584]{1,0:T(8,128)(2,1)S(1)} custom-call(bf16[32,3584]{1,0:T(8,128)(2,1)S(1)} %collective-permute-done.14.refs_0_, bf16[3584,256]{1,0:T(8,128)(2,1)S(1)} %collective-permute-done.gate.refs_2_.refs_1_, bf16[3584,256]{1,0:T(8,128)(2,1)S(1)} %collective-permute-done.1.up.refs_3_.refs_2_, ...), custom_call_target="tpu_custom_call" | custom-call | flops 10000000000 | tf_op jit(solution)/shard_map/scope_far1/pallas_call | solution.py:54
  35.0 1.5 %collective-permute-start.15 = (bf16[32,3584]{1,0:T(8,128)(2,1)S(1)}, bf16[32,3584]{1,0:T(8,128)(2,1)S(1)}, u32[]{:S(2)}, u32[]{:S(2)}) collective-permute-start(bf16[32,3584]{1,0:T(8,128)(2,1)S(1)} %scope_far1.1), channel_id=1, source_target_pairs={{0,2},{1,3},{2,0},{3,1},{4,6},{5,7},{6,4},{7,5},{8,10},{9,11},{10,... | collective-permute-start | bytes 688136 | tf_op jit(solution)/shard_map/ppermute | solution.py:21
  36.5 0.0 collective-permute-done.10.refs_4_
  36.5 1.1 %collective-permute-done.11.refs_5_ = bf16[8,3584]{1,0:T(8,128)(2,1)S(1)} collective-permute-done((bf16[8,3584]{1,0:T(8,128)(2,1)S(1)}, bf16[8,3584]{1,0:T(8,128)(2,1)S(1)}, u32[]{:S(2)}, u32[]{:S(2)}) %collective-permute-start.11) | collective-permute-done | bytes 57376 | tf_op jit(solution)/shard_map/ppermute | solution.py:21
  37.7 0.7 %collective-permute-done.9.refs_3_.refs_6_ = bf16[16,3584]{1,0:T(8,128)(2,1)S(1)} collective-permute-done((bf16[16,3584]{1,0:T(8,128)(2,1)S(1)}, bf16[16,3584]{1,0:T(8,128)(2,1)S(1)}, u32[]{:S(2)}, u32[]{:S(2)}) %collective-permute-start.9) | collective-permute-done | bytes 114720 | tf_op jit(solution)/shard_map/ppermute | solution.py:21
  38.4 0.3 scope_fold.1
  38.7 1.5 %collective-permute-start.12 = (bf16[32,3584]{1,0:T(8,128)(2,1)S(1)}, bf16[32,3584]{1,0:T(8,128)(2,1)S(1)}, u32[]{:S(2)}, u32[]{:S(2)}) collective-permute-start(bf16[32,3584]{1,0:T(8,128)(2,1)S(1)} %scope_fold.1), channel_id=1, source_target_pairs={{0,2},{1,3},{2,0},{3,1},{4,6},{5,7},{6,4},{7,5},{8,10},{9,11},{10,... | collective-permute-start | bytes 688136 | tf_op jit(solution)/shard_map/ppermute | solution.py:21
  40.2 1.0 %collective-permute-start.16 = (bf16[8,3584]{1,0:T(8,128)(2,1)S(1)}, bf16[8,3584]{1,0:T(8,128)(2,1)S(1)}, u32[]{:S(2)}, u32[]{:S(2)}) collective-permute-start(bf16[8,3584]{1,0:T(8,128)(2,1)S(1)} %get-tuple-element.49), channel_id=1, source_target_pairs={{0,8},{4,12},{8,0},{12,4},{1,9},{5,13},{9,1},{13,5},{2,10},{6,14},... | collective-permute-start | bytes 172040 | tf_op jit(solution)/shard_map/ppermute | solution.py:21
  41.2 2.0 %collective-permute-start.17 = (bf16[8,3584]{1,0:T(8,128)(2,1)S(1)}, bf16[8,3584]{1,0:T(8,128)(2,1)S(1)}, u32[]{:S(2)}, u32[]{:S(2)}) collective-permute-start(bf16[8,3584]{1,0:T(8,128)(2,1)S(1)} %get-tuple-element.50), channel_id=1, source_target_pairs={{0,12},{4,8},{8,4},{12,0},{1,13},{5,9},{9,5},{13,1},{2,14},{6,10},... | collective-permute-start | bytes 172040 | tf_op jit(solution)/shard_map/ppermute | solution.py:21
  43.1 3.3 %collective-permute-done.15.refs_4_ = bf16[32,3584]{1,0:T(8,128)(2,1)S(1)} collective-permute-done((bf16[32,3584]{1,0:T(8,128)(2,1)S(1)}, bf16[32,3584]{1,0:T(8,128)(2,1)S(1)}, u32[]{:S(2)}, u32[]{:S(2)}) %collective-permute-start.15) | collective-permute-done | bytes 229408 | tf_op jit(solution)/shard_map/ppermute | solution.py:21
  46.5 0.7 %collective-permute-done.17.refs_8_ = bf16[8,3584]{1,0:T(8,128)(2,1)S(1)} collective-permute-done((bf16[8,3584]{1,0:T(8,128)(2,1)S(1)}, bf16[8,3584]{1,0:T(8,128)(2,1)S(1)}, u32[]{:S(2)}, u32[]{:S(2)}) %collective-permute-start.17) | collective-permute-done | bytes 57376 | tf_op jit(solution)/shard_map/ppermute | solution.py:21
  47.2 3.1 %collective-permute-done.12.refs_2_ = bf16[32,3584]{1,0:T(8,128)(2,1)S(1)} collective-permute-done((bf16[32,3584]{1,0:T(8,128)(2,1)S(1)}, bf16[32,3584]{1,0:T(8,128)(2,1)S(1)}, u32[]{:S(2)}, u32[]{:S(2)}) %collective-permute-start.12) | collective-permute-done | bytes 229408 | tf_op jit(solution)/shard_map/ppermute | solution.py:21
  50.2 1.2 %scope_final.1 = bf16[128,3584]{1,0:T(8,128)(2,1)} custom-call(f32[128,3584]{1,0:T(8,128)S(1)} %get-tuple-element.32.refs_0_, bf16[256,128]{1,0:T(8,128)(2,1)S(1)} %get-tuple-element.29.refs_0_.refs_1_, bf16[32,3584]{1,0:T(8,128)(2,1)S(1)} %collective-permute-done.12.refs_2_, bf16[64,3584]{1,0:T(8,128)(2,1)S(1)} %collective-permute-done.13.refs_3_, ...), custom_call_target="tpu_custom_call" | custom-call | flops 10000000000 | tf_op jit(solution)/shard_map/scope_final/pallas_call | solution.py:372
  (6 shorter events, 0.0 us)
Async XLA Ops:
  2.1 9.6 %collective-permute-start.3 = (bf16[32,3712]{1,0:T(8,128)(2,1)S(1)}, bf16[32,3712]{1,0:T(8,128)(2,1)S(1)}, u32[]{:S(2)}, u32[]{:S(2)}) collective-permute-start(bf16[32,3712]{1,0:T(8,128)(2,1)S(1)} %get-tuple-element.33.near_ref), channel_id=1, source_target_pairs={{0,2},{1,3},{2,0},{3,1},{4,6},{5,7},{6,4},{7,5},{8,10},{9,11},{10,... | collective-permute-start | bytes 712712 | tf_op jit(solution)/shard_map/ppermute | solution.py:21
  5.1 1.5 %copy-start = (bf16[3584,256]{1,0:T(8,128)(2,1)S(1)}, bf16[3584,256]{1,0:T(8,128)(2,1)}, u32[]{:S(2)}) copy-start(bf16[3584,256]{1,0:T(8,128)(2,1)} %sg_hbm.1) | copy-start | bytes 5505028
  5.1 2.0 %copy-start.1 = (bf16[3584,256]{1,0:T(8,128)(2,1)S(1)}, bf16[3584,256]{1,0:T(8,128)(2,1)}, u32[]{:S(2)}) copy-start(bf16[3584,256]{1,0:T(8,128)(2,1)} %su_hbm.1) | copy-start | bytes 5505028
  5.1 2.6 %copy-start.2 = (bf16[256,3584]{1,0:T(8,128)(2,1)S(1)}, bf16[256,3584]{1,0:T(8,128)(2,1)}, u32[]{:S(2)}) copy-start(bf16[256,3584]{1,0:T(8,128)(2,1)} %sd_hbm.1) | copy-start | bytes 5505028
  5.5 17.7 %collective-permute-start.4 = (bf16[64,3584]{1,0:T(8,128)(2,1)S(1)}, bf16[64,3584]{1,0:T(8,128)(2,1)S(1)}, u32[]{:S(2)}, u32[]{:S(2)}) collective-permute-start(bf16[64,3584]{1,0:T(8,128)(2,1)S(1)} %get-tuple-element.34), channel_id=1, source_target_pairs={{0,2},{1,3},{2,0},{3,1},{4,6},{5,7},{6,4},{7,5},{8,10},{9,11},{10,... | collective-permute-start | bytes 1376264 | tf_op jit(solution)/shard_map/ppermute | solution.py:21
  6.6 5.4 %collective-permute-start = (bf16[3584,256]{1,0:T(8,128)(2,1)S(1)}, bf16[3584,256]{1,0:T(8,128)(2,1)S(1)}, u32[]{:S(2)}, u32[]{:S(2)}) collective-permute-start(bf16[3584,256]{1,0:T(8,128)(2,1)S(1)} %copy-done), channel_id=1, source_target_pairs={{0,1},{1,0},{2,3},{3,2},{4,5},{5,4},{6,7},{7,6},{8,9},{9,8},{10,11... | collective-permute-start | bytes 5505032 | tf_op jit(solution)/shard_map/ppermute | solution.py:21
  7.1 7.1 %collective-permute-start.1 = (bf16[3584,256]{1,0:T(8,128)(2,1)S(1)}, bf16[3584,256]{1,0:T(8,128)(2,1)S(1)}, u32[]{:S(2)}, u32[]{:S(2)}) collective-permute-start(bf16[3584,256]{1,0:T(8,128)(2,1)S(1)} %copy-done.1), channel_id=1, source_target_pairs={{0,1},{1,0},{2,3},{3,2},{4,5},{5,4},{6,7},{7,6},{8,9},{9,8},{10,11... | collective-permute-start | bytes 5505032 | tf_op jit(solution)/shard_map/ppermute | solution.py:21
  7.7 9.1 %collective-permute-start.2 = (bf16[256,3584]{1,0:T(8,128)(2,1)S(1)}, bf16[256,3584]{1,0:T(8,128)(2,1)S(1)}, u32[]{:S(2)}, u32[]{:S(2)}) collective-permute-start(bf16[256,3584]{1,0:T(8,128)(2,1)S(1)} %copy-done.2), channel_id=1, source_target_pairs={{0,1},{1,0},{2,3},{3,2},{4,5},{5,4},{6,7},{7,6},{8,9},{9,8},{10,11... | collective-permute-start | bytes 5505032 | tf_op jit(solution)/shard_map/ppermute | solution.py:21
  11.7 15.6 %collective-permute-start.8 = (bf16[10752,256]{1,0:T(8,128)(2,1)S(1)}, bf16[10752,256]{1,0:T(8,128)(2,1)S(1)}, u32[]{:S(2)}, u32[]{:S(2)}) collective-permute-start(bf16[10752,256]{1,0:T(8,128)(2,1)S(1)} %scope_load.1.refs_4_), channel_id=1, source_target_pairs={{0,1},{1,0},{2,3},{3,2},{4,5},{5,4},{6,7},{7,6},{8,9},{9,8},{10,11... | collective-permute-start | bytes 16515080 | tf_op jit(solution)/shard_map/ppermute | solution.py:21
  12.0 14.2 %collective-permute-start.5 = (bf16[16,3584]{1,0:T(8,128)(2,1)S(1)}, bf16[16,3584]{1,0:T(8,128)(2,1)S(1)}, u32[]{:S(2)}, u32[]{:S(2)}) collective-permute-start(bf16[16,3584]{1,0:T(8,128)(2,1)S(1)} %get-tuple-element.40), channel_id=1, source_target_pairs={{0,4},{4,0},{8,12},{12,8},{1,5},{5,1},{9,13},{13,9},{2,6},{6,2},{1... | collective-permute-start | bytes 344072 | tf_op jit(solution)/shard_map/ppermute | solution.py:21
  14.2 13.1 %collective-permute-start.6 = (bf16[16,3584]{1,0:T(8,128)(2,1)S(1)}, bf16[16,3584]{1,0:T(8,128)(2,1)S(1)}, u32[]{:S(2)}, u32[]{:S(2)}) collective-permute-start(bf16[16,3584]{1,0:T(8,128)(2,1)S(1)} %get-tuple-element.41), channel_id=1, source_target_pairs={{0,8},{4,12},{8,0},{12,4},{1,9},{5,13},{9,1},{13,5},{2,10},{6,14},... | collective-permute-start | bytes 344072 | tf_op jit(solution)/shard_map/ppermute | solution.py:21
  16.8 10.5 %collective-permute-start.7 = (bf16[16,3584]{1,0:T(8,128)(2,1)S(1)}, bf16[16,3584]{1,0:T(8,128)(2,1)S(1)}, u32[]{:S(2)}, u32[]{:S(2)}) collective-permute-start(bf16[16,3584]{1,0:T(8,128)(2,1)S(1)} %get-tuple-element.42), channel_id=1, source_target_pairs={{0,12},{4,8},{8,4},{12,0},{1,13},{5,9},{9,5},{13,1},{2,14},{6,10},... | collective-permute-start | bytes 344072 | tf_op jit(solution)/shard_map/ppermute | solution.py:21
  23.1 9.8 %collective-permute-start.14 = (bf16[32,3584]{1,0:T(8,128)(2,1)S(1)}, bf16[32,3584]{1,0:T(8,128)(2,1)S(1)}, u32[]{:S(2)}, u32[]{:S(2)}) collective-permute-start(bf16[32,3584]{1,0:T(8,128)(2,1)S(1)} %scope_last.1), channel_id=1, source_target_pairs={{0,2},{1,3},{2,0},{3,1},{4,6},{5,7},{6,4},{7,5},{8,10},{9,11},{10,... | collective-permute-start | bytes 688136 | tf_op jit(solution)/shard_map/ppermute | solution.py:21
  26.2 20.3 %collective-permute-start.13 = (bf16[64,3584]{1,0:T(8,128)(2,1)S(1)}, bf16[64,3584]{1,0:T(8,128)(2,1)S(1)}, u32[]{:S(2)}, u32[]{:S(2)}) collective-permute-start(bf16[64,3584]{1,0:T(8,128)(2,1)S(1)} %get-tuple-element.47), channel_id=1, source_target_pairs={{0,2},{1,3},{2,0},{3,1},{4,6},{5,7},{6,4},{7,5},{8,10},{9,11},{10,... | collective-permute-start | bytes 1376264 | tf_op jit(solution)/shard_map/ppermute | solution.py:21
  29.4 7.1 %collective-permute-start.10 = (bf16[8,3584]{1,0:T(8,128)(2,1)S(1)}, bf16[8,3584]{1,0:T(8,128)(2,1)S(1)}, u32[]{:S(2)}, u32[]{:S(2)}) collective-permute-start(bf16[8,3584]{1,0:T(8,128)(2,1)S(1)} %get-tuple-element.45), channel_id=1, source_target_pairs={{0,8},{4,12},{8,0},{12,4},{1,9},{5,13},{9,1},{13,5},{2,10},{6,14},... | collective-permute-start | bytes 172040 | tf_op jit(solution)/shard_map/ppermute | solution.py:21
  31.6 6.1 %collective-permute-start.11 = (bf16[8,3584]{1,0:T(8,128)(2,1)S(1)}, bf16[8,3584]{1,0:T(8,128)(2,1)S(1)}, u32[]{:S(2)}, u32[]{:S(2)}) collective-permute-start(bf16[8,3584]{1,0:T(8,128)(2,1)S(1)} %get-tuple-element.46), channel_id=1, source_target_pairs={{0,12},{4,8},{8,4},{12,0},{1,13},{5,9},{9,5},{13,1},{2,14},{6,10},... | collective-permute-start | bytes 172040 | tf_op jit(solution)/shard_map/ppermute | solution.py:21
  32.9 5.5 %collective-permute-start.9 = (bf16[16,3584]{1,0:T(8,128)(2,1)S(1)}, bf16[16,3584]{1,0:T(8,128)(2,1)S(1)}, u32[]{:S(2)}, u32[]{:S(2)}) collective-permute-start(bf16[16,3584]{1,0:T(8,128)(2,1)S(1)} %get-tuple-element.44), channel_id=1, source_target_pairs={{0,4},{4,0},{8,12},{12,8},{1,5},{5,1},{9,13},{13,9},{2,6},{6,2},{1... | collective-permute-start | bytes 344072 | tf_op jit(solution)/shard_map/ppermute | solution.py:21
  35.0 11.4 %collective-permute-start.15 = (bf16[32,3584]{1,0:T(8,128)(2,1)S(1)}, bf16[32,3584]{1,0:T(8,128)(2,1)S(1)}, u32[]{:S(2)}, u32[]{:S(2)}) collective-permute-start(bf16[32,3584]{1,0:T(8,128)(2,1)S(1)} %scope_far1.1), channel_id=1, source_target_pairs={{0,2},{1,3},{2,0},{3,1},{4,6},{5,7},{6,4},{7,5},{8,10},{9,11},{10,... | collective-permute-start | bytes 688136 | tf_op jit(solution)/shard_map/ppermute | solution.py:21
  38.7 11.5 %collective-permute-start.12 = (bf16[32,3584]{1,0:T(8,128)(2,1)S(1)}, bf16[32,3584]{1,0:T(8,128)(2,1)S(1)}, u32[]{:S(2)}, u32[]{:S(2)}) collective-permute-start(bf16[32,3584]{1,0:T(8,128)(2,1)S(1)} %scope_fold.1), channel_id=1, source_target_pairs={{0,2},{1,3},{2,0},{3,1},{4,6},{5,7},{6,4},{7,5},{8,10},{9,11},{10,... | collective-permute-start | bytes 688136 | tf_op jit(solution)/shard_map/ppermute | solution.py:21
  40.2 6.3 %collective-permute-start.16 = (bf16[8,3584]{1,0:T(8,128)(2,1)S(1)}, bf16[8,3584]{1,0:T(8,128)(2,1)S(1)}, u32[]{:S(2)}, u32[]{:S(2)}) collective-permute-start(bf16[8,3584]{1,0:T(8,128)(2,1)S(1)} %get-tuple-element.49), channel_id=1, source_target_pairs={{0,8},{4,12},{8,0},{12,4},{1,9},{5,13},{9,1},{13,5},{2,10},{6,14},... | collective-permute-start | bytes 172040 | tf_op jit(solution)/shard_map/ppermute | solution.py:21
  41.2 6.0 %collective-permute-start.17 = (bf16[8,3584]{1,0:T(8,128)(2,1)S(1)}, bf16[8,3584]{1,0:T(8,128)(2,1)S(1)}, u32[]{:S(2)}, u32[]{:S(2)}) collective-permute-start(bf16[8,3584]{1,0:T(8,128)(2,1)S(1)} %get-tuple-element.50), channel_id=1, source_target_pairs={{0,12},{4,8},{8,4},{12,0},{1,13},{5,9},{9,5},{13,1},{2,14},{6,10},... | collective-permute-start | bytes 172040 | tf_op jit(solution)/shard_map/ppermute | solution.py:21

commit v5 on v4

--- a/solution.py
+++ b/solution.py
@@ -203,9 +203,12 @@
         copy.start()
     rows = tokens_ref[...]
     own_ref[...] = mlp(rows, gate, up, down)
-    for copy in copies:
-        copy.wait()
-    own_ref[...] += mlp(rows, sg, su, sd)
+    copies[0].wait()
+    v = dot(rows, sg[...])
+    copies[1].wait()
+    hidden = bf16(v / (1.0 + jnp.exp(-v)) * dot(rows, su[...]))
+    copies[2].wait()
+    own_ref[...] += dot(hidden, sd[...])
 
 
 def far_kernel(groups, *refs):
@@ -279,7 +282,7 @@
         limit=16 << 20,
     )
     far_first = shift(first, "local", 2)
-    cut = tail * 2 // 3 // 16 * 16
+    cut = tail * 4 // 6 // 16 * 16
     near, *rest = call(
         "tail",
         lambda *refs: tail_kernel(head, *refs),

time: 51.6 us -> 51.2 us (level)
  waiting for transfers between devices: 10.3 us -> 9.75 us
    ppermute x18, starting transfers between devices: 22 us -> 22.5 us  [shift(): return lax.ppermute(value, axis, [(i, i ^ mask) for i in range(size)])]
    ppermute x18, waiting for transfers between devices: 10.3 us -> 9.75 us  [shift(): return lax.ppermute(value, axis, [(i, i ^ mask) for i in range(size)])]
  transfers between devices with their start and end apart: 18 -> 18, of which waited for: 6 -> 6; matrix products, arithmetic and copies ran while one was open for 0% -> 0% of each run, Pallas kernels for 27% -> 26%
where the time goes in v5:
time: 51.2 us; the launch traced here: 51 us
  starting transfers between devices  22.5 us (44%)
  Pallas kernels  16.5 us (32%)
  waiting for transfers between devices  9.75 us (19%)
  local copies, waits for them, and re-layouts  2.09 us (4%)
    ppermute x18, starting transfers between devices, shift(): return lax.ppermute(value, axis, [(i, i ^ mask) for i in range(size)])  22.5 us
    pallas_call x10, Pallas kernels, call(): pl.pallas_call(kernel, name='scope_' + name, out_shape=outs, in_specs=spe...  15.3 us
    ppermute x18, waiting for transfers between devices, shift(): return lax.ppermute(value, axis, [(i, i ^ mask) for i in range(size)])  9.75 us
    unnamed x6, local copies, waits for them, and re-layouts  2.09 us
    pallas_call x1, Pallas kernels, per_device(): pl.pallas_call(lambda *refs: final_kernel(block, len(backs), *refs), name...  1.22 us
  transfers between devices with their start and end apart: 18, of which 6 were waited for; matrix products, arithmetic and copies ran while one was open for 0% of the time, Pallas kernels for 26%

profile of v5, /device:TPU:0, one launch (start us, length us, event | category | flops | bytes accessed | tf_op | source)
XLA Modules:
  0.0 51.0 jit_solution(6180419935284503365)
XLA Ops:
  0.0 2.0 %scope_head.1 = (bf16[32,3712]{1,0:T(8,128)(2,1)S(1)}, bf16[256,128]{1,0:T(8,128)(2,1)S(1)}, bf16[64,128]{1,0:T(8,128)(2,1)S(1)}, bf16[128,3584]{1,0:T(8,128)(2,1)S(1)}) custom-call(s32[4]{0:T(128)S(1)} %xor_multiply_fusion.refs_0_, s32[8,128]{1,0:T(8,128)} %bitcast.5, f32[8,128]{1,0:T(8,128)} %bitcast.6, bf16[128,3584]{1,0:T(8,128)(2,1)} %refs_3_.1), custom_call_target="tpu_custom_call" | custom-call | flops 100000000 | tf_op jit(solution)/shard_map/scope_head/pallas_call | solution.py:54
  2.1 3.0 %collective-permute-start.3 = (bf16[32,3712]{1,0:T(8,128)(2,1)S(1)}, bf16[32,3712]{1,0:T(8,128)(2,1)S(1)}, u32[]{:S(2)}, u32[]{:S(2)}) collective-permute-start(bf16[32,3712]{1,0:T(8,128)(2,1)S(1)} %get-tuple-element.33.near_ref), channel_id=1, source_target_pairs={{0,2},{1,3},{2,0},{3,1},{4,6},{5,7},{6,4},{7,5},{8,10},{9,11},{10,... | collective-permute-start | bytes 712712 | tf_op jit(solution)/shard_map/ppermute | solution.py:21
  5.1 0.4 scope_tail.1
  5.5 0.1 collective-permute-start.4
  5.6 1.0 %copy-done = bf16[3584,256]{1,0:T(8,128)(2,1)S(1)} copy-done((bf16[3584,256]{1,0:T(8,128)(2,1)S(1)}, bf16[3584,256]{1,0:T(8,128)(2,1)}, u32[]{:S(2)}) %copy-start) | copy-done | bytes 1835032
  6.6 0.0 collective-permute-start
  6.6 0.5 %copy-done.1 = bf16[3584,256]{1,0:T(8,128)(2,1)S(1)} copy-done((bf16[3584,256]{1,0:T(8,128)(2,1)S(1)}, bf16[3584,256]{1,0:T(8,128)(2,1)}, u32[]{:S(2)}) %copy-start.1) | copy-done | bytes 1835032
  7.1 0.0 collective-permute-start.1
  7.1 0.6 %copy-done.2 = bf16[256,3584]{1,0:T(8,128)(2,1)S(1)} copy-done((bf16[256,3584]{1,0:T(8,128)(2,1)S(1)}, bf16[256,3584]{1,0:T(8,128)(2,1)}, u32[]{:S(2)}) %copy-start.2) | copy-done | bytes 1835032
  7.7 0.0 collective-permute-start.2
  7.7 2.7 %scope_load.1.refs_4_ = bf16[10752,256]{1,0:T(8,128)(2,1)S(1)} custom-call(bf16[3584,256]{1,0:T(8,128)(2,1)} %bitcast.7, bf16[3584,256]{1,0:T(8,128)(2,1)} %bitcast.8, bf16[256,3584]{1,0:T(8,128)(2,1)} %bitcast.9, bf16[32,3712]{1,0:T(8,128)(2,1)S(1)} %get-tuple-element.33.near_ref), custom_call_target="tpu_custom_call" | custom-call | flops 30000001024 | tf_op jit(solution)/shard_map/scope_load/pallas_call | solution.py:54
  10.4 1.3 %collective-permute-done.3.refs_0_.refs_1_ = bf16[32,3712]{1,0:T(8,128)(2,1)S(1)} collective-permute-done((bf16[32,3712]{1,0:T(8,128)(2,1)S(1)}, bf16[32,3712]{1,0:T(8,128)(2,1)S(1)}, u32[]{:S(2)}, u32[]{:S(2)}) %collective-permute-start.3) | collective-permute-done | bytes 237600 | tf_op jit(solution)/shard_map/ppermute | solution.py:21
  11.7 0.0 collective-permute-start.8
  11.7 0.3 scope_join.1
  12.0 0.0 collective-permute-done.gate.refs_2_.refs_1_
  12.0 2.2 %collective-permute-start.5 = (bf16[16,3584]{1,0:T(8,128)(2,1)S(1)}, bf16[16,3584]{1,0:T(8,128)(2,1)S(1)}, u32[]{:S(2)}, u32[]{:S(2)}) collective-permute-start(bf16[16,3584]{1,0:T(8,128)(2,1)S(1)} %get-tuple-element.40), channel_id=1, source_target_pairs={{0,4},{4,0},{8,12},{12,8},{1,5},{5,1},{9,13},{13,9},{2,6},{6,2},{1... | collective-permute-start | bytes 344072 | tf_op jit(solution)/shard_map/ppermute | solution.py:21
  14.2 0.0 collective-permute-done.1.up.refs_3_.refs_2_
  14.2 2.6 %collective-permute-start.6 = (bf16[16,3584]{1,0:T(8,128)(2,1)S(1)}, bf16[16,3584]{1,0:T(8,128)(2,1)S(1)}, u32[]{:S(2)}, u32[]{:S(2)}) collective-permute-start(bf16[16,3584]{1,0:T(8,128)(2,1)S(1)} %get-tuple-element.41), channel_id=1, source_target_pairs={{0,8},{4,12},{8,0},{12,4},{1,9},{5,13},{9,1},{13,5},{2,10},{6,14},... | collective-permute-start | bytes 344072 | tf_op jit(solution)/shard_map/ppermute | solution.py:21
  16.8 0.0 collective-permute-done.2.down.refs_4_.refs_3_
  16.8 2.4 %collective-permute-start.7 = (bf16[16,3584]{1,0:T(8,128)(2,1)S(1)}, bf16[16,3584]{1,0:T(8,128)(2,1)S(1)}, u32[]{:S(2)}, u32[]{:S(2)}) collective-permute-start(bf16[16,3584]{1,0:T(8,128)(2,1)S(1)} %get-tuple-element.42), channel_id=1, source_target_pairs={{0,12},{4,8},{8,4},{12,0},{1,13},{5,9},{9,5},{13,1},{2,14},{6,10},... | collective-permute-start | bytes 344072 | tf_op jit(solution)/shard_map/ppermute | solution.py:21
  19.2 0.2 scope_last.1
  19.5 3.2 %scope_own.1 = (f32[128,3584]{1,0:T(8,128)S(1)}, bf16[3584,256]{1,0:T(8,128)(2,1)S(1)}, bf16[3584,256]{1,0:T(8,128)(2,1)S(1)}, bf16[256,3584]{1,0:T(8,128)(2,1)S(1)}) custom-call(bf16[128,3584]{1,0:T(8,128)(2,1)S(1)} %get-tuple-element.28.refs_2_.tokens_ref.refs_1_, bf16[3584,256]{1,0:T(8,128)(2,1)S(1)} %collective-permute-done.gate.refs_2_.refs_1_, ...), custom_call_target="tpu_custom_call" | custom-call | flops 100000000 | tf_op jit(solution)/shard_map/scope_own/pallas_call | solution.py:54
  22.7 0.0 collective-permute-done.4.refs_1_
  22.7 1.1 %collective-permute-start.14 = (bf16[32,3584]{1,0:T(8,128)(2,1)S(1)}, bf16[32,3584]{1,0:T(8,128)(2,1)S(1)}, u32[]{:S(2)}, u32[]{:S(2)}) collective-permute-start(bf16[32,3584]{1,0:T(8,128)(2,1)S(1)} %scope_last.1), channel_id=1, source_target_pairs={{0,2},{1,3},{2,0},{3,1},{4,6},{5,7},{6,4},{7,5},{8,10},{9,11},{10,... | collective-permute-start | bytes 688136 | tf_op jit(solution)/shard_map/ppermute | solution.py:21
  23.7 2.0 %scope_far0.1 = (f32[32,3584]{1,0:T(8,128)S(1)}, bf16[64,3584]{1,0:T(8,128)(2,1)S(1)}) custom-call(bf16[32,3712]{1,0:T(8,128)(2,1)S(1)} %collective-permute-done.3.refs_0_.refs_1_, bf16[64,3584]{1,0:T(8,128)(2,1)S(1)} %collective-permute-done.4.refs_1_, bf16[3584,256]{1,0:T(8,128)(2,1)S(1)} %collective-permute-done.gate.refs_2_.refs_1_, ...), custom_call_target="tpu_custom_call" | custom-call | flops 1 | tf_op jit(solution)/shard_map/scope_far0/pallas_call | solution.py:54
  25.7 0.0 collective-permute-done.5.refs_1_
  25.7 1.1 %collective-permute-start.13 = (bf16[64,3584]{1,0:T(8,128)(2,1)S(1)}, bf16[64,3584]{1,0:T(8,128)(2,1)S(1)}, u32[]{:S(2)}, u32[]{:S(2)}) collective-permute-start(bf16[64,3584]{1,0:T(8,128)(2,1)S(1)} %get-tuple-element.47), channel_id=1, source_target_pairs={{0,2},{1,3},{2,0},{3,1},{4,6},{5,7},{6,4},{7,5},{8,10},{9,11},{10,... | collective-permute-start | bytes 1376264 | tf_op jit(solution)/shard_map/ppermute | solution.py:21
  26.8 0.0 collective-permute-done.6.refs_2_
  26.8 0.0 collective-permute-done.7.refs_3_
  26.8 0.0 collective-permute-done.8.refs_5_
  26.8 2.1 %scope_expert.1 = (bf16[8,3584]{1,0:T(8,128)(2,1)S(1)}, bf16[8,3584]{1,0:T(8,128)(2,1)S(1)}, bf16[16,3584]{1,0:T(8,128)(2,1)S(1)}, bf16[8,3584]{1,0:T(8,128)(2,1...) custom-call(bf16[16,3584]{1,0:T(8,128)(2,1)S(1)} %get-tuple-element.39.refs_0_.refs_2_,, ...), custom_call_target="tpu_custom_call" | custom-call | flops 30000001024 | tf_op jit(solution)/shard_map/scope_expert/pallas_call | solution.py:54
  29.0 2.6 %collective-permute-start.10 = (bf16[8,3584]{1,0:T(8,128)(2,1)S(1)}, bf16[8,3584]{1,0:T(8,128)(2,1)S(1)}, u32[]{:S(2)}, u32[]{:S(2)}) collective-permute-start(bf16[8,3584]{1,0:T(8,128)(2,1)S(1)} %get-tuple-element.45), channel_id=1, source_target_pairs={{0,8},{4,12},{8,0},{12,4},{1,9},{5,13},{9,1},{13,5},{2,10},{6,14},... | collective-permute-start | bytes 172040 | tf_op jit(solution)/shard_map/ppermute | solution.py:21
  31.6 1.3 %collective-permute-start.11 = (bf16[8,3584]{1,0:T(8,128)(2,1)S(1)}, bf16[8,3584]{1,0:T(8,128)(2,1)S(1)}, u32[]{:S(2)}, u32[]{:S(2)}) collective-permute-start(bf16[8,3584]{1,0:T(8,128)(2,1)S(1)} %get-tuple-element.46), channel_id=1, source_target_pairs={{0,12},{4,8},{8,4},{12,0},{1,13},{5,9},{9,5},{13,1},{2,14},{6,10},... | collective-permute-start | bytes 172040 | tf_op jit(solution)/shard_map/ppermute | solution.py:21
  32.9 0.0 collective-permute-start.9
  32.9 2.1 %scope_far1.1 = bf16[32,3584]{1,0:T(8,128)(2,1)S(1)} custom-call(bf16[32,3584]{1,0:T(8,128)(2,1)S(1)} %collective-permute-done.14.refs_0_, bf16[3584,256]{1,0:T(8,128)(2,1)S(1)} %collective-permute-done.gate.refs_2_.refs_1_, bf16[3584,256]{1,0:T(8,128)(2,1)S(1)} %collective-permute-done.1.up.refs_3_.refs_2_, ...), custom_call_target="tpu_custom_call" | custom-call | flops 10000000000 | tf_op jit(solution)/shard_map/scope_far1/pallas_call | solution.py:54
  35.0 1.5 %collective-permute-start.15 = (bf16[32,3584]{1,0:T(8,128)(2,1)S(1)}, bf16[32,3584]{1,0:T(8,128)(2,1)S(1)}, u32[]{:S(2)}, u32[]{:S(2)}) collective-permute-start(bf16[32,3584]{1,0:T(8,128)(2,1)S(1)} %scope_far1.1), channel_id=1, source_target_pairs={{0,2},{1,3},{2,0},{3,1},{4,6},{5,7},{6,4},{7,5},{8,10},{9,11},{10,... | collective-permute-start | bytes 688136 | tf_op jit(solution)/shard_map/ppermute | solution.py:21
  36.5 1.1 %collective-permute-done.11.refs_5_ = bf16[8,3584]{1,0:T(8,128)(2,1)S(1)} collective-permute-done((bf16[8,3584]{1,0:T(8,128)(2,1)S(1)}, bf16[8,3584]{1,0:T(8,128)(2,1)S(1)}, u32[]{:S(2)}, u32[]{:S(2)}) %collective-permute-start.11) | collective-permute-done | bytes 57376 | tf_op jit(solution)/shard_map/ppermute | solution.py:21
  37.7 0.6 %collective-permute-done.9.refs_3_.refs_6_ = bf16[16,3584]{1,0:T(8,128)(2,1)S(1)} collective-permute-done((bf16[16,3584]{1,0:T(8,128)(2,1)S(1)}, bf16[16,3584]{1,0:T(8,128)(2,1)S(1)}, u32[]{:S(2)}, u32[]{:S(2)}) %collective-permute-start.9) | collective-permute-done | bytes 114720 | tf_op jit(solution)/shard_map/ppermute | solution.py:21
  38.3 0.3 scope_fold.1
  38.6 1.6 %collective-permute-start.12 = (bf16[32,3584]{1,0:T(8,128)(2,1)S(1)}, bf16[32,3584]{1,0:T(8,128)(2,1)S(1)}, u32[]{:S(2)}, u32[]{:S(2)}) collective-permute-start(bf16[32,3584]{1,0:T(8,128)(2,1)S(1)} %scope_fold.1), channel_id=1, source_target_pairs={{0,2},{1,3},{2,0},{3,1},{4,6},{5,7},{6,4},{7,5},{8,10},{9,11},{10,... | collective-permute-start | bytes 688136 | tf_op jit(solution)/shard_map/ppermute | solution.py:21
  40.2 1.0 %collective-permute-start.16 = (bf16[8,3584]{1,0:T(8,128)(2,1)S(1)}, bf16[8,3584]{1,0:T(8,128)(2,1)S(1)}, u32[]{:S(2)}, u32[]{:S(2)}) collective-permute-start(bf16[8,3584]{1,0:T(8,128)(2,1)S(1)} %get-tuple-element.49), channel_id=1, source_target_pairs={{0,8},{4,12},{8,0},{12,4},{1,9},{5,13},{9,1},{13,5},{2,10},{6,14},... | collective-permute-start | bytes 172040 | tf_op jit(solution)/shard_map/ppermute | solution.py:21
  41.2 1.9 %collective-permute-start.17 = (bf16[8,3584]{1,0:T(8,128)(2,1)S(1)}, bf16[8,3584]{1,0:T(8,128)(2,1)S(1)}, u32[]{:S(2)}, u32[]{:S(2)}) collective-permute-start(bf16[8,3584]{1,0:T(8,128)(2,1)S(1)} %get-tuple-element.50), channel_id=1, source_target_pairs={{0,12},{4,8},{8,4},{12,0},{1,13},{5,9},{9,5},{13,1},{2,14},{6,10},... | collective-permute-start | bytes 172040 | tf_op jit(solution)/shard_map/ppermute | solution.py:21
  43.1 2.8 %collective-permute-done.15.refs_4_ = bf16[32,3584]{1,0:T(8,128)(2,1)S(1)} collective-permute-done((bf16[32,3584]{1,0:T(8,128)(2,1)S(1)}, bf16[32,3584]{1,0:T(8,128)(2,1)S(1)}, u32[]{:S(2)}, u32[]{:S(2)}) %collective-permute-start.15) | collective-permute-done | bytes 229408 | tf_op jit(solution)/shard_map/ppermute | solution.py:21
  46.0 0.0 collective-permute-done.13.refs_3_
  46.0 0.0 collective-permute-done.16.refs_7_
  46.0 1.2 %collective-permute-done.17.refs_8_ = bf16[8,3584]{1,0:T(8,128)(2,1)S(1)} collective-permute-done((bf16[8,3584]{1,0:T(8,128)(2,1)S(1)}, bf16[8,3584]{1,0:T(8,128)(2,1)S(1)}, u32[]{:S(2)}, u32[]{:S(2)}) %collective-permute-start.17) | collective-permute-done | bytes 57376 | tf_op jit(solution)/shard_map/ppermute | solution.py:21
  47.2 2.6 %collective-permute-done.12.refs_2_ = bf16[32,3584]{1,0:T(8,128)(2,1)S(1)} collective-permute-done((bf16[32,3584]{1,0:T(8,128)(2,1)S(1)}, bf16[32,3584]{1,0:T(8,128)(2,1)S(1)}, u32[]{:S(2)}, u32[]{:S(2)}) %collective-permute-start.12) | collective-permute-done | bytes 229408 | tf_op jit(solution)/shard_map/ppermute | solution.py:21
  49.8 1.2 %scope_final.1 = bf16[128,3584]{1,0:T(8,128)(2,1)} custom-call(f32[128,3584]{1,0:T(8,128)S(1)} %get-tuple-element.32.refs_0_, bf16[256,128]{1,0:T(8,128)(2,1)S(1)} %get-tuple-element.29.refs_0_.refs_1_, bf16[32,3584]{1,0:T(8,128)(2,1)S(1)} %collective-permute-done.12.refs_2_, bf16[64,3584]{1,0:T(8,128)(2,1)S(1)} %collective-permute-done.13.refs_3_, ...), custom_call_target="tpu_custom_call" | custom-call | flops 10000000000 | tf_op jit(solution)/shard_map/scope_final/pallas_call | solution.py:375
  (6 shorter events, 0.0 us)
Async XLA Ops:
  2.1 9.6 %collective-permute-start.3 = (bf16[32,3712]{1,0:T(8,128)(2,1)S(1)}, bf16[32,3712]{1,0:T(8,128)(2,1)S(1)}, u32[]{:S(2)}, u32[]{:S(2)}) collective-permute-start(bf16[32,3712]{1,0:T(8,128)(2,1)S(1)} %get-tuple-element.33.near_ref), channel_id=1, source_target_pairs={{0,2},{1,3},{2,0},{3,1},{4,6},{5,7},{6,4},{7,5},{8,10},{9,11},{10,... | collective-permute-start | bytes 712712 | tf_op jit(solution)/shard_map/ppermute | solution.py:21
  5.1 1.5 %copy-start = (bf16[3584,256]{1,0:T(8,128)(2,1)S(1)}, bf16[3584,256]{1,0:T(8,128)(2,1)}, u32[]{:S(2)}) copy-start(bf16[3584,256]{1,0:T(8,128)(2,1)} %sg_hbm.1) | copy-start | bytes 5505028
  5.1 2.0 %copy-start.1 = (bf16[3584,256]{1,0:T(8,128)(2,1)S(1)}, bf16[3584,256]{1,0:T(8,128)(2,1)}, u32[]{:S(2)}) copy-start(bf16[3584,256]{1,0:T(8,128)(2,1)} %su_hbm.1) | copy-start | bytes 5505028
  5.1 2.6 %copy-start.2 = (bf16[256,3584]{1,0:T(8,128)(2,1)S(1)}, bf16[256,3584]{1,0:T(8,128)(2,1)}, u32[]{:S(2)}) copy-start(bf16[256,3584]{1,0:T(8,128)(2,1)} %sd_hbm.1) | copy-start | bytes 5505028
  5.5 17.2 %collective-permute-start.4 = (bf16[64,3584]{1,0:T(8,128)(2,1)S(1)}, bf16[64,3584]{1,0:T(8,128)(2,1)S(1)}, u32[]{:S(2)}, u32[]{:S(2)}) collective-permute-start(bf16[64,3584]{1,0:T(8,128)(2,1)S(1)} %get-tuple-element.34), channel_id=1, source_target_pairs={{0,2},{1,3},{2,0},{3,1},{4,6},{5,7},{6,4},{7,5},{8,10},{9,11},{10,... | collective-permute-start | bytes 1376264 | tf_op jit(solution)/shard_map/ppermute | solution.py:21
  6.6 5.4 %collective-permute-start = (bf16[3584,256]{1,0:T(8,128)(2,1)S(1)}, bf16[3584,256]{1,0:T(8,128)(2,1)S(1)}, u32[]{:S(2)}, u32[]{:S(2)}) collective-permute-start(bf16[3584,256]{1,0:T(8,128)(2,1)S(1)} %copy-done), channel_id=1, source_target_pairs={{0,1},{1,0},{2,3},{3,2},{4,5},{5,4},{6,7},{7,6},{8,9},{9,8},{10,11... | collective-permute-start | bytes 5505032 | tf_op jit(solution)/shard_map/ppermute | solution.py:21
  7.1 7.1 %collective-permute-start.1 = (bf16[3584,256]{1,0:T(8,128)(2,1)S(1)}, bf16[3584,256]{1,0:T(8,128)(2,1)S(1)}, u32[]{:S(2)}, u32[]{:S(2)}) collective-permute-start(bf16[3584,256]{1,0:T(8,128)(2,1)S(1)} %copy-done.1), channel_id=1, source_target_pairs={{0,1},{1,0},{2,3},{3,2},{4,5},{5,4},{6,7},{7,6},{8,9},{9,8},{10,11... | collective-permute-start | bytes 5505032 | tf_op jit(solution)/shard_map/ppermute | solution.py:21
  7.7 9.1 %collective-permute-start.2 = (bf16[256,3584]{1,0:T(8,128)(2,1)S(1)}, bf16[256,3584]{1,0:T(8,128)(2,1)S(1)}, u32[]{:S(2)}, u32[]{:S(2)}) collective-permute-start(bf16[256,3584]{1,0:T(8,128)(2,1)S(1)} %copy-done.2), channel_id=1, source_target_pairs={{0,1},{1,0},{2,3},{3,2},{4,5},{5,4},{6,7},{7,6},{8,9},{9,8},{10,11... | collective-permute-start | bytes 5505032 | tf_op jit(solution)/shard_map/ppermute | solution.py:21
  11.7 15.2 %collective-permute-start.8 = (bf16[10752,256]{1,0:T(8,128)(2,1)S(1)}, bf16[10752,256]{1,0:T(8,128)(2,1)S(1)}, u32[]{:S(2)}, u32[]{:S(2)}) collective-permute-start(bf16[10752,256]{1,0:T(8,128)(2,1)S(1)} %scope_load.1.refs_4_), channel_id=1, source_target_pairs={{0,1},{1,0},{2,3},{3,2},{4,5},{5,4},{6,7},{7,6},{8,9},{9,8},{10,11... | collective-permute-start | bytes 16515080 | tf_op jit(solution)/shard_map/ppermute | solution.py:21
  12.0 13.7 %collective-permute-start.5 = (bf16[16,3584]{1,0:T(8,128)(2,1)S(1)}, bf16[16,3584]{1,0:T(8,128)(2,1)S(1)}, u32[]{:S(2)}, u32[]{:S(2)}) collective-permute-start(bf16[16,3584]{1,0:T(8,128)(2,1)S(1)} %get-tuple-element.40), channel_id=1, source_target_pairs={{0,4},{4,0},{8,12},{12,8},{1,5},{5,1},{9,13},{13,9},{2,6},{6,2},{1... | collective-permute-start | bytes 344072 | tf_op jit(solution)/shard_map/ppermute | solution.py:21
  14.2 12.6 %collective-permute-start.6 = (bf16[16,3584]{1,0:T(8,128)(2,1)S(1)}, bf16[16,3584]{1,0:T(8,128)(2,1)S(1)}, u32[]{:S(2)}, u32[]{:S(2)}) collective-permute-start(bf16[16,3584]{1,0:T(8,128)(2,1)S(1)} %get-tuple-element.41), channel_id=1, source_target_pairs={{0,8},{4,12},{8,0},{12,4},{1,9},{5,13},{9,1},{13,5},{2,10},{6,14},... | collective-permute-start | bytes 344072 | tf_op jit(solution)/shard_map/ppermute | solution.py:21
  16.8 10.0 %collective-permute-start.7 = (bf16[16,3584]{1,0:T(8,128)(2,1)S(1)}, bf16[16,3584]{1,0:T(8,128)(2,1)S(1)}, u32[]{:S(2)}, u32[]{:S(2)}) collective-permute-start(bf16[16,3584]{1,0:T(8,128)(2,1)S(1)} %get-tuple-element.42), channel_id=1, source_target_pairs={{0,12},{4,8},{8,4},{12,0},{1,13},{5,9},{9,5},{13,1},{2,14},{6,10},... | collective-permute-start | bytes 344072 | tf_op jit(solution)/shard_map/ppermute | solution.py:21
  22.7 10.2 %collective-permute-start.14 = (bf16[32,3584]{1,0:T(8,128)(2,1)S(1)}, bf16[32,3584]{1,0:T(8,128)(2,1)S(1)}, u32[]{:S(2)}, u32[]{:S(2)}) collective-permute-start(bf16[32,3584]{1,0:T(8,128)(2,1)S(1)} %scope_last.1), channel_id=1, source_target_pairs={{0,2},{1,3},{2,0},{3,1},{4,6},{5,7},{6,4},{7,5},{8,10},{9,11},{10,... | collective-permute-start | bytes 688136 | tf_op jit(solution)/shard_map/ppermute | solution.py:21
  25.7 20.3 %collective-permute-start.13 = (bf16[64,3584]{1,0:T(8,128)(2,1)S(1)}, bf16[64,3584]{1,0:T(8,128)(2,1)S(1)}, u32[]{:S(2)}, u32[]{:S(2)}) collective-permute-start(bf16[64,3584]{1,0:T(8,128)(2,1)S(1)} %get-tuple-element.47), channel_id=1, source_target_pairs={{0,2},{1,3},{2,0},{3,1},{4,6},{5,7},{6,4},{7,5},{8,10},{9,11},{10,... | collective-permute-start | bytes 1376264 | tf_op jit(solution)/shard_map/ppermute | solution.py:21
  29.0 7.6 %collective-permute-start.10 = (bf16[8,3584]{1,0:T(8,128)(2,1)S(1)}, bf16[8,3584]{1,0:T(8,128)(2,1)S(1)}, u32[]{:S(2)}, u32[]{:S(2)}) collective-permute-start(bf16[8,3584]{1,0:T(8,128)(2,1)S(1)} %get-tuple-element.45), channel_id=1, source_target_pairs={{0,8},{4,12},{8,0},{12,4},{1,9},{5,13},{9,1},{13,5},{2,10},{6,14},... | collective-permute-start | bytes 172040 | tf_op jit(solution)/shard_map/ppermute | solution.py:21
  31.6 6.1 %collective-permute-start.11 = (bf16[8,3584]{1,0:T(8,128)(2,1)S(1)}, bf16[8,3584]{1,0:T(8,128)(2,1)S(1)}, u32[]{:S(2)}, u32[]{:S(2)}) collective-permute-start(bf16[8,3584]{1,0:T(8,128)(2,1)S(1)} %get-tuple-element.46), channel_id=1, source_target_pairs={{0,12},{4,8},{8,4},{12,0},{1,13},{5,9},{9,5},{13,1},{2,14},{6,10},... | collective-permute-start | bytes 172040 | tf_op jit(solution)/shard_map/ppermute | solution.py:21
  32.9 5.4 %collective-permute-start.9 = (bf16[16,3584]{1,0:T(8,128)(2,1)S(1)}, bf16[16,3584]{1,0:T(8,128)(2,1)S(1)}, u32[]{:S(2)}, u32[]{:S(2)}) collective-permute-start(bf16[16,3584]{1,0:T(8,128)(2,1)S(1)} %get-tuple-element.44), channel_id=1, source_target_pairs={{0,4},{4,0},{8,12},{12,8},{1,5},{5,1},{9,13},{13,9},{2,6},{6,2},{1... | collective-permute-start | bytes 344072 | tf_op jit(solution)/shard_map/ppermute | solution.py:21
  35.0 11.0 %collective-permute-start.15 = (bf16[32,3584]{1,0:T(8,128)(2,1)S(1)}, bf16[32,3584]{1,0:T(8,128)(2,1)S(1)}, u32[]{:S(2)}, u32[]{:S(2)}) collective-permute-start(bf16[32,3584]{1,0:T(8,128)(2,1)S(1)} %scope_far1.1), channel_id=1, source_target_pairs={{0,2},{1,3},{2,0},{3,1},{4,6},{5,7},{6,4},{7,5},{8,10},{9,11},{10,... | collective-permute-start | bytes 688136 | tf_op jit(solution)/shard_map/ppermute | solution.py:21
  38.6 11.2 %collective-permute-start.12 = (bf16[32,3584]{1,0:T(8,128)(2,1)S(1)}, bf16[32,3584]{1,0:T(8,128)(2,1)S(1)}, u32[]{:S(2)}, u32[]{:S(2)}) collective-permute-start(bf16[32,3584]{1,0:T(8,128)(2,1)S(1)} %scope_fold.1), channel_id=1, source_target_pairs={{0,2},{1,3},{2,0},{3,1},{4,6},{5,7},{6,4},{7,5},{8,10},{9,11},{10,... | collective-permute-start | bytes 688136 | tf_op jit(solution)/shard_map/ppermute | solution.py:21
  40.2 5.8 %collective-permute-start.16 = (bf16[8,3584]{1,0:T(8,128)(2,1)S(1)}, bf16[8,3584]{1,0:T(8,128)(2,1)S(1)}, u32[]{:S(2)}, u32[]{:S(2)}) collective-permute-start(bf16[8,3584]{1,0:T(8,128)(2,1)S(1)} %get-tuple-element.49), channel_id=1, source_target_pairs={{0,8},{4,12},{8,0},{12,4},{1,9},{5,13},{9,1},{13,5},{2,10},{6,14},... | collective-permute-start | bytes 172040 | tf_op jit(solution)/shard_map/ppermute | solution.py:21
  41.2 6.0 %collective-permute-start.17 = (bf16[8,3584]{1,0:T(8,128)(2,1)S(1)}, bf16[8,3584]{1,0:T(8,128)(2,1)S(1)}, u32[]{:S(2)}, u32[]{:S(2)}) collective-permute-start(bf16[8,3584]{1,0:T(8,128)(2,1)S(1)} %get-tuple-element.50), channel_id=1, source_target_pairs={{0,12},{4,8},{8,4},{12,0},{1,13},{5,9},{9,5},{13,1},{2,14},{6,10},... | collective-permute-start | bytes 172040 | tf_op jit(solution)/shard_map/ppermute | solution.py:21

commit v6 on v5

--- a/solution.py
+++ b/solution.py
@@ -149,7 +149,7 @@
     return dot(hidden, down[...])
 
 
-def load_kernel(gate_hbm, up_hbm, down_hbm, near_ref, pack_ref, sems):
+def load_kernel(gate_hbm, up_hbm, down_hbm, sg_hbm, near_ref, pack_ref, sg, sems):
     width, part = gate_hbm.shape
     copies = [(gate_hbm, 0), (up_hbm, width)]
     copies += [(down_hbm.at[:, i : i + part], 2 * width + i) for i in range(0, width, part)]
@@ -159,6 +159,7 @@
         )
         for i, (source, place) in enumerate(copies)
     ]
+    copies.append(pltpu.make_async_copy(sg_hbm, sg, sems.at[len(copies)]))
     for copy in copies:
         copy.start()
     for copy in copies:
@@ -195,20 +196,22 @@
 
 
 def own_kernel(
-    tokens_ref, gate, up, down, after_ref, sg_hbm, su_hbm, sd_hbm, own_ref, sg, su, sd, sems,
+    tokens_ref, gate, up, down, after_ref, sg, su_hbm, sd_hbm, own_ref, su, sd, sems
 ):
-    pairs = zip((sg_hbm, su_hbm, sd_hbm), (sg, su, sd))
-    copies = [pltpu.make_async_copy(a, b, sems.at[i]) for i, (a, b) in enumerate(pairs)]
+    copies = [
+        pltpu.make_async_copy(su_hbm, su, sems.at[0]),
+        pltpu.make_async_copy(sd_hbm, sd, sems.at[1]),
+    ]
     for copy in copies:
         copy.start()
     rows = tokens_ref[...]
-    own_ref[...] = mlp(rows, gate, up, down)
+    v = dot(rows, gate[...])
+    hidden = bf16(v / (1.0 + jnp.exp(-v)) * dot(rows, up[...]))
+    v = dot(rows, sg[...])
     copies[0].wait()
-    v = dot(rows, sg[...])
+    own_hidden = bf16(v / (1.0 + jnp.exp(-v)) * dot(rows, su[...]))
     copies[1].wait()
-    hidden = bf16(v / (1.0 + jnp.exp(-v)) * dot(rows, su[...]))
-    copies[2].wait()
-    own_ref[...] += dot(hidden, sd[...])
+    own_ref[...] = dot(hidden, down[...]) + dot(own_hidden, sd[...])
 
 
 def far_kernel(groups, *refs):
@@ -301,13 +304,13 @@
         room=8 * slots * width,
     )
     part = w_gate.shape[2]
-    pack = call(
+    pack, own_gate = call(
         "load",
         load_kernel,
-        struct(3 * width, part),
-        (w_gate[0], w_up[0], w_down[0], first),
-        specs=[HBM] * 3 + [VMEM],
-        scratch=[pltpu.SemaphoreType.DMA((2 + width // part,))],
+        [struct(3 * width, part), struct(*s_gate.shape)],
+        (w_gate[0], w_up[0], w_down[0], s_gate, first),
+        specs=[HBM] * 4 + [VMEM],
+        scratch=[pltpu.SemaphoreType.DMA((3 + width // part,))],
         limit=16 << 20,
     )
     far_pack = shift(pack, "local", 1)
@@ -324,15 +327,13 @@
     own, *mats = call(
         "own",
         own_kernel,
-        [
-            struct(count, width, jnp.float32),
-            *[struct(*w.shape) for w in shared_mats],
-        ],
-        (held, *shared_far, near, *shared_mats),
-        specs=[VMEM] * 5 + [HBM] * 3,
-        scratch=[pltpu.SemaphoreType.DMA((3,))],
+        [struct(count, width, jnp.float32)] + [struct(*w.shape) for w in shared_mats[1:]],
+        (held, *shared_far, near, own_gate, *shared_mats[1:]),
+        specs=[VMEM] * 6 + [HBM] * 2,
+        scratch=[pltpu.SemaphoreType.DMA((2,))],
         limit=16 << 20,
     )
+    mats = [own_gate, *mats]
     whole = [n == 1 and nodes <= FEW_NODES for n in range(nodes)]
     replied = call(
         "expert",

time: 51.2 us -> 51.7 us (level)
  Pallas kernels: 16.5 us -> 17.7 us
  starting transfers between devices: 22.5 us -> 21.8 us
    pallas_call x10, Pallas kernels: 15.3 us -> 16.5 us  [call(): pl.pallas_call(kernel, name='scope_' + name, out_shape=outs, in_specs=spe...]
    ppermute x18, starting transfers between devices: 22.5 us -> 21.8 us  [shift(): return lax.ppermute(value, axis, [(i, i ^ mask) for i in range(size)])]
  transfers between devices with their start and end apart: 18 -> 18, of which waited for: 6 -> 6; matrix products, arithmetic and copies ran while one was open for 0% -> 0% of each run, Pallas kernels for 26% -> 28%
where the time goes in v6:
time: 51.7 us; the launch traced here: 51.5 us
  starting transfers between devices  21.8 us (42%)
  Pallas kernels  17.7 us (34%)
  waiting for transfers between devices  9.79 us (19%)
  local copies, waits for them, and re-layouts  2.09 us (4%)
    ppermute x18, starting transfers between devices, shift(): return lax.ppermute(value, axis, [(i, i ^ mask) for i in range(size)])  21.8 us
    pallas_call x10, Pallas kernels, call(): pl.pallas_call(kernel, name='scope_' + name, out_shape=outs, in_specs=spe...  16.5 us
    ppermute x18, waiting for transfers between devices, shift(): return lax.ppermute(value, axis, [(i, i ^ mask) for i in range(size)])  9.79 us
    unnamed x6, local copies, waits for them, and re-layouts  2.09 us
    pallas_call x1, Pallas kernels, per_device(): pl.pallas_call(lambda *refs: final_kernel(block, len(backs), *refs), name...  1.22 us
  transfers between devices with their start and end apart: 18, of which 6 were waited for; matrix products, arithmetic and copies ran while one was open for 0% of the time, Pallas kernels for 28%

profile of v6, /device:TPU:0, one launch (start us, length us, event | category | flops | bytes accessed | tf_op | source)
XLA Modules:
  0.0 51.5 jit_solution(13763548770919548727)
XLA Ops:
  0.0 2.0 %scope_head.1 = (bf16[32,3712]{1,0:T(8,128)(2,1)S(1)}, bf16[256,128]{1,0:T(8,128)(2,1)S(1)}, bf16[64,128]{1,0:T(8,128)(2,1)S(1)}, bf16[128,3584]{1,0:T(8,128)(2,1)S(1)}) custom-call(s32[4]{0:T(128)S(1)} %xor_multiply_fusion.refs_0_, s32[8,128]{1,0:T(8,128)} %bitcast.5, f32[8,128]{1,0:T(8,128)} %bitcast.6, bf16[128,3584]{1,0:T(8,128)(2,1)} %refs_3_.1), custom_call_target="tpu_custom_call" | custom-call | flops 100000000 | tf_op jit(solution)/shard_map/scope_head/pallas_call | solution.py:54
  2.1 3.0 %collective-permute-start.3 = (bf16[32,3712]{1,0:T(8,128)(2,1)S(1)}, bf16[32,3712]{1,0:T(8,128)(2,1)S(1)}, u32[]{:S(2)}, u32[]{:S(2)}) collective-permute-start(bf16[32,3712]{1,0:T(8,128)(2,1)S(1)} %get-tuple-element.33.near_ref), channel_id=1, source_target_pairs={{0,2},{1,3},{2,0},{3,1},{4,6},{5,7},{6,4},{7,5},{8,10},{9,11},{10,... | collective-permute-start | bytes 712712 | tf_op jit(solution)/shard_map/ppermute | solution.py:21
  5.1 0.4 scope_tail.1
  5.5 0.1 collective-permute-start.4
  5.6 1.0 %copy-done.2 = bf16[3584,256]{1,0:T(8,128)(2,1)S(1)} copy-done((bf16[3584,256]{1,0:T(8,128)(2,1)S(1)}, bf16[3584,256]{1,0:T(8,128)(2,1)}, u32[]{:S(2)}) %copy-start.2) | copy-done | bytes 1835032
  6.6 0.0 collective-permute-start
  6.6 0.5 %copy-done = bf16[3584,256]{1,0:T(8,128)(2,1)S(1)} copy-done((bf16[3584,256]{1,0:T(8,128)(2,1)S(1)}, bf16[3584,256]{1,0:T(8,128)(2,1)}, u32[]{:S(2)}) %copy-start) | copy-done | bytes 1835032
  7.1 0.0 collective-permute-start.1
  7.1 0.6 %copy-done.1 = bf16[256,3584]{1,0:T(8,128)(2,1)S(1)} copy-done((bf16[256,3584]{1,0:T(8,128)(2,1)S(1)}, bf16[256,3584]{1,0:T(8,128)(2,1)}, u32[]{:S(2)}) %copy-start.1) | copy-done | bytes 1835032
  7.7 0.0 collective-permute-start.2
  7.7 3.3 %scope_load.1 = (bf16[10752,256]{1,0:T(8,128)(2,1)S(1)}, bf16[3584,256]{1,0:T(8,128)(2,1)S(1)}) custom-call(bf16[3584,256]{1,0:T(8,128)(2,1)} %bitcast.7, bf16[3584,256]{1,0:T(8,128)(2,1)} %bitcast.8, bf16[256,3584]{1,0:T(8,128)(2,1)} %bitcast.9, bf16[3584,256]{1,0:T(8,128)(2,1)} %sg_hbm.1, bf16[32,3712]{1,0:T(8,128)(2,1)S(1)} %get-tuple-element.33.near_ref), custom_call_target="tpu_custom_call" | custom-call | flops 30000001024 | tf_op jit(solution)/shard_map/scope_load/pallas_call | solution.py:54
  11.0 0.7 %collective-permute-done.3.refs_0_.refs_1_ = bf16[32,3712]{1,0:T(8,128)(2,1)S(1)} collective-permute-done((bf16[32,3712]{1,0:T(8,128)(2,1)S(1)}, bf16[32,3712]{1,0:T(8,128)(2,1)S(1)}, u32[]{:S(2)}, u32[]{:S(2)}) %collective-permute-start.3) | collective-permute-done | bytes 237600 | tf_op jit(solution)/shard_map/ppermute | solution.py:21
  11.7 0.0 collective-permute-start.8
  11.7 0.3 scope_join.1
  12.0 0.0 collective-permute-done.gate.refs_2_.refs_1_
  12.0 2.2 %collective-permute-start.5 = (bf16[16,3584]{1,0:T(8,128)(2,1)S(1)}, bf16[16,3584]{1,0:T(8,128)(2,1)S(1)}, u32[]{:S(2)}, u32[]{:S(2)}) collective-permute-start(bf16[16,3584]{1,0:T(8,128)(2,1)S(1)} %get-tuple-element.41), channel_id=1, source_target_pairs={{0,4},{4,0},{8,12},{12,8},{1,5},{5,1},{9,13},{13,9},{2,6},{6,2},{1... | collective-permute-start | bytes 344072 | tf_op jit(solution)/shard_map/ppermute | solution.py:21
  14.2 0.0 collective-permute-done.1.up.refs_3_.refs_2_
  14.2 2.6 %collective-permute-start.6 = (bf16[16,3584]{1,0:T(8,128)(2,1)S(1)}, bf16[16,3584]{1,0:T(8,128)(2,1)S(1)}, u32[]{:S(2)}, u32[]{:S(2)}) collective-permute-start(bf16[16,3584]{1,0:T(8,128)(2,1)S(1)} %get-tuple-element.42), channel_id=1, source_target_pairs={{0,8},{4,12},{8,0},{12,4},{1,9},{5,13},{9,1},{13,5},{2,10},{6,14},... | collective-permute-start | bytes 344072 | tf_op jit(solution)/shard_map/ppermute | solution.py:21
  16.8 0.0 collective-permute-done.2.down.refs_4_.refs_3_
  16.8 2.4 %collective-permute-start.7 = (bf16[16,3584]{1,0:T(8,128)(2,1)S(1)}, bf16[16,3584]{1,0:T(8,128)(2,1)S(1)}, u32[]{:S(2)}, u32[]{:S(2)}) collective-permute-start(bf16[16,3584]{1,0:T(8,128)(2,1)S(1)} %get-tuple-element.43), channel_id=1, source_target_pairs={{0,12},{4,8},{8,4},{12,0},{1,13},{5,9},{9,5},{13,1},{2,14},{6,10},... | collective-permute-start | bytes 344072 | tf_op jit(solution)/shard_map/ppermute | solution.py:21
  19.2 0.2 scope_last.1
  19.5 3.7 %scope_own.1 = (f32[128,3584]{1,0:T(8,128)S(1)}, bf16[3584,256]{1,0:T(8,128)(2,1)S(1)}, bf16[256,3584]{1,0:T(8,128)(2,1)S(1)}) custom-call(bf16[128,3584]{1,0:T(8,128)(2,1)S(1)} %get-tuple-element.29.refs_2_.tokens_ref.refs_1_, bf16[3584,256]{1,0:T(8,128)(2,1)S(1)} %collective-permute-done.gate.refs_2_.refs_1_, ...), custom_call_target="tpu_custom_call" | custom-call | flops 100000000 | tf_op jit(solution)/shard_map/scope_own/pallas_call | solution.py:54
  23.2 0.0 collective-permute-done.4.refs_1_
  23.2 1.1 %collective-permute-start.14 = (bf16[32,3584]{1,0:T(8,128)(2,1)S(1)}, bf16[32,3584]{1,0:T(8,128)(2,1)S(1)}, u32[]{:S(2)}, u32[]{:S(2)}) collective-permute-start(bf16[32,3584]{1,0:T(8,128)(2,1)S(1)} %scope_last.1), channel_id=1, source_target_pairs={{0,2},{1,3},{2,0},{3,1},{4,6},{5,7},{6,4},{7,5},{8,10},{9,11},{10,... | collective-permute-start | bytes 688136 | tf_op jit(solution)/shard_map/ppermute | solution.py:21
  24.3 2.0 %scope_far0.1 = (f32[32,3584]{1,0:T(8,128)S(1)}, bf16[64,3584]{1,0:T(8,128)(2,1)S(1)}) custom-call(bf16[32,3712]{1,0:T(8,128)(2,1)S(1)} %collective-permute-done.3.refs_0_.refs_1_, bf16[64,3584]{1,0:T(8,128)(2,1)S(1)} %collective-permute-done.4.refs_1_, bf16[3584,256]{1,0:T(8,128)(2,1)S(1)} %collective-permute-done.gate.refs_2_.refs_1_, ...), custom_call_target="tpu_custom_call" | custom-call | flops 1 | tf_op jit(solution)/shard_map/scope_far0/pallas_call | solution.py:54
  26.2 0.0 collective-permute-done.5.refs_1_
  26.3 1.1 %collective-permute-start.13 = (bf16[64,3584]{1,0:T(8,128)(2,1)S(1)}, bf16[64,3584]{1,0:T(8,128)(2,1)S(1)}, u32[]{:S(2)}, u32[]{:S(2)}) collective-permute-start(bf16[64,3584]{1,0:T(8,128)(2,1)S(1)} %get-tuple-element.49), channel_id=1, source_target_pairs={{0,2},{1,3},{2,0},{3,1},{4,6},{5,7},{6,4},{7,5},{8,10},{9,11},{10,... | collective-permute-start | bytes 1376264 | tf_op jit(solution)/shard_map/ppermute | solution.py:21
  27.3 0.0 collective-permute-done.6.refs_2_
  27.3 0.0 collective-permute-done.7.refs_3_
  27.4 2.1 %scope_expert.1 = (bf16[8,3584]{1,0:T(8,128)(2,1)S(1)}, bf16[8,3584]{1,0:T(8,128)(2,1)S(1)}, bf16[16,3584]{1,0:T(8,128)(2,1)S(1)}, bf16[8,3584]{1,0:T(8,128)(2,1...) custom-call(bf16[16,3584]{1,0:T(8,128)(2,1)S(1)} %get-tuple-element.40.refs_0_.refs_2_,, ...), custom_call_target="tpu_custom_call" | custom-call | flops 30000001024 | tf_op jit(solution)/shard_map/scope_expert/pallas_call | solution.py:54
  29.5 2.1 %collective-permute-start.10 = (bf16[8,3584]{1,0:T(8,128)(2,1)S(1)}, bf16[8,3584]{1,0:T(8,128)(2,1)S(1)}, u32[]{:S(2)}, u32[]{:S(2)}) collective-permute-start(bf16[8,3584]{1,0:T(8,128)(2,1)S(1)} %get-tuple-element.47), channel_id=1, source_target_pairs={{0,8},{4,12},{8,0},{12,4},{1,9},{5,13},{9,1},{13,5},{2,10},{6,14},... | collective-permute-start | bytes 172040 | tf_op jit(solution)/shard_map/ppermute | solution.py:21
  31.6 1.3 %collective-permute-start.11 = (bf16[8,3584]{1,0:T(8,128)(2,1)S(1)}, bf16[8,3584]{1,0:T(8,128)(2,1)S(1)}, u32[]{:S(2)}, u32[]{:S(2)}) collective-permute-start(bf16[8,3584]{1,0:T(8,128)(2,1)S(1)} %get-tuple-element.48), channel_id=1, source_target_pairs={{0,12},{4,8},{8,4},{12,0},{1,13},{5,9},{9,5},{13,1},{2,14},{6,10},... | collective-permute-start | bytes 172040 | tf_op jit(solution)/shard_map/ppermute | solution.py:21
  32.9 0.1 collective-permute-start.9
  33.0 0.0 collective-permute-done.14.refs_0_
  33.0 2.1 %scope_far1.1 = bf16[32,3584]{1,0:T(8,128)(2,1)S(1)} custom-call(bf16[32,3584]{1,0:T(8,128)(2,1)S(1)} %collective-permute-done.14.refs_0_, bf16[3584,256]{1,0:T(8,128)(2,1)S(1)} %collective-permute-done.gate.refs_2_.refs_1_, bf16[3584,256]{1,0:T(8,128)(2,1)S(1)} %collective-permute-done.1.up.refs_3_.refs_2_, ...), custom_call_target="tpu_custom_call" | custom-call | flops 10000000000 | tf_op jit(solution)/shard_map/scope_far1/pallas_call | solution.py:54
  35.1 1.4 %collective-permute-start.15 = (bf16[32,3584]{1,0:T(8,128)(2,1)S(1)}, bf16[32,3584]{1,0:T(8,128)(2,1)S(1)}, u32[]{:S(2)}, u32[]{:S(2)}) collective-permute-start(bf16[32,3584]{1,0:T(8,128)(2,1)S(1)} %scope_far1.1), channel_id=1, source_target_pairs={{0,2},{1,3},{2,0},{3,1},{4,6},{5,7},{6,4},{7,5},{8,10},{9,11},{10,... | collective-permute-start | bytes 688136 | tf_op jit(solution)/shard_map/ppermute | solution.py:21
  36.5 0.0 collective-permute-done.10.refs_4_
  36.5 1.1 %collective-permute-done.11.refs_5_ = bf16[8,3584]{1,0:T(8,128)(2,1)S(1)} collective-permute-done((bf16[8,3584]{1,0:T(8,128)(2,1)S(1)}, bf16[8,3584]{1,0:T(8,128)(2,1)S(1)}, u32[]{:S(2)}, u32[]{:S(2)}) %collective-permute-start.11) | collective-permute-done | bytes 57376 | tf_op jit(solution)/shard_map/ppermute | solution.py:21
  37.7 0.8 %collective-permute-done.9.refs_3_.refs_6_ = bf16[16,3584]{1,0:T(8,128)(2,1)S(1)} collective-permute-done((bf16[16,3584]{1,0:T(8,128)(2,1)S(1)}, bf16[16,3584]{1,0:T(8,128)(2,1)S(1)}, u32[]{:S(2)}, u32[]{:S(2)}) %collective-permute-start.9) | collective-permute-done | bytes 114720 | tf_op jit(solution)/shard_map/ppermute | solution.py:21
  38.5 0.3 scope_fold.1
  38.8 1.4 %collective-permute-start.12 = (bf16[32,3584]{1,0:T(8,128)(2,1)S(1)}, bf16[32,3584]{1,0:T(8,128)(2,1)S(1)}, u32[]{:S(2)}, u32[]{:S(2)}) collective-permute-start(bf16[32,3584]{1,0:T(8,128)(2,1)S(1)} %scope_fold.1), channel_id=1, source_target_pairs={{0,2},{1,3},{2,0},{3,1},{4,6},{5,7},{6,4},{7,5},{8,10},{9,11},{10,... | collective-permute-start | bytes 688136 | tf_op jit(solution)/shard_map/ppermute | solution.py:21
  40.2 1.0 %collective-permute-start.16 = (bf16[8,3584]{1,0:T(8,128)(2,1)S(1)}, bf16[8,3584]{1,0:T(8,128)(2,1)S(1)}, u32[]{:S(2)}, u32[]{:S(2)}) collective-permute-start(bf16[8,3584]{1,0:T(8,128)(2,1)S(1)} %get-tuple-element.51), channel_id=1, source_target_pairs={{0,8},{4,12},{8,0},{12,4},{1,9},{5,13},{9,1},{13,5},{2,10},{6,14},... | collective-permute-start | bytes 172040 | tf_op jit(solution)/shard_map/ppermute | solution.py:21
  41.2 2.0 %collective-permute-start.17 = (bf16[8,3584]{1,0:T(8,128)(2,1)S(1)}, bf16[8,3584]{1,0:T(8,128)(2,1)S(1)}, u32[]{:S(2)}, u32[]{:S(2)}) collective-permute-start(bf16[8,3584]{1,0:T(8,128)(2,1)S(1)} %get-tuple-element.52), channel_id=1, source_target_pairs={{0,12},{4,8},{8,4},{12,0},{1,13},{5,9},{9,5},{13,1},{2,14},{6,10},... | collective-permute-start | bytes 172040 | tf_op jit(solution)/shard_map/ppermute | solution.py:21
  43.1 3.4 %collective-permute-done.15.refs_4_ = bf16[32,3584]{1,0:T(8,128)(2,1)S(1)} collective-permute-done((bf16[32,3584]{1,0:T(8,128)(2,1)S(1)}, bf16[32,3584]{1,0:T(8,128)(2,1)S(1)}, u32[]{:S(2)}, u32[]{:S(2)}) %collective-permute-start.15) | collective-permute-done | bytes 229408 | tf_op jit(solution)/shard_map/ppermute | solution.py:21
  46.5 0.0 collective-permute-done.13.refs_3_
  46.5 0.6 %collective-permute-done.17.refs_8_ = bf16[8,3584]{1,0:T(8,128)(2,1)S(1)} collective-permute-done((bf16[8,3584]{1,0:T(8,128)(2,1)S(1)}, bf16[8,3584]{1,0:T(8,128)(2,1)S(1)}, u32[]{:S(2)}, u32[]{:S(2)}) %collective-permute-start.17) | collective-permute-done | bytes 57376 | tf_op jit(solution)/shard_map/ppermute | solution.py:21
  47.2 3.1 %collective-permute-done.12.refs_2_ = bf16[32,3584]{1,0:T(8,128)(2,1)S(1)} collective-permute-done((bf16[32,3584]{1,0:T(8,128)(2,1)S(1)}, bf16[32,3584]{1,0:T(8,128)(2,1)S(1)}, u32[]{:S(2)}, u32[]{:S(2)}) %collective-permute-start.12) | collective-permute-done | bytes 229408 | tf_op jit(solution)/shard_map/ppermute | solution.py:21
  50.3 1.2 %scope_final.1 = bf16[128,3584]{1,0:T(8,128)(2,1)} custom-call(f32[128,3584]{1,0:T(8,128)S(1)} %get-tuple-element.35.refs_0_, bf16[256,128]{1,0:T(8,128)(2,1)S(1)} %get-tuple-element.30.refs_0_.refs_1_, bf16[32,3584]{1,0:T(8,128)(2,1)S(1)} %collective-permute-done.12.refs_2_, bf16[64,3584]{1,0:T(8,128)(2,1)S(1)} %collective-permute-done.13.refs_3_, ...), custom_call_target="tpu_custom_call" | custom-call | flops 10000000000 | tf_op jit(solution)/shard_map/scope_final/pallas_call | solution.py:376
  (6 shorter events, 0.0 us)
Async XLA Ops:
  2.1 9.6 %collective-permute-start.3 = (bf16[32,3712]{1,0:T(8,128)(2,1)S(1)}, bf16[32,3712]{1,0:T(8,128)(2,1)S(1)}, u32[]{:S(2)}, u32[]{:S(2)}) collective-permute-start(bf16[32,3712]{1,0:T(8,128)(2,1)S(1)} %get-tuple-element.33.near_ref), channel_id=1, source_target_pairs={{0,2},{1,3},{2,0},{3,1},{4,6},{5,7},{6,4},{7,5},{8,10},{9,11},{10,... | collective-permute-start | bytes 712712 | tf_op jit(solution)/shard_map/ppermute | solution.py:21
  5.1 1.5 %copy-start.2 = (bf16[3584,256]{1,0:T(8,128)(2,1)S(1)}, bf16[3584,256]{1,0:T(8,128)(2,1)}, u32[]{:S(2)}) copy-start(bf16[3584,256]{1,0:T(8,128)(2,1)} %sg_hbm.1) | copy-start | bytes 5505028
  5.1 2.0 %copy-start = (bf16[3584,256]{1,0:T(8,128)(2,1)S(1)}, bf16[3584,256]{1,0:T(8,128)(2,1)}, u32[]{:S(2)}) copy-start(bf16[3584,256]{1,0:T(8,128)(2,1)} %su_hbm.1) | copy-start | bytes 5505028
  5.1 2.6 %copy-start.1 = (bf16[256,3584]{1,0:T(8,128)(2,1)S(1)}, bf16[256,3584]{1,0:T(8,128)(2,1)}, u32[]{:S(2)}) copy-start(bf16[256,3584]{1,0:T(8,128)(2,1)} %sd_hbm.1) | copy-start | bytes 5505028
  5.5 17.7 %collective-permute-start.4 = (bf16[64,3584]{1,0:T(8,128)(2,1)S(1)}, bf16[64,3584]{1,0:T(8,128)(2,1)S(1)}, u32[]{:S(2)}, u32[]{:S(2)}) collective-permute-start(bf16[64,3584]{1,0:T(8,128)(2,1)S(1)} %get-tuple-element.36), channel_id=1, source_target_pairs={{0,2},{1,3},{2,0},{3,1},{4,6},{5,7},{6,4},{7,5},{8,10},{9,11},{10,... | collective-permute-start | bytes 1376264 | tf_op jit(solution)/shard_map/ppermute | solution.py:21
  6.6 5.4 %collective-permute-start = (bf16[3584,256]{1,0:T(8,128)(2,1)S(1)}, bf16[3584,256]{1,0:T(8,128)(2,1)S(1)}, u32[]{:S(2)}, u32[]{:S(2)}) collective-permute-start(bf16[3584,256]{1,0:T(8,128)(2,1)S(1)} %copy-done.2), channel_id=1, source_target_pairs={{0,1},{1,0},{2,3},{3,2},{4,5},{5,4},{6,7},{7,6},{8,9},{9,8},{10,11... | collective-permute-start | bytes 5505032 | tf_op jit(solution)/shard_map/ppermute | solution.py:21
  7.1 7.1 %collective-permute-start.1 = (bf16[3584,256]{1,0:T(8,128)(2,1)S(1)}, bf16[3584,256]{1,0:T(8,128)(2,1)S(1)}, u32[]{:S(2)}, u32[]{:S(2)}) collective-permute-start(bf16[3584,256]{1,0:T(8,128)(2,1)S(1)} %copy-done), channel_id=1, source_target_pairs={{0,1},{1,0},{2,3},{3,2},{4,5},{5,4},{6,7},{7,6},{8,9},{9,8},{10,11... | collective-permute-start | bytes 5505032 | tf_op jit(solution)/shard_map/ppermute | solution.py:21
  7.7 9.1 %collective-permute-start.2 = (bf16[256,3584]{1,0:T(8,128)(2,1)S(1)}, bf16[256,3584]{1,0:T(8,128)(2,1)S(1)}, u32[]{:S(2)}, u32[]{:S(2)}) collective-permute-start(bf16[256,3584]{1,0:T(8,128)(2,1)S(1)} %copy-done.1), channel_id=1, source_target_pairs={{0,1},{1,0},{2,3},{3,2},{4,5},{5,4},{6,7},{7,6},{8,9},{9,8},{10,11... | collective-permute-start | bytes 5505032 | tf_op jit(solution)/shard_map/ppermute | solution.py:21
  11.7 15.7 %collective-permute-start.8 = (bf16[10752,256]{1,0:T(8,128)(2,1)S(1)}, bf16[10752,256]{1,0:T(8,128)(2,1)S(1)}, u32[]{:S(2)}, u32[]{:S(2)}) collective-permute-start(bf16[10752,256]{1,0:T(8,128)(2,1)S(1)} %get-tuple-element.44.refs_4_), channel_id=1, source_target_pairs={{0,1},{1,0},{2,3},{3,2},{4,5},{5,4},{6,7},{7,6},{8,9},{9,8},{10,11... | collective-permute-start | bytes 16515080 | tf_op jit(solution)/shard_map/ppermute | solution.py:21
  12.0 14.2 %collective-permute-start.5 = (bf16[16,3584]{1,0:T(8,128)(2,1)S(1)}, bf16[16,3584]{1,0:T(8,128)(2,1)S(1)}, u32[]{:S(2)}, u32[]{:S(2)}) collective-permute-start(bf16[16,3584]{1,0:T(8,128)(2,1)S(1)} %get-tuple-element.41), channel_id=1, source_target_pairs={{0,4},{4,0},{8,12},{12,8},{1,5},{5,1},{9,13},{13,9},{2,6},{6,2},{1... | collective-permute-start | bytes 344072 | tf_op jit(solution)/shard_map/ppermute | solution.py:21
  14.2 13.1 %collective-permute-start.6 = (bf16[16,3584]{1,0:T(8,128)(2,1)S(1)}, bf16[16,3584]{1,0:T(8,128)(2,1)S(1)}, u32[]{:S(2)}, u32[]{:S(2)}) collective-permute-start(bf16[16,3584]{1,0:T(8,128)(2,1)S(1)} %get-tuple-element.42), channel_id=1, source_target_pairs={{0,8},{4,12},{8,0},{12,4},{1,9},{5,13},{9,1},{13,5},{2,10},{6,14},... | collective-permute-start | bytes 344072 | tf_op jit(solution)/shard_map/ppermute | solution.py:21
  16.8 10.5 %collective-permute-start.7 = (bf16[16,3584]{1,0:T(8,128)(2,1)S(1)}, bf16[16,3584]{1,0:T(8,128)(2,1)S(1)}, u32[]{:S(2)}, u32[]{:S(2)}) collective-permute-start(bf16[16,3584]{1,0:T(8,128)(2,1)S(1)} %get-tuple-element.43), channel_id=1, source_target_pairs={{0,12},{4,8},{8,4},{12,0},{1,13},{5,9},{9,5},{13,1},{2,14},{6,10},... | collective-permute-start | bytes 344072 | tf_op jit(solution)/shard_map/ppermute | solution.py:21
  23.2 9.8 %collective-permute-start.14 = (bf16[32,3584]{1,0:T(8,128)(2,1)S(1)}, bf16[32,3584]{1,0:T(8,128)(2,1)S(1)}, u32[]{:S(2)}, u32[]{:S(2)}) collective-permute-start(bf16[32,3584]{1,0:T(8,128)(2,1)S(1)} %scope_last.1), channel_id=1, source_target_pairs={{0,2},{1,3},{2,0},{3,1},{4,6},{5,7},{6,4},{7,5},{8,10},{9,11},{10,... | collective-permute-start | bytes 688136 | tf_op jit(solution)/shard_map/ppermute | solution.py:21
  26.3 20.3 %collective-permute-start.13 = (bf16[64,3584]{1,0:T(8,128)(2,1)S(1)}, bf16[64,3584]{1,0:T(8,128)(2,1)S(1)}, u32[]{:S(2)}, u32[]{:S(2)}) collective-permute-start(bf16[64,3584]{1,0:T(8,128)(2,1)S(1)} %get-tuple-element.49), channel_id=1, source_target_pairs={{0,2},{1,3},{2,0},{3,1},{4,6},{5,7},{6,4},{7,5},{8,10},{9,11},{10,... | collective-permute-start | bytes 1376264 | tf_op jit(solution)/shard_map/ppermute | solution.py:21
  29.5 7.1 %collective-permute-start.10 = (bf16[8,3584]{1,0:T(8,128)(2,1)S(1)}, bf16[8,3584]{1,0:T(8,128)(2,1)S(1)}, u32[]{:S(2)}, u32[]{:S(2)}) collective-permute-start(bf16[8,3584]{1,0:T(8,128)(2,1)S(1)} %get-tuple-element.47), channel_id=1, source_target_pairs={{0,8},{4,12},{8,0},{12,4},{1,9},{5,13},{9,1},{13,5},{2,10},{6,14},... | collective-permute-start | bytes 172040 | tf_op jit(solution)/shard_map/ppermute | solution.py:21
  31.6 6.1 %collective-permute-start.11 = (bf16[8,3584]{1,0:T(8,128)(2,1)S(1)}, bf16[8,3584]{1,0:T(8,128)(2,1)S(1)}, u32[]{:S(2)}, u32[]{:S(2)}) collective-permute-start(bf16[8,3584]{1,0:T(8,128)(2,1)S(1)} %get-tuple-element.48), channel_id=1, source_target_pairs={{0,12},{4,8},{8,4},{12,0},{1,13},{5,9},{9,5},{13,1},{2,14},{6,10},... | collective-permute-start | bytes 172040 | tf_op jit(solution)/shard_map/ppermute | solution.py:21
  32.9 5.6 %collective-permute-start.9 = (bf16[16,3584]{1,0:T(8,128)(2,1)S(1)}, bf16[16,3584]{1,0:T(8,128)(2,1)S(1)}, u32[]{:S(2)}, u32[]{:S(2)}) collective-permute-start(bf16[16,3584]{1,0:T(8,128)(2,1)S(1)} %get-tuple-element.46), channel_id=1, source_target_pairs={{0,4},{4,0},{8,12},{12,8},{1,5},{5,1},{9,13},{13,9},{2,6},{6,2},{1... | collective-permute-start | bytes 344072 | tf_op jit(solution)/shard_map/ppermute | solution.py:21
  35.1 11.4 %collective-permute-start.15 = (bf16[32,3584]{1,0:T(8,128)(2,1)S(1)}, bf16[32,3584]{1,0:T(8,128)(2,1)S(1)}, u32[]{:S(2)}, u32[]{:S(2)}) collective-permute-start(bf16[32,3584]{1,0:T(8,128)(2,1)S(1)} %scope_far1.1), channel_id=1, source_target_pairs={{0,2},{1,3},{2,0},{3,1},{4,6},{5,7},{6,4},{7,5},{8,10},{9,11},{10,... | collective-permute-start | bytes 688136 | tf_op jit(solution)/shard_map/ppermute | solution.py:21
  38.8 11.5 %collective-permute-start.12 = (bf16[32,3584]{1,0:T(8,128)(2,1)S(1)}, bf16[32,3584]{1,0:T(8,128)(2,1)S(1)}, u32[]{:S(2)}, u32[]{:S(2)}) collective-permute-start(bf16[32,3584]{1,0:T(8,128)(2,1)S(1)} %scope_fold.1), channel_id=1, source_target_pairs={{0,2},{1,3},{2,0},{3,1},{4,6},{5,7},{6,4},{7,5},{8,10},{9,11},{10,... | collective-permute-start | bytes 688136 | tf_op jit(solution)/shard_map/ppermute | solution.py:21
  40.2 6.4 %collective-permute-start.16 = (bf16[8,3584]{1,0:T(8,128)(2,1)S(1)}, bf16[8,3584]{1,0:T(8,128)(2,1)S(1)}, u32[]{:S(2)}, u32[]{:S(2)}) collective-permute-start(bf16[8,3584]{1,0:T(8,128)(2,1)S(1)} %get-tuple-element.51), channel_id=1, source_target_pairs={{0,8},{4,12},{8,0},{12,4},{1,9},{5,13},{9,1},{13,5},{2,10},{6,14},... | collective-permute-start | bytes 172040 | tf_op jit(solution)/shard_map/ppermute | solution.py:21
  41.2 6.0 %collective-permute-start.17 = (bf16[8,3584]{1,0:T(8,128)(2,1)S(1)}, bf16[8,3584]{1,0:T(8,128)(2,1)S(1)}, u32[]{:S(2)}, u32[]{:S(2)}) collective-permute-start(bf16[8,3584]{1,0:T(8,128)(2,1)S(1)} %get-tuple-element.52), channel_id=1, source_target_pairs={{0,12},{4,8},{8,4},{12,0},{1,13},{5,9},{9,5},{13,1},{2,14},{6,10},... | collective-permute-start | bytes 172040 | tf_op jit(solution)/shard_map/ppermute | solution.py:21

commit v7 on v6

--- a/solution.py
+++ b/solution.py
@@ -205,13 +205,12 @@
     for copy in copies:
         copy.start()
     rows = tokens_ref[...]
-    v = dot(rows, gate[...])
-    hidden = bf16(v / (1.0 + jnp.exp(-v)) * dot(rows, up[...]))
+    own_ref[...] = mlp(rows, gate, up, down)
     v = dot(rows, sg[...])
     copies[0].wait()
-    own_hidden = bf16(v / (1.0 + jnp.exp(-v)) * dot(rows, su[...]))
+    hidden = bf16(v / (1.0 + jnp.exp(-v)) * dot(rows, su[...]))
     copies[1].wait()
-    own_ref[...] = dot(hidden, down[...]) + dot(own_hidden, sd[...])
+    own_ref[...] += dot(hidden, sd[...])
 
 
 def far_kernel(groups, *refs):

time: 51.7 us -> 51 us (0.986)
  starting transfers between devices: 21.8 us -> 22.7 us
  waiting for transfers between devices: 9.79 us -> 8.95 us
  Pallas kernels: 17.7 us -> 17 us
    ppermute x18, waiting for transfers between devices: 9.79 us -> 8.95 us  [shift(): return lax.ppermute(value, axis, [(i, i ^ mask) for i in range(size)])]
    ppermute x18, starting transfers between devices: 21.8 us -> 22.7 us  [shift(): return lax.ppermute(value, axis, [(i, i ^ mask) for i in range(size)])]
    pallas_call x10, Pallas kernels: 16.5 us -> 15.8 us  [call(): pl.pallas_call(kernel, name='scope_' + name, out_shape=outs, in_specs=spe...]
  transfers between devices with their start and end apart: 18 -> 18, of which waited for: 6 -> 6; matrix products, arithmetic and copies ran while one was open for 0% -> 0% of each run, Pallas kernels for 28% -> 27%
where the time goes in v7:
time: 51 us; the launch traced here: 50.8 us
  starting transfers between devices  22.7 us (45%)
  Pallas kernels  17 us (33%)
  waiting for transfers between devices  8.95 us (18%)
  local copies, waits for them, and re-layouts  2.09 us (4%)
    ppermute x18, starting transfers between devices, shift(): return lax.ppermute(value, axis, [(i, i ^ mask) for i in range(size)])  22.7 us
    pallas_call x10, Pallas kernels, call(): pl.pallas_call(kernel, name='scope_' + name, out_shape=outs, in_specs=spe...  15.8 us
    ppermute x18, waiting for transfers between devices, shift(): return lax.ppermute(value, axis, [(i, i ^ mask) for i in range(size)])  8.95 us
    unnamed x6, local copies, waits for them, and re-layouts  2.09 us
    pallas_call x1, Pallas kernels, per_device(): pl.pallas_call(lambda *refs: final_kernel(block, len(backs), *refs), name...  1.22 us
  transfers between devices with their start and end apart: 18, of which 6 were waited for; matrix products, arithmetic and copies ran while one was open for 0% of the time, Pallas kernels for 27%

profile of v7, /device:TPU:0, one launch (start us, length us, event | category | flops | bytes accessed | tf_op | source)
XLA Modules:
  0.0 50.8 jit_solution(6084327638901455224)
XLA Ops:
  0.0 2.0 %scope_head.1 = (bf16[32,3712]{1,0:T(8,128)(2,1)S(1)}, bf16[256,128]{1,0:T(8,128)(2,1)S(1)}, bf16[64,128]{1,0:T(8,128)(2,1)S(1)}, bf16[128,3584]{1,0:T(8,128)(2,1)S(1)}) custom-call(s32[4]{0:T(128)S(1)} %xor_multiply_fusion.refs_0_, s32[8,128]{1,0:T(8,128)} %bitcast.5, f32[8,128]{1,0:T(8,128)} %bitcast.6, bf16[128,3584]{1,0:T(8,128)(2,1)} %refs_3_.1), custom_call_target="tpu_custom_call" | custom-call | flops 100000000 | tf_op jit(solution)/shard_map/scope_head/pallas_call | solution.py:54
  2.1 3.0 %collective-permute-start.3 = (bf16[32,3712]{1,0:T(8,128)(2,1)S(1)}, bf16[32,3712]{1,0:T(8,128)(2,1)S(1)}, u32[]{:S(2)}, u32[]{:S(2)}) collective-permute-start(bf16[32,3712]{1,0:T(8,128)(2,1)S(1)} %get-tuple-element.33.near_ref), channel_id=1, source_target_pairs={{0,2},{1,3},{2,0},{3,1},{4,6},{5,7},{6,4},{7,5},{8,10},{9,11},{10,... | collective-permute-start | bytes 712712 | tf_op jit(solution)/shard_map/ppermute | solution.py:21
  5.1 0.4 scope_tail.1
  5.5 0.1 collective-permute-start.4
  5.6 1.0 %copy-done.2 = bf16[3584,256]{1,0:T(8,128)(2,1)S(1)} copy-done((bf16[3584,256]{1,0:T(8,128)(2,1)S(1)}, bf16[3584,256]{1,0:T(8,128)(2,1)}, u32[]{:S(2)}) %copy-start.2) | copy-done | bytes 1835032
  6.6 0.0 collective-permute-start
  6.6 0.5 %copy-done = bf16[3584,256]{1,0:T(8,128)(2,1)S(1)} copy-done((bf16[3584,256]{1,0:T(8,128)(2,1)S(1)}, bf16[3584,256]{1,0:T(8,128)(2,1)}, u32[]{:S(2)}) %copy-start) | copy-done | bytes 1835032
  7.1 0.0 collective-permute-start.1
  7.1 0.6 %copy-done.1 = bf16[256,3584]{1,0:T(8,128)(2,1)S(1)} copy-done((bf16[256,3584]{1,0:T(8,128)(2,1)S(1)}, bf16[256,3584]{1,0:T(8,128)(2,1)}, u32[]{:S(2)}) %copy-start.1) | copy-done | bytes 1835032
  7.7 0.0 collective-permute-start.2
  7.7 3.3 %scope_load.1 = (bf16[10752,256]{1,0:T(8,128)(2,1)S(1)}, bf16[3584,256]{1,0:T(8,128)(2,1)S(1)}) custom-call(bf16[3584,256]{1,0:T(8,128)(2,1)} %bitcast.7, bf16[3584,256]{1,0:T(8,128)(2,1)} %bitcast.8, bf16[256,3584]{1,0:T(8,128)(2,1)} %bitcast.9, bf16[3584,256]{1,0:T(8,128)(2,1)} %sg_hbm.1, bf16[32,3712]{1,0:T(8,128)(2,1)S(1)} %get-tuple-element.33.near_ref), custom_call_target="tpu_custom_call" | custom-call | flops 30000001024 | tf_op jit(solution)/shard_map/scope_load/pallas_call | solution.py:54
  11.0 0.7 %collective-permute-done.3.refs_0_.refs_1_ = bf16[32,3712]{1,0:T(8,128)(2,1)S(1)} collective-permute-done((bf16[32,3712]{1,0:T(8,128)(2,1)S(1)}, bf16[32,3712]{1,0:T(8,128)(2,1)S(1)}, u32[]{:S(2)}, u32[]{:S(2)}) %collective-permute-start.3) | collective-permute-done | bytes 237600 | tf_op jit(solution)/shard_map/ppermute | solution.py:21
  11.7 0.0 collective-permute-start.8
  11.7 0.3 scope_join.1
  12.0 0.0 collective-permute-done.gate.refs_2_.refs_1_
  12.0 2.2 %collective-permute-start.5 = (bf16[16,3584]{1,0:T(8,128)(2,1)S(1)}, bf16[16,3584]{1,0:T(8,128)(2,1)S(1)}, u32[]{:S(2)}, u32[]{:S(2)}) collective-permute-start(bf16[16,3584]{1,0:T(8,128)(2,1)S(1)} %get-tuple-element.41), channel_id=1, source_target_pairs={{0,4},{4,0},{8,12},{12,8},{1,5},{5,1},{9,13},{13,9},{2,6},{6,2},{1... | collective-permute-start | bytes 344072 | tf_op jit(solution)/shard_map/ppermute | solution.py:21
  14.2 0.0 collective-permute-done.1.up.refs_3_.refs_2_
  14.2 2.6 %collective-permute-start.6 = (bf16[16,3584]{1,0:T(8,128)(2,1)S(1)}, bf16[16,3584]{1,0:T(8,128)(2,1)S(1)}, u32[]{:S(2)}, u32[]{:S(2)}) collective-permute-start(bf16[16,3584]{1,0:T(8,128)(2,1)S(1)} %get-tuple-element.42), channel_id=1, source_target_pairs={{0,8},{4,12},{8,0},{12,4},{1,9},{5,13},{9,1},{13,5},{2,10},{6,14},... | collective-permute-start | bytes 344072 | tf_op jit(solution)/shard_map/ppermute | solution.py:21
  16.8 0.0 collective-permute-done.2.down.refs_4_.refs_3_
  16.8 2.4 %collective-permute-start.7 = (bf16[16,3584]{1,0:T(8,128)(2,1)S(1)}, bf16[16,3584]{1,0:T(8,128)(2,1)S(1)}, u32[]{:S(2)}, u32[]{:S(2)}) collective-permute-start(bf16[16,3584]{1,0:T(8,128)(2,1)S(1)} %get-tuple-element.43), channel_id=1, source_target_pairs={{0,12},{4,8},{8,4},{12,0},{1,13},{5,9},{9,5},{13,1},{2,14},{6,10},... | collective-permute-start | bytes 344072 | tf_op jit(solution)/shard_map/ppermute | solution.py:21
  19.2 0.2 scope_last.1
  19.5 3.1 %scope_own.1 = (f32[128,3584]{1,0:T(8,128)S(1)}, bf16[3584,256]{1,0:T(8,128)(2,1)S(1)}, bf16[256,3584]{1,0:T(8,128)(2,1)S(1)}) custom-call(bf16[128,3584]{1,0:T(8,128)(2,1)S(1)} %get-tuple-element.29.refs_2_.tokens_ref.refs_1_, bf16[3584,256]{1,0:T(8,128)(2,1)S(1)} %collective-permute-done.gate.refs_2_.refs_1_, ...), custom_call_target="tpu_custom_call" | custom-call | flops 100000000 | tf_op jit(solution)/shard_map/scope_own/pallas_call | solution.py:54
  22.5 1.1 %collective-permute-start.14 = (bf16[32,3584]{1,0:T(8,128)(2,1)S(1)}, bf16[32,3584]{1,0:T(8,128)(2,1)S(1)}, u32[]{:S(2)}, u32[]{:S(2)}) collective-permute-start(bf16[32,3584]{1,0:T(8,128)(2,1)S(1)} %scope_last.1), channel_id=1, source_target_pairs={{0,2},{1,3},{2,0},{3,1},{4,6},{5,7},{6,4},{7,5},{8,10},{9,11},{10,... | collective-permute-start | bytes 688136 | tf_op jit(solution)/shard_map/ppermute | solution.py:21
  23.6 2.0 %scope_far0.1 = (f32[32,3584]{1,0:T(8,128)S(1)}, bf16[64,3584]{1,0:T(8,128)(2,1)S(1)}) custom-call(bf16[32,3712]{1,0:T(8,128)(2,1)S(1)} %collective-permute-done.3.refs_0_.refs_1_, bf16[64,3584]{1,0:T(8,128)(2,1)S(1)} %collective-permute-done.4.refs_1_, bf16[3584,256]{1,0:T(8,128)(2,1)S(1)} %collective-permute-done.gate.refs_2_.refs_1_, ...), custom_call_target="tpu_custom_call" | custom-call | flops 1 | tf_op jit(solution)/shard_map/scope_far0/pallas_call | solution.py:54
  25.6 1.1 %collective-permute-start.13 = (bf16[64,3584]{1,0:T(8,128)(2,1)S(1)}, bf16[64,3584]{1,0:T(8,128)(2,1)S(1)}, u32[]{:S(2)}, u32[]{:S(2)}) collective-permute-start(bf16[64,3584]{1,0:T(8,128)(2,1)S(1)} %get-tuple-element.49), channel_id=1, source_target_pairs={{0,2},{1,3},{2,0},{3,1},{4,6},{5,7},{6,4},{7,5},{8,10},{9,11},{10,... | collective-permute-start | bytes 1376264 | tf_op jit(solution)/shard_map/ppermute | solution.py:21
  26.7 0.0 collective-permute-done.6.refs_2_
  26.7 0.0 collective-permute-done.7.refs_3_
  26.7 0.0 collective-permute-done.8.refs_5_
  26.7 2.1 %scope_expert.1 = (bf16[8,3584]{1,0:T(8,128)(2,1)S(1)}, bf16[8,3584]{1,0:T(8,128)(2,1)S(1)}, bf16[16,3584]{1,0:T(8,128)(2,1)S(1)}, bf16[8,3584]{1,0:T(8,128)(2,1...) custom-call(bf16[16,3584]{1,0:T(8,128)(2,1)S(1)} %get-tuple-element.40.refs_0_.refs_2_,, ...), custom_call_target="tpu_custom_call" | custom-call | flops 30000001024 | tf_op jit(solution)/shard_map/scope_expert/pallas_call | solution.py:54
  28.8 2.8 %collective-permute-start.10 = (bf16[8,3584]{1,0:T(8,128)(2,1)S(1)}, bf16[8,3584]{1,0:T(8,128)(2,1)S(1)}, u32[]{:S(2)}, u32[]{:S(2)}) collective-permute-start(bf16[8,3584]{1,0:T(8,128)(2,1)S(1)} %get-tuple-element.47), channel_id=1, source_target_pairs={{0,8},{4,12},{8,0},{12,4},{1,9},{5,13},{9,1},{13,5},{2,10},{6,14},... | collective-permute-start | bytes 172040 | tf_op jit(solution)/shard_map/ppermute | solution.py:21
  31.6 1.3 %collective-permute-start.11 = (bf16[8,3584]{1,0:T(8,128)(2,1)S(1)}, bf16[8,3584]{1,0:T(8,128)(2,1)S(1)}, u32[]{:S(2)}, u32[]{:S(2)}) collective-permute-start(bf16[8,3584]{1,0:T(8,128)(2,1)S(1)} %get-tuple-element.48), channel_id=1, source_target_pairs={{0,12},{4,8},{8,4},{12,0},{1,13},{5,9},{9,5},{13,1},{2,14},{6,10},... | collective-permute-start | bytes 172040 | tf_op jit(solution)/shard_map/ppermute | solution.py:21
  32.9 0.0 collective-permute-start.9
  32.9 0.0 collective-permute-done.14.refs_0_
  32.9 2.1 %scope_far1.1 = bf16[32,3584]{1,0:T(8,128)(2,1)S(1)} custom-call(bf16[32,3584]{1,0:T(8,128)(2,1)S(1)} %collective-permute-done.14.refs_0_, bf16[3584,256]{1,0:T(8,128)(2,1)S(1)} %collective-permute-done.gate.refs_2_.refs_1_, bf16[3584,256]{1,0:T(8,128)(2,1)S(1)} %collective-permute-done.1.up.refs_3_.refs_2_, ...), custom_call_target="tpu_custom_call" | custom-call | flops 10000000000 | tf_op jit(solution)/shard_map/scope_far1/pallas_call | solution.py:54
  35.0 1.5 %collective-permute-start.15 = (bf16[32,3584]{1,0:T(8,128)(2,1)S(1)}, bf16[32,3584]{1,0:T(8,128)(2,1)S(1)}, u32[]{:S(2)}, u32[]{:S(2)}) collective-permute-start(bf16[32,3584]{1,0:T(8,128)(2,1)S(1)} %scope_far1.1), channel_id=1, source_target_pairs={{0,2},{1,3},{2,0},{3,1},{4,6},{5,7},{6,4},{7,5},{8,10},{9,11},{10,... | collective-permute-start | bytes 688136 | tf_op jit(solution)/shard_map/ppermute | solution.py:21
  36.5 0.0 collective-permute-done.10.refs_4_
  36.5 1.1 %collective-permute-done.11.refs_5_ = bf16[8,3584]{1,0:T(8,128)(2,1)S(1)} collective-permute-done((bf16[8,3584]{1,0:T(8,128)(2,1)S(1)}, bf16[8,3584]{1,0:T(8,128)(2,1)S(1)}, u32[]{:S(2)}, u32[]{:S(2)}) %collective-permute-start.11) | collective-permute-done | bytes 57376 | tf_op jit(solution)/shard_map/ppermute | solution.py:21
  37.7 0.6 %collective-permute-done.9.refs_3_.refs_6_ = bf16[16,3584]{1,0:T(8,128)(2,1)S(1)} collective-permute-done((bf16[16,3584]{1,0:T(8,128)(2,1)S(1)}, bf16[16,3584]{1,0:T(8,128)(2,1)S(1)}, u32[]{:S(2)}, u32[]{:S(2)}) %collective-permute-start.9) | collective-permute-done | bytes 114720 | tf_op jit(solution)/shard_map/ppermute | solution.py:21
  38.3 0.3 scope_fold.1
  38.6 1.6 %collective-permute-start.12 = (bf16[32,3584]{1,0:T(8,128)(2,1)S(1)}, bf16[32,3584]{1,0:T(8,128)(2,1)S(1)}, u32[]{:S(2)}, u32[]{:S(2)}) collective-permute-start(bf16[32,3584]{1,0:T(8,128)(2,1)S(1)} %scope_fold.1), channel_id=1, source_target_pairs={{0,2},{1,3},{2,0},{3,1},{4,6},{5,7},{6,4},{7,5},{8,10},{9,11},{10,... | collective-permute-start | bytes 688136 | tf_op jit(solution)/shard_map/ppermute | solution.py:21
  40.2 1.0 %collective-permute-start.16 = (bf16[8,3584]{1,0:T(8,128)(2,1)S(1)}, bf16[8,3584]{1,0:T(8,128)(2,1)S(1)}, u32[]{:S(2)}, u32[]{:S(2)}) collective-permute-start(bf16[8,3584]{1,0:T(8,128)(2,1)S(1)} %get-tuple-element.51), channel_id=1, source_target_pairs={{0,8},{4,12},{8,0},{12,4},{1,9},{5,13},{9,1},{13,5},{2,10},{6,14},... | collective-permute-start | bytes 172040 | tf_op jit(solution)/shard_map/ppermute | solution.py:21
  41.2 1.9 %collective-permute-start.17 = (bf16[8,3584]{1,0:T(8,128)(2,1)S(1)}, bf16[8,3584]{1,0:T(8,128)(2,1)S(1)}, u32[]{:S(2)}, u32[]{:S(2)}) collective-permute-start(bf16[8,3584]{1,0:T(8,128)(2,1)S(1)} %get-tuple-element.52), channel_id=1, source_target_pairs={{0,12},{4,8},{8,4},{12,0},{1,13},{5,9},{9,5},{13,1},{2,14},{6,10},... | collective-permute-start | bytes 172040 | tf_op jit(solution)/shard_map/ppermute | solution.py:21
  43.1 2.7 %collective-permute-done.15.refs_4_ = bf16[32,3584]{1,0:T(8,128)(2,1)S(1)} collective-permute-done((bf16[32,3584]{1,0:T(8,128)(2,1)S(1)}, bf16[32,3584]{1,0:T(8,128)(2,1)S(1)}, u32[]{:S(2)}, u32[]{:S(2)}) %collective-permute-start.15) | collective-permute-done | bytes 229408 | tf_op jit(solution)/shard_map/ppermute | solution.py:21
  45.8 0.0 collective-permute-done.13.refs_3_
  45.8 0.0 collective-permute-done.16.refs_7_
  45.9 1.3 %collective-permute-done.17.refs_8_ = bf16[8,3584]{1,0:T(8,128)(2,1)S(1)} collective-permute-done((bf16[8,3584]{1,0:T(8,128)(2,1)S(1)}, bf16[8,3584]{1,0:T(8,128)(2,1)S(1)}, u32[]{:S(2)}, u32[]{:S(2)}) %collective-permute-start.17) | collective-permute-done | bytes 57376 | tf_op jit(solution)/shard_map/ppermute | solution.py:21
  47.2 2.4 %collective-permute-done.12.refs_2_ = bf16[32,3584]{1,0:T(8,128)(2,1)S(1)} collective-permute-done((bf16[32,3584]{1,0:T(8,128)(2,1)S(1)}, bf16[32,3584]{1,0:T(8,128)(2,1)S(1)}, u32[]{:S(2)}, u32[]{:S(2)}) %collective-permute-start.12) | collective-permute-done | bytes 229408 | tf_op jit(solution)/shard_map/ppermute | solution.py:21
  49.6 1.2 %scope_final.1 = bf16[128,3584]{1,0:T(8,128)(2,1)} custom-call(f32[128,3584]{1,0:T(8,128)S(1)} %get-tuple-element.35.refs_0_, bf16[256,128]{1,0:T(8,128)(2,1)S(1)} %get-tuple-element.30.refs_0_.refs_1_, bf16[32,3584]{1,0:T(8,128)(2,1)S(1)} %collective-permute-done.12.refs_2_, bf16[64,3584]{1,0:T(8,128)(2,1)S(1)} %collective-permute-done.13.refs_3_, ...), custom_call_target="tpu_custom_call" | custom-call | flops 10000000000 | tf_op jit(solution)/shard_map/scope_final/pallas_call | solution.py:375
  (6 shorter events, 0.0 us)
Async XLA Ops:
  2.1 9.6 %collective-permute-start.3 = (bf16[32,3712]{1,0:T(8,128)(2,1)S(1)}, bf16[32,3712]{1,0:T(8,128)(2,1)S(1)}, u32[]{:S(2)}, u32[]{:S(2)}) collective-permute-start(bf16[32,3712]{1,0:T(8,128)(2,1)S(1)} %get-tuple-element.33.near_ref), channel_id=1, source_target_pairs={{0,2},{1,3},{2,0},{3,1},{4,6},{5,7},{6,4},{7,5},{8,10},{9,11},{10,... | collective-permute-start | bytes 712712 | tf_op jit(solution)/shard_map/ppermute | solution.py:21
  5.1 1.5 %copy-start.2 = (bf16[3584,256]{1,0:T(8,128)(2,1)S(1)}, bf16[3584,256]{1,0:T(8,128)(2,1)}, u32[]{:S(2)}) copy-start(bf16[3584,256]{1,0:T(8,128)(2,1)} %sg_hbm.1) | copy-start | bytes 5505028
  5.1 2.0 %copy-start = (bf16[3584,256]{1,0:T(8,128)(2,1)S(1)}, bf16[3584,256]{1,0:T(8,128)(2,1)}, u32[]{:S(2)}) copy-start(bf16[3584,256]{1,0:T(8,128)(2,1)} %su_hbm.1) | copy-start | bytes 5505028
  5.1 2.6 %copy-start.1 = (bf16[256,3584]{1,0:T(8,128)(2,1)S(1)}, bf16[256,3584]{1,0:T(8,128)(2,1)}, u32[]{:S(2)}) copy-start(bf16[256,3584]{1,0:T(8,128)(2,1)} %sd_hbm.1) | copy-start | bytes 5505028
  5.5 17.0 %collective-permute-start.4 = (bf16[64,3584]{1,0:T(8,128)(2,1)S(1)}, bf16[64,3584]{1,0:T(8,128)(2,1)S(1)}, u32[]{:S(2)}, u32[]{:S(2)}) collective-permute-start(bf16[64,3584]{1,0:T(8,128)(2,1)S(1)} %get-tuple-element.36), channel_id=1, source_target_pairs={{0,2},{1,3},{2,0},{3,1},{4,6},{5,7},{6,4},{7,5},{8,10},{9,11},{10,... | collective-permute-start | bytes 1376264 | tf_op jit(solution)/shard_map/ppermute | solution.py:21
  6.6 5.4 %collective-permute-start = (bf16[3584,256]{1,0:T(8,128)(2,1)S(1)}, bf16[3584,256]{1,0:T(8,128)(2,1)S(1)}, u32[]{:S(2)}, u32[]{:S(2)}) collective-permute-start(bf16[3584,256]{1,0:T(8,128)(2,1)S(1)} %copy-done.2), channel_id=1, source_target_pairs={{0,1},{1,0},{2,3},{3,2},{4,5},{5,4},{6,7},{7,6},{8,9},{9,8},{10,11... | collective-permute-start | bytes 5505032 | tf_op jit(solution)/shard_map/ppermute | solution.py:21
  7.1 7.1 %collective-permute-start.1 = (bf16[3584,256]{1,0:T(8,128)(2,1)S(1)}, bf16[3584,256]{1,0:T(8,128)(2,1)S(1)}, u32[]{:S(2)}, u32[]{:S(2)}) collective-permute-start(bf16[3584,256]{1,0:T(8,128)(2,1)S(1)} %copy-done), channel_id=1, source_target_pairs={{0,1},{1,0},{2,3},{3,2},{4,5},{5,4},{6,7},{7,6},{8,9},{9,8},{10,11... | collective-permute-start | bytes 5505032 | tf_op jit(solution)/shard_map/ppermute | solution.py:21
  7.7 9.1 %collective-permute-start.2 = (bf16[256,3584]{1,0:T(8,128)(2,1)S(1)}, bf16[256,3584]{1,0:T(8,128)(2,1)S(1)}, u32[]{:S(2)}, u32[]{:S(2)}) collective-permute-start(bf16[256,3584]{1,0:T(8,128)(2,1)S(1)} %copy-done.1), channel_id=1, source_target_pairs={{0,1},{1,0},{2,3},{3,2},{4,5},{5,4},{6,7},{7,6},{8,9},{9,8},{10,11... | collective-permute-start | bytes 5505032 | tf_op jit(solution)/shard_map/ppermute | solution.py:21
  11.7 15.0 %collective-permute-start.8 = (bf16[10752,256]{1,0:T(8,128)(2,1)S(1)}, bf16[10752,256]{1,0:T(8,128)(2,1)S(1)}, u32[]{:S(2)}, u32[]{:S(2)}) collective-permute-start(bf16[10752,256]{1,0:T(8,128)(2,1)S(1)} %get-tuple-element.44.refs_4_), channel_id=1, source_target_pairs={{0,1},{1,0},{2,3},{3,2},{4,5},{5,4},{6,7},{7,6},{8,9},{9,8},{10,11... | collective-permute-start | bytes 16515080 | tf_op jit(solution)/shard_map/ppermute | solution.py:21
  12.0 13.6 %collective-permute-start.5 = (bf16[16,3584]{1,0:T(8,128)(2,1)S(1)}, bf16[16,3584]{1,0:T(8,128)(2,1)S(1)}, u32[]{:S(2)}, u32[]{:S(2)}) collective-permute-start(bf16[16,3584]{1,0:T(8,128)(2,1)S(1)} %get-tuple-element.41), channel_id=1, source_target_pairs={{0,4},{4,0},{8,12},{12,8},{1,5},{5,1},{9,13},{13,9},{2,6},{6,2},{1... | collective-permute-start | bytes 344072 | tf_op jit(solution)/shard_map/ppermute | solution.py:21
  14.2 12.5 %collective-permute-start.6 = (bf16[16,3584]{1,0:T(8,128)(2,1)S(1)}, bf16[16,3584]{1,0:T(8,128)(2,1)S(1)}, u32[]{:S(2)}, u32[]{:S(2)}) collective-permute-start(bf16[16,3584]{1,0:T(8,128)(2,1)S(1)} %get-tuple-element.42), channel_id=1, source_target_pairs={{0,8},{4,12},{8,0},{12,4},{1,9},{5,13},{9,1},{13,5},{2,10},{6,14},... | collective-permute-start | bytes 344072 | tf_op jit(solution)/shard_map/ppermute | solution.py:21
  16.8 9.9 %collective-permute-start.7 = (bf16[16,3584]{1,0:T(8,128)(2,1)S(1)}, bf16[16,3584]{1,0:T(8,128)(2,1)S(1)}, u32[]{:S(2)}, u32[]{:S(2)}) collective-permute-start(bf16[16,3584]{1,0:T(8,128)(2,1)S(1)} %get-tuple-element.43), channel_id=1, source_target_pairs={{0,12},{4,8},{8,4},{12,0},{1,13},{5,9},{9,5},{13,1},{2,14},{6,10},... | collective-permute-start | bytes 344072 | tf_op jit(solution)/shard_map/ppermute | solution.py:21
  22.5 10.4 %collective-permute-start.14 = (bf16[32,3584]{1,0:T(8,128)(2,1)S(1)}, bf16[32,3584]{1,0:T(8,128)(2,1)S(1)}, u32[]{:S(2)}, u32[]{:S(2)}) collective-permute-start(bf16[32,3584]{1,0:T(8,128)(2,1)S(1)} %scope_last.1), channel_id=1, source_target_pairs={{0,2},{1,3},{2,0},{3,1},{4,6},{5,7},{6,4},{7,5},{8,10},{9,11},{10,... | collective-permute-start | bytes 688136 | tf_op jit(solution)/shard_map/ppermute | solution.py:21
  25.6 20.3 %collective-permute-start.13 = (bf16[64,3584]{1,0:T(8,128)(2,1)S(1)}, bf16[64,3584]{1,0:T(8,128)(2,1)S(1)}, u32[]{:S(2)}, u32[]{:S(2)}) collective-permute-start(bf16[64,3584]{1,0:T(8,128)(2,1)S(1)} %get-tuple-element.49), channel_id=1, source_target_pairs={{0,2},{1,3},{2,0},{3,1},{4,6},{5,7},{6,4},{7,5},{8,10},{9,11},{10,... | collective-permute-start | bytes 1376264 | tf_op jit(solution)/shard_map/ppermute | solution.py:21
  28.8 7.7 %collective-permute-start.10 = (bf16[8,3584]{1,0:T(8,128)(2,1)S(1)}, bf16[8,3584]{1,0:T(8,128)(2,1)S(1)}, u32[]{:S(2)}, u32[]{:S(2)}) collective-permute-start(bf16[8,3584]{1,0:T(8,128)(2,1)S(1)} %get-tuple-element.47), channel_id=1, source_target_pairs={{0,8},{4,12},{8,0},{12,4},{1,9},{5,13},{9,1},{13,5},{2,10},{6,14},... | collective-permute-start | bytes 172040 | tf_op jit(solution)/shard_map/ppermute | solution.py:21
  31.6 6.1 %collective-permute-start.11 = (bf16[8,3584]{1,0:T(8,128)(2,1)S(1)}, bf16[8,3584]{1,0:T(8,128)(2,1)S(1)}, u32[]{:S(2)}, u32[]{:S(2)}) collective-permute-start(bf16[8,3584]{1,0:T(8,128)(2,1)S(1)} %get-tuple-element.48), channel_id=1, source_target_pairs={{0,12},{4,8},{8,4},{12,0},{1,13},{5,9},{9,5},{13,1},{2,14},{6,10},... | collective-permute-start | bytes 172040 | tf_op jit(solution)/shard_map/ppermute | solution.py:21
  32.9 5.4 %collective-permute-start.9 = (bf16[16,3584]{1,0:T(8,128)(2,1)S(1)}, bf16[16,3584]{1,0:T(8,128)(2,1)S(1)}, u32[]{:S(2)}, u32[]{:S(2)}) collective-permute-start(bf16[16,3584]{1,0:T(8,128)(2,1)S(1)} %get-tuple-element.46), channel_id=1, source_target_pairs={{0,4},{4,0},{8,12},{12,8},{1,5},{5,1},{9,13},{13,9},{2,6},{6,2},{1... | collective-permute-start | bytes 344072 | tf_op jit(solution)/shard_map/ppermute | solution.py:21
  35.0 10.8 %collective-permute-start.15 = (bf16[32,3584]{1,0:T(8,128)(2,1)S(1)}, bf16[32,3584]{1,0:T(8,128)(2,1)S(1)}, u32[]{:S(2)}, u32[]{:S(2)}) collective-permute-start(bf16[32,3584]{1,0:T(8,128)(2,1)S(1)} %scope_far1.1), channel_id=1, source_target_pairs={{0,2},{1,3},{2,0},{3,1},{4,6},{5,7},{6,4},{7,5},{8,10},{9,11},{10,... | collective-permute-start | bytes 688136 | tf_op jit(solution)/shard_map/ppermute | solution.py:21
  38.6 11.0 %collective-permute-start.12 = (bf16[32,3584]{1,0:T(8,128)(2,1)S(1)}, bf16[32,3584]{1,0:T(8,128)(2,1)S(1)}, u32[]{:S(2)}, u32[]{:S(2)}) collective-permute-start(bf16[32,3584]{1,0:T(8,128)(2,1)S(1)} %scope_fold.1), channel_id=1, source_target_pairs={{0,2},{1,3},{2,0},{3,1},{4,6},{5,7},{6,4},{7,5},{8,10},{9,11},{10,... | collective-permute-start | bytes 688136 | tf_op jit(solution)/shard_map/ppermute | solution.py:21
  40.2 5.7 %collective-permute-start.16 = (bf16[8,3584]{1,0:T(8,128)(2,1)S(1)}, bf16[8,3584]{1,0:T(8,128)(2,1)S(1)}, u32[]{:S(2)}, u32[]{:S(2)}) collective-permute-start(bf16[8,3584]{1,0:T(8,128)(2,1)S(1)} %get-tuple-element.51), channel_id=1, source_target_pairs={{0,8},{4,12},{8,0},{12,4},{1,9},{5,13},{9,1},{13,5},{2,10},{6,14},... | collective-permute-start | bytes 172040 | tf_op jit(solution)/shard_map/ppermute | solution.py:21
  41.2 6.0 %collective-permute-start.17 = (bf16[8,3584]{1,0:T(8,128)(2,1)S(1)}, bf16[8,3584]{1,0:T(8,128)(2,1)S(1)}, u32[]{:S(2)}, u32[]{:S(2)}) collective-permute-start(bf16[8,3584]{1,0:T(8,128)(2,1)S(1)} %get-tuple-element.52), channel_id=1, source_target_pairs={{0,12},{4,8},{8,4},{12,0},{1,13},{5,9},{9,5},{13,1},{2,14},{6,10},... | collective-permute-start | bytes 172040 | tf_op jit(solution)/shard_map/ppermute | solution.py:21

commit v8 on v7

--- a/solution.py
+++ b/solution.py
@@ -149,7 +149,7 @@
     return dot(hidden, down[...])
 
 
-def load_kernel(gate_hbm, up_hbm, down_hbm, sg_hbm, near_ref, pack_ref, sg, sems):
+def load_kernel(gate_hbm, up_hbm, down_hbm, sg_hbm, su_hbm, near_ref, pack_ref, sg, su, sems):
     width, part = gate_hbm.shape
     copies = [(gate_hbm, 0), (up_hbm, width)]
     copies += [(down_hbm.at[:, i : i + part], 2 * width + i) for i in range(0, width, part)]
@@ -160,6 +160,7 @@
         for i, (source, place) in enumerate(copies)
     ]
     copies.append(pltpu.make_async_copy(sg_hbm, sg, sems.at[len(copies)]))
+    copies.append(pltpu.make_async_copy(su_hbm, su, sems.at[len(copies)]))
     for copy in copies:
         copy.start()
     for copy in copies:
@@ -195,21 +196,14 @@
     return bf16(jnp.concatenate(pieces, axis=0))
 
 
-def own_kernel(
-    tokens_ref, gate, up, down, after_ref, sg, su_hbm, sd_hbm, own_ref, su, sd, sems
-):
-    copies = [
-        pltpu.make_async_copy(su_hbm, su, sems.at[0]),
-        pltpu.make_async_copy(sd_hbm, sd, sems.at[1]),
-    ]
-    for copy in copies:
-        copy.start()
+def own_kernel(tokens_ref, gate, up, down, after_ref, sg, su, sd_hbm, own_ref, sd, sem):
+    copy = pltpu.make_async_copy(sd_hbm, sd, sem)
+    copy.start()
     rows = tokens_ref[...]
     own_ref[...] = mlp(rows, gate, up, down)
     v = dot(rows, sg[...])
-    copies[0].wait()
     hidden = bf16(v / (1.0 + jnp.exp(-v)) * dot(rows, su[...]))
-    copies[1].wait()
+    copy.wait()
     own_ref[...] += dot(hidden, sd[...])
 
 
@@ -303,13 +297,13 @@
         room=8 * slots * width,
     )
     part = w_gate.shape[2]
-    pack, own_gate = call(
+    pack, own_gate, own_up = call(
         "load",
         load_kernel,
-        [struct(3 * width, part), struct(*s_gate.shape)],
-        (w_gate[0], w_up[0], w_down[0], s_gate, first),
-        specs=[HBM] * 4 + [VMEM],
-        scratch=[pltpu.SemaphoreType.DMA((3 + width // part,))],
+        [struct(3 * width, part), struct(*s_gate.shape), struct(*s_up.shape)],
+        (w_gate[0], w_up[0], w_down[0], s_gate, s_up, first),
+        specs=[HBM] * 5 + [VMEM],
+        scratch=[pltpu.SemaphoreType.DMA((4 + width // part,))],
         limit=16 << 20,
     )
     far_pack = shift(pack, "local", 1)
@@ -323,16 +317,16 @@
             room=4 * count * width,
         )
         rest_far.append(shift(last, "local", 2))
-    own, *mats = call(
+    own, own_down = call(
         "own",
         own_kernel,
-        [struct(count, width, jnp.float32)] + [struct(*w.shape) for w in shared_mats[1:]],
-        (held, *shared_far, near, own_gate, *shared_mats[1:]),
-        specs=[VMEM] * 6 + [HBM] * 2,
-        scratch=[pltpu.SemaphoreType.DMA((2,))],
+        [struct(count, width, jnp.float32), struct(*s_down.shape)],
+        (held, *shared_far, near, own_gate, own_up, s_down),
+        specs=[VMEM] * 7 + [HBM],
+        scratch=[pltpu.SemaphoreType.DMA],
         limit=16 << 20,
     )
-    mats = [own_gate, *mats]
+    mats = [own_gate, own_up, own_down]
     whole = [n == 1 and nodes <= FEW_NODES for n in range(nodes)]
     replied = call(
         "expert",

time: 51 us -> 49.9 us (0.978)
  waiting for transfers between devices: 8.95 us -> 7.78 us
  Pallas kernels: 17 us -> 16.4 us
  starting transfers between devices: 22.7 us -> 23.3 us
    ppermute x18, waiting for transfers between devices: 8.95 us -> 7.78 us  [shift(): return lax.ppermute(value, axis, [(i, i ^ mask) for i in range(size)])]
    ppermute x18, starting transfers between devices: 22.7 us -> 23.3 us  [shift(): return lax.ppermute(value, axis, [(i, i ^ mask) for i in range(size)])]
    pallas_call x10, Pallas kernels: 15.8 us -> 15.2 us  [call(): pl.pallas_call(kernel, name='scope_' + name, out_shape=outs, in_specs=spe...]
  transfers between devices with their start and end apart: 18 -> 18, of which waited for: 6 -> 8; matrix products, arithmetic and copies ran while one was open for 0% -> 0% of each run, Pallas kernels for 27% -> 26%
where the time goes in v8:
time: 49.9 us; the launch traced here: 49.7 us
  starting transfers between devices  23.3 us (47%)
  Pallas kernels  16.4 us (33%)
  waiting for transfers between devices  7.78 us (16%)
  local copies, waits for them, and re-layouts  2.09 us (4%)
    ppermute x18, starting transfers between devices, shift(): return lax.ppermute(value, axis, [(i, i ^ mask) for i in range(size)])  23.3 us
    pallas_call x10, Pallas kernels, call(): pl.pallas_call(kernel, name='scope_' + name, out_shape=outs, in_specs=spe...  15.2 us
    ppermute x18, waiting for transfers between devices, shift(): return lax.ppermute(value, axis, [(i, i ^ mask) for i in range(size)])  7.78 us
    unnamed x6, local copies, waits for them, and re-layouts  2.09 us
    pallas_call x1, Pallas kernels, per_device(): pl.pallas_call(lambda *refs: final_kernel(block, len(backs), *refs), name...  1.21 us
  transfers between devices with their start and end apart: 18, of which 8 were waited for; matrix products, arithmetic and copies ran while one was open for 0% of the time, Pallas kernels for 26%

profile of v8, /device:TPU:0, one launch (start us, length us, event | category | flops | bytes accessed | tf_op | source)
XLA Modules:
  0.0 49.7 jit_solution(13624191626052587688)
XLA Ops:
  0.0 2.0 %scope_head.1 = (bf16[32,3712]{1,0:T(8,128)(2,1)S(1)}, bf16[256,128]{1,0:T(8,128)(2,1)S(1)}, bf16[64,128]{1,0:T(8,128)(2,1)S(1)}, bf16[128,3584]{1,0:T(8,128)(2,1)S(1)}) custom-call(s32[4]{0:T(128)S(1)} %xor_multiply_fusion.refs_0_, s32[8,128]{1,0:T(8,128)} %bitcast.5, f32[8,128]{1,0:T(8,128)} %bitcast.6, bf16[128,3584]{1,0:T(8,128)(2,1)} %refs_3_.1), custom_call_target="tpu_custom_call" | custom-call | flops 100000000 | tf_op jit(solution)/shard_map/scope_head/pallas_call | solution.py:54
  2.1 3.0 %collective-permute-start.3 = (bf16[32,3712]{1,0:T(8,128)(2,1)S(1)}, bf16[32,3712]{1,0:T(8,128)(2,1)S(1)}, u32[]{:S(2)}, u32[]{:S(2)}) collective-permute-start(bf16[32,3712]{1,0:T(8,128)(2,1)S(1)} %get-tuple-element.33.near_ref), channel_id=1, source_target_pairs={{0,2},{1,3},{2,0},{3,1},{4,6},{5,7},{6,4},{7,5},{8,10},{9,11},{10,... | collective-permute-start | bytes 712712 | tf_op jit(solution)/shard_map/ppermute | solution.py:21
  5.1 0.4 scope_tail.1
  5.5 0.1 collective-permute-start.4
  5.6 1.0 %copy-done.1 = bf16[3584,256]{1,0:T(8,128)(2,1)S(1)} copy-done((bf16[3584,256]{1,0:T(8,128)(2,1)S(1)}, bf16[3584,256]{1,0:T(8,128)(2,1)}, u32[]{:S(2)}) %copy-start.1) | copy-done | bytes 1835032
  6.6 0.0 collective-permute-start
  6.6 0.5 %copy-done.2 = bf16[3584,256]{1,0:T(8,128)(2,1)S(1)} copy-done((bf16[3584,256]{1,0:T(8,128)(2,1)S(1)}, bf16[3584,256]{1,0:T(8,128)(2,1)}, u32[]{:S(2)}) %copy-start.2) | copy-done | bytes 1835032
  7.1 0.6 %copy-done = bf16[256,3584]{1,0:T(8,128)(2,1)S(1)} copy-done((bf16[256,3584]{1,0:T(8,128)(2,1)S(1)}, bf16[256,3584]{1,0:T(8,128)(2,1)}, u32[]{:S(2)}) %copy-start) | copy-done | bytes 1835032
  7.7 0.0 collective-permute-start.2
  7.7 3.9 %scope_load.1 = (bf16[10752,256]{1,0:T(8,128)(2,1)S(1)}, bf16[3584,256]{1,0:T(8,128)(2,1)S(1)}, bf16[3584,256]{1,0:T(8,128)(2,1)S(1)}) custom-call(bf16[3584,256]{1,0:T(8,128)(2,1)} %bitcast.7, bf16[3584,256]{1,0:T(8,128)(2,1)} %bitcast.8, bf16[256,3584]{1,0:T(8,128)(2,1)} %bitcast.9, bf16[3584,256]{1,0:T(8,128)(2,1)} %sg_hbm.1, bf16[3584,256]{1,0:T(8,128)(2,1)} %su_hbm.1, ...), custom_call_target="tpu_custom_call" | custom-call | flops 30000001024 | tf_op jit(solution)/shard_map/scope_load/pallas_call | solution.py:54
  11.5 0.1 collective-permute-done.3.refs_0_.refs_1_
  11.7 0.5 collective-permute-start.8
  12.1 0.3 scope_join.1
  12.4 0.0 collective-permute-done.gate.refs_2_.refs_1_
  12.5 1.8 %collective-permute-start.5 = (bf16[16,3584]{1,0:T(8,128)(2,1)S(1)}, bf16[16,3584]{1,0:T(8,128)(2,1)S(1)}, u32[]{:S(2)}, u32[]{:S(2)}) collective-permute-start(bf16[16,3584]{1,0:T(8,128)(2,1)S(1)} %get-tuple-element.41), channel_id=1, source_target_pairs={{0,4},{4,0},{8,12},{12,8},{1,5},{5,1},{9,13},{13,9},{2,6},{6,2},{1... | collective-permute-start | bytes 344072 | tf_op jit(solution)/shard_map/ppermute | solution.py:21
  14.2 2.6 %collective-permute-start.6 = (bf16[16,3584]{1,0:T(8,128)(2,1)S(1)}, bf16[16,3584]{1,0:T(8,128)(2,1)S(1)}, u32[]{:S(2)}, u32[]{:S(2)}) collective-permute-start(bf16[16,3584]{1,0:T(8,128)(2,1)S(1)} %get-tuple-element.42), channel_id=1, source_target_pairs={{0,8},{4,12},{8,0},{12,4},{1,9},{5,13},{9,1},{13,5},{2,10},{6,14},... | collective-permute-start | bytes 344072 | tf_op jit(solution)/shard_map/ppermute | solution.py:21
  16.8 0.0 collective-permute-done.2.down.refs_4_.refs_3_
  16.8 2.4 %collective-permute-start.7 = (bf16[16,3584]{1,0:T(8,128)(2,1)S(1)}, bf16[16,3584]{1,0:T(8,128)(2,1)S(1)}, u32[]{:S(2)}, u32[]{:S(2)}) collective-permute-start(bf16[16,3584]{1,0:T(8,128)(2,1)S(1)} %get-tuple-element.43), channel_id=1, source_target_pairs={{0,12},{4,8},{8,4},{12,0},{1,13},{5,9},{9,5},{13,1},{2,14},{6,10},... | collective-permute-start | bytes 344072 | tf_op jit(solution)/shard_map/ppermute | solution.py:21
  19.2 0.2 scope_last.1
  19.5 1.9 %scope_own.1 = (f32[128,3584]{1,0:T(8,128)S(1)}, bf16[256,3584]{1,0:T(8,128)(2,1)S(1)}) custom-call(bf16[128,3584]{1,0:T(8,128)(2,1)S(1)} %get-tuple-element.29.refs_2_.tokens_ref.refs_1_, bf16[3584,256]{1,0:T(8,128)(2,1)S(1)} %collective-permute-done.gate.refs_2_.refs_1_, bf16[3584,256]{1,0:T(8,128)(2,1)S(1)} %collective-permute-done.1.up.refs_3_.refs_2_, ...), custom_call_target="tpu_custom_call" | custom-call | flops 100000000 | tf_op jit(solution)/shard_map/scope_own/pallas_call | solution.py:54
  21.4 0.0 collective-permute-done.4.refs_1_
  21.4 1.1 %collective-permute-start.14 = (bf16[32,3584]{1,0:T(8,128)(2,1)S(1)}, bf16[32,3584]{1,0:T(8,128)(2,1)S(1)}, u32[]{:S(2)}, u32[]{:S(2)}) collective-permute-start(bf16[32,3584]{1,0:T(8,128)(2,1)S(1)} %scope_last.1), channel_id=1, source_target_pairs={{0,2},{1,3},{2,0},{3,1},{4,6},{5,7},{6,4},{7,5},{8,10},{9,11},{10,... | collective-permute-start | bytes 688136 | tf_op jit(solution)/shard_map/ppermute | solution.py:21
  22.5 2.0 %scope_far0.1 = (f32[32,3584]{1,0:T(8,128)S(1)}, bf16[64,3584]{1,0:T(8,128)(2,1)S(1)}) custom-call(bf16[32,3712]{1,0:T(8,128)(2,1)S(1)} %collective-permute-done.3.refs_0_.refs_1_, bf16[64,3584]{1,0:T(8,128)(2,1)S(1)} %collective-permute-done.4.refs_1_, bf16[3584,256]{1,0:T(8,128)(2,1)S(1)} %collective-permute-done.gate.refs_2_.refs_1_, ...), custom_call_target="tpu_custom_call" | custom-call | flops 1 | tf_op jit(solution)/shard_map/scope_far0/pallas_call | solution.py:54
  24.5 0.0 collective-permute-done.5.refs_1_
  24.5 1.1 %collective-permute-start.13 = (bf16[64,3584]{1,0:T(8,128)(2,1)S(1)}, bf16[64,3584]{1,0:T(8,128)(2,1)S(1)}, u32[]{:S(2)}, u32[]{:S(2)}) collective-permute-start(bf16[64,3584]{1,0:T(8,128)(2,1)S(1)} %get-tuple-element.49), channel_id=1, source_target_pairs={{0,2},{1,3},{2,0},{3,1},{4,6},{5,7},{6,4},{7,5},{8,10},{9,11},{10,... | collective-permute-start | bytes 1376264 | tf_op jit(solution)/shard_map/ppermute | solution.py:21
  25.6 0.5 collective-permute-done.6.refs_2_
  26.0 0.0 collective-permute-done.7.refs_3_
  26.0 0.0 collective-permute-done.8.refs_5_
  26.0 2.1 %scope_expert.1 = (bf16[8,3584]{1,0:T(8,128)(2,1)S(1)}, bf16[8,3584]{1,0:T(8,128)(2,1)S(1)}, bf16[16,3584]{1,0:T(8,128)(2,1)S(1)}, bf16[8,3584]{1,0:T(8,128)(2,1...) custom-call(bf16[16,3584]{1,0:T(8,128)(2,1)S(1)} %get-tuple-element.40.refs_0_.refs_2_,, ...), custom_call_target="tpu_custom_call" | custom-call | flops 30000001024 | tf_op jit(solution)/shard_map/scope_expert/pallas_call | solution.py:54
  28.2 3.4 %collective-permute-start.10 = (bf16[8,3584]{1,0:T(8,128)(2,1)S(1)}, bf16[8,3584]{1,0:T(8,128)(2,1)S(1)}, u32[]{:S(2)}, u32[]{:S(2)}) collective-permute-start(bf16[8,3584]{1,0:T(8,128)(2,1)S(1)} %get-tuple-element.47), channel_id=1, source_target_pairs={{0,8},{4,12},{8,0},{12,4},{1,9},{5,13},{9,1},{13,5},{2,10},{6,14},... | collective-permute-start | bytes 172040 | tf_op jit(solution)/shard_map/ppermute | solution.py:21
  31.6 1.3 %collective-permute-start.11 = (bf16[8,3584]{1,0:T(8,128)(2,1)S(1)}, bf16[8,3584]{1,0:T(8,128)(2,1)S(1)}, u32[]{:S(2)}, u32[]{:S(2)}) collective-permute-start(bf16[8,3584]{1,0:T(8,128)(2,1)S(1)} %get-tuple-element.48), channel_id=1, source_target_pairs={{0,12},{4,8},{8,4},{12,0},{1,13},{5,9},{9,5},{13,1},{2,14},{6,10},... | collective-permute-start | bytes 172040 | tf_op jit(solution)/shard_map/ppermute | solution.py:21
  32.9 0.0 collective-permute-start.9
  32.9 0.0 collective-permute-done.14.refs_0_
  32.9 2.1 %scope_far1.1 = bf16[32,3584]{1,0:T(8,128)(2,1)S(1)} custom-call(bf16[32,3584]{1,0:T(8,128)(2,1)S(1)} %collective-permute-done.14.refs_0_, bf16[3584,256]{1,0:T(8,128)(2,1)S(1)} %collective-permute-done.gate.refs_2_.refs_1_, bf16[3584,256]{1,0:T(8,128)(2,1)S(1)} %collective-permute-done.1.up.refs_3_.refs_2_, ...), custom_call_target="tpu_custom_call" | custom-call | flops 10000000000 | tf_op jit(solution)/shard_map/scope_far1/pallas_call | solution.py:54
  35.0 1.5 %collective-permute-start.15 = (bf16[32,3584]{1,0:T(8,128)(2,1)S(1)}, bf16[32,3584]{1,0:T(8,128)(2,1)S(1)}, u32[]{:S(2)}, u32[]{:S(2)}) collective-permute-start(bf16[32,3584]{1,0:T(8,128)(2,1)S(1)} %scope_far1.1), channel_id=1, source_target_pairs={{0,2},{1,3},{2,0},{3,1},{4,6},{5,7},{6,4},{7,5},{8,10},{9,11},{10,... | collective-permute-start | bytes 688136 | tf_op jit(solution)/shard_map/ppermute | solution.py:21
  36.5 0.0 collective-permute-done.10.refs_4_
  36.5 1.1 %collective-permute-done.11.refs_5_ = bf16[8,3584]{1,0:T(8,128)(2,1)S(1)} collective-permute-done((bf16[8,3584]{1,0:T(8,128)(2,1)S(1)}, bf16[8,3584]{1,0:T(8,128)(2,1)S(1)}, u32[]{:S(2)}, u32[]{:S(2)}) %collective-permute-start.11) | collective-permute-done | bytes 57376 | tf_op jit(solution)/shard_map/ppermute | solution.py:21
  37.7 0.6 %collective-permute-done.9.refs_3_.refs_6_ = bf16[16,3584]{1,0:T(8,128)(2,1)S(1)} collective-permute-done((bf16[16,3584]{1,0:T(8,128)(2,1)S(1)}, bf16[16,3584]{1,0:T(8,128)(2,1)S(1)}, u32[]{:S(2)}, u32[]{:S(2)}) %collective-permute-start.9) | collective-permute-done | bytes 114720 | tf_op jit(solution)/shard_map/ppermute | solution.py:21
  38.3 0.3 scope_fold.1
  38.6 1.6 %collective-permute-start.12 = (bf16[32,3584]{1,0:T(8,128)(2,1)S(1)}, bf16[32,3584]{1,0:T(8,128)(2,1)S(1)}, u32[]{:S(2)}, u32[]{:S(2)}) collective-permute-start(bf16[32,3584]{1,0:T(8,128)(2,1)S(1)} %scope_fold.1), channel_id=1, source_target_pairs={{0,2},{1,3},{2,0},{3,1},{4,6},{5,7},{6,4},{7,5},{8,10},{9,11},{10,... | collective-permute-start | bytes 688136 | tf_op jit(solution)/shard_map/ppermute | solution.py:21
  40.2 1.0 %collective-permute-start.16 = (bf16[8,3584]{1,0:T(8,128)(2,1)S(1)}, bf16[8,3584]{1,0:T(8,128)(2,1)S(1)}, u32[]{:S(2)}, u32[]{:S(2)}) collective-permute-start(bf16[8,3584]{1,0:T(8,128)(2,1)S(1)} %get-tuple-element.51), channel_id=1, source_target_pairs={{0,8},{4,12},{8,0},{12,4},{1,9},{5,13},{9,1},{13,5},{2,10},{6,14},... | collective-permute-start | bytes 172040 | tf_op jit(solution)/shard_map/ppermute | solution.py:21
  41.2 1.9 %collective-permute-start.17 = (bf16[8,3584]{1,0:T(8,128)(2,1)S(1)}, bf16[8,3584]{1,0:T(8,128)(2,1)S(1)}, u32[]{:S(2)}, u32[]{:S(2)}) collective-permute-start(bf16[8,3584]{1,0:T(8,128)(2,1)S(1)} %get-tuple-element.52), channel_id=1, source_target_pairs={{0,12},{4,8},{8,4},{12,0},{1,13},{5,9},{9,5},{13,1},{2,14},{6,10},... | collective-permute-start | bytes 172040 | tf_op jit(solution)/shard_map/ppermute | solution.py:21
  43.1 1.6 %collective-permute-done.15.refs_4_ = bf16[32,3584]{1,0:T(8,128)(2,1)S(1)} collective-permute-done((bf16[32,3584]{1,0:T(8,128)(2,1)S(1)}, bf16[32,3584]{1,0:T(8,128)(2,1)S(1)}, u32[]{:S(2)}, u32[]{:S(2)}) %collective-permute-start.15) | collective-permute-done | bytes 229408 | tf_op jit(solution)/shard_map/ppermute | solution.py:21
  44.7 0.0 collective-permute-done.13.refs_3_
  44.7 1.1 %collective-permute-done.16.refs_7_ = bf16[8,3584]{1,0:T(8,128)(2,1)S(1)} collective-permute-done((bf16[8,3584]{1,0:T(8,128)(2,1)S(1)}, bf16[8,3584]{1,0:T(8,128)(2,1)S(1)}, u32[]{:S(2)}, u32[]{:S(2)}) %collective-permute-start.16) | collective-permute-done | bytes 57376 | tf_op jit(solution)/shard_map/ppermute | solution.py:21
  45.9 1.3 %collective-permute-done.17.refs_8_ = bf16[8,3584]{1,0:T(8,128)(2,1)S(1)} collective-permute-done((bf16[8,3584]{1,0:T(8,128)(2,1)S(1)}, bf16[8,3584]{1,0:T(8,128)(2,1)S(1)}, u32[]{:S(2)}, u32[]{:S(2)}) %collective-permute-start.17) | collective-permute-done | bytes 57376 | tf_op jit(solution)/shard_map/ppermute | solution.py:21
  47.2 1.3 %collective-permute-done.12.refs_2_ = bf16[32,3584]{1,0:T(8,128)(2,1)S(1)} collective-permute-done((bf16[32,3584]{1,0:T(8,128)(2,1)S(1)}, bf16[32,3584]{1,0:T(8,128)(2,1)S(1)}, u32[]{:S(2)}, u32[]{:S(2)}) %collective-permute-start.12) | collective-permute-done | bytes 229408 | tf_op jit(solution)/shard_map/ppermute | solution.py:21
  48.5 1.2 %scope_final.1 = bf16[128,3584]{1,0:T(8,128)(2,1)} custom-call(f32[128,3584]{1,0:T(8,128)S(1)} %get-tuple-element.36.refs_0_, bf16[256,128]{1,0:T(8,128)(2,1)S(1)} %get-tuple-element.30.refs_0_.refs_1_, bf16[32,3584]{1,0:T(8,128)(2,1)S(1)} %collective-permute-done.12.refs_2_, bf16[64,3584]{1,0:T(8,128)(2,1)S(1)} %collective-permute-done.13.refs_3_, ...), custom_call_target="tpu_custom_call" | custom-call | flops 10000000000 | tf_op jit(solution)/shard_map/scope_final/pallas_call | solution.py:369
  (6 shorter events, 0.0 us)
Async XLA Ops:
  2.1 9.6 %collective-permute-start.3 = (bf16[32,3712]{1,0:T(8,128)(2,1)S(1)}, bf16[32,3712]{1,0:T(8,128)(2,1)S(1)}, u32[]{:S(2)}, u32[]{:S(2)}) collective-permute-start(bf16[32,3712]{1,0:T(8,128)(2,1)S(1)} %get-tuple-element.33.near_ref), channel_id=1, source_target_pairs={{0,2},{1,3},{2,0},{3,1},{4,6},{5,7},{6,4},{7,5},{8,10},{9,11},{10,... | collective-permute-start | bytes 712712 | tf_op jit(solution)/shard_map/ppermute | solution.py:21
  5.1 1.5 %copy-start.1 = (bf16[3584,256]{1,0:T(8,128)(2,1)S(1)}, bf16[3584,256]{1,0:T(8,128)(2,1)}, u32[]{:S(2)}) copy-start(bf16[3584,256]{1,0:T(8,128)(2,1)} %sg_hbm.1) | copy-start | bytes 5505028
  5.1 2.0 %copy-start.2 = (bf16[3584,256]{1,0:T(8,128)(2,1)S(1)}, bf16[3584,256]{1,0:T(8,128)(2,1)}, u32[]{:S(2)}) copy-start(bf16[3584,256]{1,0:T(8,128)(2,1)} %su_hbm.1) | copy-start | bytes 5505028
  5.1 2.6 %copy-start = (bf16[256,3584]{1,0:T(8,128)(2,1)S(1)}, bf16[256,3584]{1,0:T(8,128)(2,1)}, u32[]{:S(2)}) copy-start(bf16[256,3584]{1,0:T(8,128)(2,1)} %sd_hbm.1) | copy-start | bytes 5505028
  5.5 15.9 %collective-permute-start.4 = (bf16[64,3584]{1,0:T(8,128)(2,1)S(1)}, bf16[64,3584]{1,0:T(8,128)(2,1)S(1)}, u32[]{:S(2)}, u32[]{:S(2)}) collective-permute-start(bf16[64,3584]{1,0:T(8,128)(2,1)S(1)} %get-tuple-element.37), channel_id=1, source_target_pairs={{0,2},{1,3},{2,0},{3,1},{4,6},{5,7},{6,4},{7,5},{8,10},{9,11},{10,... | collective-permute-start | bytes 1376264 | tf_op jit(solution)/shard_map/ppermute | solution.py:21
  6.6 5.9 %collective-permute-start = (bf16[3584,256]{1,0:T(8,128)(2,1)S(1)}, bf16[3584,256]{1,0:T(8,128)(2,1)S(1)}, u32[]{:S(2)}, u32[]{:S(2)}) collective-permute-start(bf16[3584,256]{1,0:T(8,128)(2,1)S(1)} %copy-done.1), channel_id=1, source_target_pairs={{0,1},{1,0},{2,3},{3,2},{4,5},{5,4},{6,7},{7,6},{8,9},{9,8},{10,11... | collective-permute-start | bytes 5505032 | tf_op jit(solution)/shard_map/ppermute | solution.py:21
  7.1 7.1 %collective-permute-start.1 = (bf16[3584,256]{1,0:T(8,128)(2,1)S(1)}, bf16[3584,256]{1,0:T(8,128)(2,1)S(1)}, u32[]{:S(2)}, u32[]{:S(2)}) collective-permute-start(bf16[3584,256]{1,0:T(8,128)(2,1)S(1)} %copy-done.2), channel_id=1, source_target_pairs={{0,1},{1,0},{2,3},{3,2},{4,5},{5,4},{6,7},{7,6},{8,9},{9,8},{10,11... | collective-permute-start | bytes 5505032 | tf_op jit(solution)/shard_map/ppermute | solution.py:21
  7.7 9.1 %collective-permute-start.2 = (bf16[256,3584]{1,0:T(8,128)(2,1)S(1)}, bf16[256,3584]{1,0:T(8,128)(2,1)S(1)}, u32[]{:S(2)}, u32[]{:S(2)}) collective-permute-start(bf16[256,3584]{1,0:T(8,128)(2,1)S(1)} %copy-done), channel_id=1, source_target_pairs={{0,1},{1,0},{2,3},{3,2},{4,5},{5,4},{6,7},{7,6},{8,9},{9,8},{10,11... | collective-permute-start | bytes 5505032 | tf_op jit(solution)/shard_map/ppermute | solution.py:21
  11.7 14.4 %collective-permute-start.8 = (bf16[10752,256]{1,0:T(8,128)(2,1)S(1)}, bf16[10752,256]{1,0:T(8,128)(2,1)S(1)}, u32[]{:S(2)}, u32[]{:S(2)}) collective-permute-start(bf16[10752,256]{1,0:T(8,128)(2,1)S(1)} %get-tuple-element.44.refs_4_), channel_id=1, source_target_pairs={{0,1},{1,0},{2,3},{3,2},{4,5},{5,4},{6,7},{7,6},{8,9},{9,8},{10,11... | collective-permute-start | bytes 16515080 | tf_op jit(solution)/shard_map/ppermute | solution.py:21
  12.5 12.0 %collective-permute-start.5 = (bf16[16,3584]{1,0:T(8,128)(2,1)S(1)}, bf16[16,3584]{1,0:T(8,128)(2,1)S(1)}, u32[]{:S(2)}, u32[]{:S(2)}) collective-permute-start(bf16[16,3584]{1,0:T(8,128)(2,1)S(1)} %get-tuple-element.41), channel_id=1, source_target_pairs={{0,4},{4,0},{8,12},{12,8},{1,5},{5,1},{9,13},{13,9},{2,6},{6,2},{1... | collective-permute-start | bytes 344072 | tf_op jit(solution)/shard_map/ppermute | solution.py:21
  14.2 11.8 %collective-permute-start.6 = (bf16[16,3584]{1,0:T(8,128)(2,1)S(1)}, bf16[16,3584]{1,0:T(8,128)(2,1)S(1)}, u32[]{:S(2)}, u32[]{:S(2)}) collective-permute-start(bf16[16,3584]{1,0:T(8,128)(2,1)S(1)} %get-tuple-element.42), channel_id=1, source_target_pairs={{0,8},{4,12},{8,0},{12,4},{1,9},{5,13},{9,1},{13,5},{2,10},{6,14},... | collective-permute-start | bytes 344072 | tf_op jit(solution)/shard_map/ppermute | solution.py:21
  16.8 9.2 %collective-permute-start.7 = (bf16[16,3584]{1,0:T(8,128)(2,1)S(1)}, bf16[16,3584]{1,0:T(8,128)(2,1)S(1)}, u32[]{:S(2)}, u32[]{:S(2)}) collective-permute-start(bf16[16,3584]{1,0:T(8,128)(2,1)S(1)} %get-tuple-element.43), channel_id=1, source_target_pairs={{0,12},{4,8},{8,4},{12,0},{1,13},{5,9},{9,5},{13,1},{2,14},{6,10},... | collective-permute-start | bytes 344072 | tf_op jit(solution)/shard_map/ppermute | solution.py:21
  21.4 11.5 %collective-permute-start.14 = (bf16[32,3584]{1,0:T(8,128)(2,1)S(1)}, bf16[32,3584]{1,0:T(8,128)(2,1)S(1)}, u32[]{:S(2)}, u32[]{:S(2)}) collective-permute-start(bf16[32,3584]{1,0:T(8,128)(2,1)S(1)} %scope_last.1), channel_id=1, source_target_pairs={{0,2},{1,3},{2,0},{3,1},{4,6},{5,7},{6,4},{7,5},{8,10},{9,11},{10,... | collective-permute-start | bytes 688136 | tf_op jit(solution)/shard_map/ppermute | solution.py:21
  24.5 20.2 %collective-permute-start.13 = (bf16[64,3584]{1,0:T(8,128)(2,1)S(1)}, bf16[64,3584]{1,0:T(8,128)(2,1)S(1)}, u32[]{:S(2)}, u32[]{:S(2)}) collective-permute-start(bf16[64,3584]{1,0:T(8,128)(2,1)S(1)} %get-tuple-element.49), channel_id=1, source_target_pairs={{0,2},{1,3},{2,0},{3,1},{4,6},{5,7},{6,4},{7,5},{8,10},{9,11},{10,... | collective-permute-start | bytes 1376264 | tf_op jit(solution)/shard_map/ppermute | solution.py:21
  28.2 8.4 %collective-permute-start.10 = (bf16[8,3584]{1,0:T(8,128)(2,1)S(1)}, bf16[8,3584]{1,0:T(8,128)(2,1)S(1)}, u32[]{:S(2)}, u32[]{:S(2)}) collective-permute-start(bf16[8,3584]{1,0:T(8,128)(2,1)S(1)} %get-tuple-element.47), channel_id=1, source_target_pairs={{0,8},{4,12},{8,0},{12,4},{1,9},{5,13},{9,1},{13,5},{2,10},{6,14},... | collective-permute-start | bytes 172040 | tf_op jit(solution)/shard_map/ppermute | solution.py:21
  31.6 6.1 %collective-permute-start.11 = (bf16[8,3584]{1,0:T(8,128)(2,1)S(1)}, bf16[8,3584]{1,0:T(8,128)(2,1)S(1)}, u32[]{:S(2)}, u32[]{:S(2)}) collective-permute-start(bf16[8,3584]{1,0:T(8,128)(2,1)S(1)} %get-tuple-element.48), channel_id=1, source_target_pairs={{0,12},{4,8},{8,4},{12,0},{1,13},{5,9},{9,5},{13,1},{2,14},{6,10},... | collective-permute-start | bytes 172040 | tf_op jit(solution)/shard_map/ppermute | solution.py:21
  32.9 5.4 %collective-permute-start.9 = (bf16[16,3584]{1,0:T(8,128)(2,1)S(1)}, bf16[16,3584]{1,0:T(8,128)(2,1)S(1)}, u32[]{:S(2)}, u32[]{:S(2)}) collective-permute-start(bf16[16,3584]{1,0:T(8,128)(2,1)S(1)} %get-tuple-element.46), channel_id=1, source_target_pairs={{0,4},{4,0},{8,12},{12,8},{1,5},{5,1},{9,13},{13,9},{2,6},{6,2},{1... | collective-permute-start | bytes 344072 | tf_op jit(solution)/shard_map/ppermute | solution.py:21
  35.0 9.7 %collective-permute-start.15 = (bf16[32,3584]{1,0:T(8,128)(2,1)S(1)}, bf16[32,3584]{1,0:T(8,128)(2,1)S(1)}, u32[]{:S(2)}, u32[]{:S(2)}) collective-permute-start(bf16[32,3584]{1,0:T(8,128)(2,1)S(1)} %scope_far1.1), channel_id=1, source_target_pairs={{0,2},{1,3},{2,0},{3,1},{4,6},{5,7},{6,4},{7,5},{8,10},{9,11},{10,... | collective-permute-start | bytes 688136 | tf_op jit(solution)/shard_map/ppermute | solution.py:21
  38.6 9.9 %collective-permute-start.12 = (bf16[32,3584]{1,0:T(8,128)(2,1)S(1)}, bf16[32,3584]{1,0:T(8,128)(2,1)S(1)}, u32[]{:S(2)}, u32[]{:S(2)}) collective-permute-start(bf16[32,3584]{1,0:T(8,128)(2,1)S(1)} %scope_fold.1), channel_id=1, source_target_pairs={{0,2},{1,3},{2,0},{3,1},{4,6},{5,7},{6,4},{7,5},{8,10},{9,11},{10,... | collective-permute-start | bytes 688136 | tf_op jit(solution)/shard_map/ppermute | solution.py:21
  40.2 5.7 %collective-permute-start.16 = (bf16[8,3584]{1,0:T(8,128)(2,1)S(1)}, bf16[8,3584]{1,0:T(8,128)(2,1)S(1)}, u32[]{:S(2)}, u32[]{:S(2)}) collective-permute-start(bf16[8,3584]{1,0:T(8,128)(2,1)S(1)} %get-tuple-element.51), channel_id=1, source_target_pairs={{0,8},{4,12},{8,0},{12,4},{1,9},{5,13},{9,1},{13,5},{2,10},{6,14},... | collective-permute-start | bytes 172040 | tf_op jit(solution)/shard_map/ppermute | solution.py:21
  41.2 6.0 %collective-permute-start.17 = (bf16[8,3584]{1,0:T(8,128)(2,1)S(1)}, bf16[8,3584]{1,0:T(8,128)(2,1)S(1)}, u32[]{:S(2)}, u32[]{:S(2)}) collective-permute-start(bf16[8,3584]{1,0:T(8,128)(2,1)S(1)} %get-tuple-element.52), channel_id=1, source_target_pairs={{0,12},{4,8},{8,4},{12,0},{1,13},{5,9},{9,5},{13,1},{2,14},{6,10},... | collective-permute-start | bytes 172040 | tf_op jit(solution)/shard_map/ppermute | solution.py:21
